TPU v7x, 256 devices: a whole 4x4x8 slice. The times are simulated.
256 devices in a mesh: ctx: 8 (over x, core), exp: 32 (over y, z).
Axes of the slice: x: 4, y: 4, z: 8, core: 2. Of those that a mesh axis runs over, the one named last changes fastest.
Arguments:
- logits: bfloat16 [1024, 81920], P('ctx', 'exp'), may hold values from -16 to 250
- head_weight: bfloat16 [81920, 7168], P('exp', 'ctx'), may hold values from -0.0625 to 0.0625
- token_ids: int32 [1024], P('ctx'), may hold values from 0 to 81919
- slab_order: int32 [16], replicated, may hold values from 0 to 15, each once
- token_weights: float32 [1024], P('ctx'), may hold values from 4 to 64
- moe_input: bfloat16 [1024, 7168], P('exp', 'ctx'), may hold values from -6 to 6
- routes: int32 [1024, 8], P('exp'), may hold values from 0 to 31, all different within a row; in each aligned block of 32 rows (0 to 31, 32 to 63, ...) at most 16 rows name the same one
- probs: bfloat16 [1024, 8], P('exp'), may hold values from 0.049804688 to 1
- w_gate: bfloat16 [32, 7168, 1024], P('exp', 'ctx'), may hold values from -0.0625 to 0.0625
- w_up: bfloat16 [32, 7168, 1024], P('exp', 'ctx'), may hold values from -0.0625 to 0.0625
- w_down: bfloat16 [32, 1024, 7168], P('exp', None, 'ctx'), may hold values from -0.1875 to 0.1875
Outputs:
- d_x: float32 [1024, 7168], P('exp', 'ctx')
- d_prob: float32 [1024, 8], P('exp')
Inputs may be any that keep to these rules, and one draw needn't show every extreme that they name: `slab_order`: a permutation of the 16 slabs. `routes`: each row names 8 different experts; among the rows of one exp index (32 rows) no expert is named more than 16 times, a bound that some block reaches.
All inputs are finite; a program needn't handle non-finite values.
Results may differ from a plain program's by a relative error of at most 0.0042.
Values may be sent and summed in bfloat16 or wider, within the bound.
No kernel may reach another device: no remote copies, remote signals or barrier semaphores. Data moves between devices by JAX's collectives and lax.ppermute only.
A program may use at most 64 MiB of HBM per device.

v0:
```python
import jax
import jax.numpy as jnp
from jax import lax
from jax.sharding import PartitionSpec as P

SLAB = 64


def unit_backward(gate_sum, up_sum, back_sum, slot_prob):
    gate_sigmoid = jax.nn.sigmoid(gate_sum)
    gate_silu = gate_sum * gate_sigmoid
    prob_part = jnp.sum(gate_silu * up_sum * back_sum, axis=1)
    scaled_back = slot_prob[:, None] * back_sum
    gate_grad = (
        scaled_back * up_sum * gate_sigmoid * (1.0 + gate_sum * (1.0 - gate_sigmoid))
    ).astype(jnp.bfloat16)
    up_grad = (scaled_back * gate_silu).astype(jnp.bfloat16)
    return (gate_grad, up_grad, prob_part)


def local(
    logits,
    head_weight,
    token_ids,
    slab_order,
    token_weights,
    moe_input,
    routes,
    probs,
    w_gate,
    w_up,
    w_down,
):
    ctx_count = lax.axis_size("ctx")
    exp_count = lax.axis_size("exp")
    row_count, vocab_width = logits.shape
    seq_length = row_count * ctx_count
    all_ids = lax.all_gather(token_ids, "ctx", axis=0, tiled=True)
    local_rows = jnp.arange(row_count, dtype=jnp.int32)
    slab_index = lax.axis_index("ctx") * 2 + local_rows // SLAB
    slab_match = jnp.arange(slab_order.shape[0], dtype=jnp.int32)[None, :] == slab_index[:, None]
    placed_slab = jnp.sum(jnp.where(slab_match, slab_order[None, :], 0), axis=1)
    position = placed_slab * SLAB + local_rows % SLAB
    has_target = position < seq_length - 1
    target = jnp.take(all_ids, jnp.minimum(position + 1, seq_length - 1))
    local_target = target - lax.axis_index("exp") * vocab_width
    scores = logits.astype(jnp.float32)
    local_max = jnp.max(scores, axis=1)
    row_max = lax.pmax(local_max, "exp")
    row_total = lax.psum(jnp.sum(jnp.exp(scores - row_max[:, None]), axis=1), "exp")
    is_target = jnp.arange(vocab_width, dtype=jnp.int32)[None, :] == local_target[:, None]
    weighting = jnp.where(has_target, token_weights, 0.0)
    logit_grads = (
        weighting[:, None]
        * (jnp.exp(scores - row_max[:, None]) / row_total[:, None] - is_target.astype(jnp.float32))
    ).astype(jnp.bfloat16)
    gathered = lax.all_gather(logit_grads, "ctx", axis=0, tiled=True)
    token_count, route_count = routes.shape
    upstream = lax.psum_scatter(
        jnp.dot(gathered, head_weight, preferred_element_type=jnp.float32),
        "exp",
        scatter_dimension=0,
        tiled=True,
    )
    upstream_sent = upstream.astype(jnp.bfloat16)
    capacity = min(token_count, 2 * token_count * route_count // exp_count)
    slot_count = exp_count * capacity
    route_list = routes.reshape(-1)
    expert_match = (route_list[:, None] == jnp.arange(exp_count, dtype=jnp.int32)[None, :]).astype(
        jnp.int32
    )
    route_rank = jnp.sum((jnp.cumsum(expert_match, axis=0) - 1) * expert_match, axis=1)
    slot_of_route = route_list * capacity + route_rank
    chosen = (jnp.arange(slot_count, dtype=jnp.int32)[:, None] == slot_of_route[None, :]).astype(
        jnp.float32
    )
    slot_owner_wide = jnp.sum(chosen.reshape(slot_count, token_count, route_count), axis=2)
    slot_owner = slot_owner_wide.astype(jnp.bfloat16)
    feature_width = moe_input.shape[1]
    send_input = (
        jnp.dot(slot_owner, moe_input, preferred_element_type=jnp.float32)
        .astype(jnp.bfloat16)
        .reshape(exp_count, capacity, feature_width)
    )
    send_upstream = (
        jnp.dot(slot_owner, upstream_sent, preferred_element_type=jnp.float32)
        .astype(jnp.bfloat16)
        .reshape(exp_count, capacity, feature_width)
    )
    send_prob = (
        jnp.dot(chosen, probs.reshape(-1).astype(jnp.float32), precision=lax.Precision.HIGHEST)
        .astype(jnp.bfloat16)
        .reshape(exp_count, capacity)
    )
    gate_w = w_gate[0]
    up_w = w_up[0]
    down_w = w_down[0]
    contract_last = (((1,), (1,)), ((), ()))
    slot_inputs = lax.all_to_all(send_input, "exp", split_axis=0, concat_axis=0, tiled=True)
    slot_upstream = lax.all_to_all(send_upstream, "exp", split_axis=0, concat_axis=0, tiled=True)
    slot_prob = lax.all_to_all(send_prob, "exp", split_axis=0, concat_axis=0, tiled=True)
    item_count = slot_inputs.shape[1]
    flat_inputs = slot_inputs.reshape(-1, feature_width)
    flat_upstream = slot_upstream.reshape(-1, feature_width)
    flat_prob = slot_prob.reshape(-1).astype(jnp.float32)
    part_gate = jnp.dot(flat_inputs, gate_w, preferred_element_type=jnp.float32)
    part_up = jnp.dot(flat_inputs, up_w, preferred_element_type=jnp.float32)
    part_back = lax.dot_general(
        flat_upstream, down_w, contract_last, preferred_element_type=jnp.float32
    )
    gate_sum, up_sum, back_sum = lax.psum((part_gate, part_up, part_back), "ctx")
    gate_grad, up_grad, prob_grad = unit_backward(gate_sum, up_sum, back_sum, flat_prob)
    input_grad = lax.dot_general(
        gate_grad, gate_w, contract_last, preferred_element_type=jnp.float32
    ) + lax.dot_general(up_grad, up_w, contract_last, preferred_element_type=jnp.float32)
    back_input = lax.all_to_all(
        input_grad.reshape(exp_count, item_count, feature_width),
        "exp",
        split_axis=0,
        concat_axis=0,
        tiled=True,
    )
    back_prob = lax.all_to_all(
        prob_grad.reshape(exp_count, item_count), "exp", split_axis=0, concat_axis=0, tiled=True
    )
    d_x = upstream + jnp.dot(
        slot_owner_wide.T,
        back_input.reshape(slot_count, feature_width),
        precision=lax.Precision.HIGHEST,
    )
    d_prob = jnp.dot(back_prob.reshape(-1), chosen, precision=lax.Precision.HIGHEST).reshape(
        token_count, route_count
    )
    return (d_x, d_prob)


def solution(mesh):
    placed = (
        P("ctx", "exp"),
        P("exp", "ctx"),
        P("ctx"),
        P(),
        P("ctx"),
        P("exp", "ctx"),
        P("exp", None),
        P("exp", None),
        P("exp", "ctx", None),
        P("exp", "ctx", None),
        P("exp", None, "ctx"),
    )
    return jax.shard_map(
        local,
        mesh=mesh,
        in_specs=placed,
        out_specs=(P("exp", "ctx"), P("exp", None)),
        check_vma=False,
    )
```

profile of v0, /device:TPU:32, one launch (start us, length us, event | category | flops | bytes accessed | tf_op | source)
XLA Modules:
  0.0 647.7 jit_solution(9948729076130467570)
XLA Ops:
  7.3 0.9 select_reduce_fusion
  8.2 10.7 %all-gather = s32[8,1,128]{2,1,0:T(1,128)S(1)} all-gather(s32[1,1,128]{2,1,0:T(1,128)} %bitcast.66), channel_id=1, replica_groups=mesh['ctx'=8,'exp'=32] {'ctx'}, dimensions={0}, use_global_device_ids=true | all-gather | bytes 4608 | tf_op jit(solution)/shard_map/all_gather | solution.py:38
  18.9 0.7 compare_select_fusion.2
  19.5 1.3 reduce_max.14
  20.8 73.7 %pmax.7 = f32[128]{0:T(128)S(1)} all-reduce(bf16[128]{0:T(256)(128)(2,1)S(1)} %reduce_max.14), channel_id=1, replica_groups=mesh['ctx'=8,'exp'=32] {'exp'}, use_global_device_ids=true, to_apply=%region_2.3 | all-reduce | flops 128 | bytes 768 | tf_op jit(solution)/shard_map/pmax | solution.py:49
  94.5 1.5 fusion.14
  95.9 74.0 %psum.28 = f32[128]{0:T(128)S(1)} all-reduce(f32[128]{0:T(128)S(1)} %fusion.14), channel_id=1, replica_groups=mesh['ctx'=8,'exp'=32] {'exp'}, use_global_device_ids=true, to_apply=%region_4.5 | all-reduce | flops 128 | bytes 1024 | tf_op jit(solution)/shard_map/psum | solution.py:50
  169.9 1.0 gather_fusion
  170.9 1.5 multiply_convert_fusion.2
  172.5 31.6 %all-gather.3.cloned.1.call-done = bf16[1024,2560]{1,0:T(8,128)(2,1)} async-done(((bf16[128,2560]{1,0:T(8,128)(2,1)}), bf16[1024,2560]{1,0:T(8,128)(2,1)}) %all-gather.3.cloned.1.call-update) | async-done | bytes 5242896 | tf_op jit(solution)/shard_map/all_gather | solution.py:57
  204.1 10.2 %fusion.36 = f32[1024,896]{1,0:T(8,128)} fusion(bf16[1024,2560]{1,0:T(8,128)(2,1)} %all-gather.3.cloned.1.call-done, bf16[2560,896]{1,0:T(8,128)(2,1)} %param.12), kind=kOutput, calls=%fused_computation.68 | convolution fusion | flops 4697620480 | bytes 13500416 | tf_op jit(solution)/shard_map/dot_general | solution.py:60
  214.3 0.7 copy-done.6
  215.0 0.1 eq.99
  215.1 0.1 eq.95
  215.2 0.6 reduce-window.6
  215.8 0.2 slice_reduce_fusion
  216.1 0.1 fusion.25
  216.2 0.1 reduce_sum.50
  216.3 0.2 convert_reduce_fusion
  216.5 1.3 convolution_convert_fusion
  217.9 10.1 %all-to-all-start.2 = ((bf16[32,16,896]{2,1,0:T(8,128)(2,1)}), bf16[32,16,896]{2,1,0:T(8,128)(2,1)S(1)}, u32[]{:S(2)}, u32[]{:S(2)}) async-start(bf16[32,16,896]{2,1,0:T(8,128)(2,1)} %bitcast.9), calls=%async_computation.3 | async-start | bytes 1835008 | tf_op jit(solution)/shard_map/all_to_all | solution.py:99
  228.0 212.4 %reduce-scatter.2.cloned.1.call-done = f32[32,896]{1,0:T(8,128)} async-done(((f32[1024,896]{1,0:T(8,128)}), f32[32,896]{1,0:T(8,128)}) %reduce-scatter.2.cloned.1.call-update) | async-done | bytes 114704 | tf_op jit(solution)/shard_map/reduce_scatter | solution.py:59
  440.4 2.3 convolution_convert_fusion.1
  442.6 8.0 %all-to-all-start.1 = ((bf16[32,16,896]{2,1,0:T(8,128)(2,1)}), bf16[32,16,896]{2,1,0:T(8,128)(2,1)}, u32[]{:S(2)}, u32[]{:S(2)}) async-start(bf16[32,16,896]{2,1,0:T(8,128)(2,1)} %bitcast.6), calls=%async_computation.2 | async-start | bytes 1835008 | tf_op jit(solution)/shard_map/all_to_all | solution.py:100
  450.7 2.6 fusion.3
  453.3 2.5 fusion.7
  455.8 15.8 %all-to-all-done.1 = bf16[32,16,896]{2,1,0:T(8,128)(2,1)} async-done(((bf16[32,16,896]{2,1,0:T(8,128)(2,1)}), bf16[32,16,896]{2,1,0:T(8,128)(2,1)}, u32[]{:S(2)}, u32[]{:S(2)}) %all-to-all-start.1) | async-done | bytes 917536 | tf_op jit(solution)/shard_map/all_to_all | solution.py:100
  471.7 4.4 fusion.9
  476.1 0.7 copy-done.7
  476.8 0.1 copy.30
  476.9 0.1 reshape.214
  477.0 0.2 fusion.17
  477.2 0.1 all_to_all.28
  477.3 13.5 %all_to_all.34 = bf16[32,1,16]{2,1,0:T(2,128)(2,1)S(1)} all-to-all(bf16[32,1,16]{2,1,0:T(2,128)(2,1)S(1)} %all_to_all.28), channel_id=1, replica_groups=mesh['ctx'=8,'exp'=32] {'exp'}, dimensions={0} | all-to-all | bytes 2048 | tf_op jit(solution)/shard_map/all_to_all | solution.py:101
  490.9 71.3 %all-reduce.3.cloned.1.call-done = (f32[512,1024]{1,0:T(8,128)}, f32[512,1024]{1,0:T(8,128)}, f32[512,1024]{1,0:T(8,128)}) async-done(((f32[512,1024]{1,0:T(8,128)}, f32[512,1024]{1,0:T(8,128)}, f32[512,1024]{1,0:T(8,128)}), (f32[512,1024]{1,0:T(8,128)}, f32[512,1024]{1,0:T(8,128)}, f32[512,1024]{1,0:T(8,128)})) %all-reduce.3.cloned.1.call-update) | async-done | bytes 6291472 | tf_op jit(solution)/shard_map/psum | solution.py:111
  562.2 3.5 multiply_reduce_fusion
  565.7 0.7 all_to_all.26
  566.4 10.1 %all-to-all-start.4 = ((f32[32,1,16]{2,1,0:T(1,128)}), f32[32,1,16]{2,1,0:T(1,128)S(1)}, u32[]{:S(2)}, u32[]{:S(2)}) async-start(f32[32,1,16]{2,1,0:T(1,128)} %bitcast.15), calls=%async_computation.5 | async-start | bytes 32768 | tf_op jit(solution)/shard_map/all_to_all | solution.py:123
  576.6 4.6 fusion.1
  581.2 2.6 fusion.11
  583.8 1.3 all-to-all-done.4
  585.1 8.7 %all-to-all-start.3 = ((f32[32,16,896]{2,1,0:T(8,128)}), f32[32,16,896]{2,1,0:T(8,128)}, u32[]{:S(2)}, u32[]{:S(2)}) async-start(f32[32,16,896]{2,1,0:T(8,128)} %bitcast.61), calls=%async_computation.4 | async-start | bytes 3670016 | tf_op jit(solution)/shard_map/all_to_all | solution.py:116
  593.8 0.5 broadcast.264
  594.3 0.7 reduce.10
  595.0 1.9 fusion.18
  597.0 0.7 copy.33
  597.6 40.3 %all-to-all-done.3 = f32[32,16,896]{2,1,0:T(8,128)} async-done(((f32[32,16,896]{2,1,0:T(8,128)}), f32[32,16,896]{2,1,0:T(8,128)}, u32[]{:S(2)}, u32[]{:S(2)}) %all-to-all-start.3) | async-done | bytes 1835040 | tf_op jit(solution)/shard_map/all_to_all | solution.py:116
  638.0 3.2 convolution_add_fusion
  (39 shorter events, 0.6 us)
Async XLA Ops:
  7.2 443.5 %copy-start = (bf16[1,896,1024]{2,1,0:T(8,128)(2,1)S(1)}, bf16[1,896,1024]{2,1,0:T(8,128)(2,1)}, u32[]{:S(2)}) copy-start(bf16[1,896,1024]{2,1,0:T(8,128)(2,1)} %param.19) | copy-start | bytes 5505028
  7.2 163.7 %copy-start.1 = (bf16[128,2560]{1,0:T(8,128)(2,1)S(1)}, bf16[128,2560]{1,0:T(8,128)(2,1)}, u32[]{:S(2)}) copy-start(bf16[128,2560]{1,0:T(8,128)(2,1)} %param.11) | copy-start | bytes 1966084
  7.2 196.9 %all-gather.3.cloned.1.call-start = ((), (), s32[]{:S(2)}) async-start(), calls=%async_computation.6 | async-start | bytes 5898240 | tf_op jit(solution)/shard_map/all_gather | solution.py:57
  172.4 267.9 %reduce-scatter.2.cloned.1.call-start = ((), (), s32[]{:S(2)}) async-start(), calls=%async_computation.7 | async-start | bytes 3784704 | tf_op jit(solution)/shard_map/reduce_scatter | solution.py:59
  214.3 0.7 copy-start.6
  214.3 2.2 copy-start.5
  217.9 224.8 %all-to-all-start.2 = ((bf16[32,16,896]{2,1,0:T(8,128)(2,1)}), bf16[32,16,896]{2,1,0:T(8,128)(2,1)S(1)}, u32[]{:S(2)}, u32[]{:S(2)}) async-start(bf16[32,16,896]{2,1,0:T(8,128)(2,1)} %bitcast.9), calls=%async_computation.3 | async-start | bytes 1835008 | tf_op jit(solution)/shard_map/all_to_all | solution.py:99
  442.6 29.1 %all-to-all-start.1 = ((bf16[32,16,896]{2,1,0:T(8,128)(2,1)}), bf16[32,16,896]{2,1,0:T(8,128)(2,1)}, u32[]{:S(2)}, u32[]{:S(2)}) async-start(bf16[32,16,896]{2,1,0:T(8,128)(2,1)} %bitcast.6), calls=%async_computation.2 | async-start | bytes 1835008 | tf_op jit(solution)/shard_map/all_to_all | solution.py:100
  450.6 111.6 %all-reduce.3.cloned.1.call-start = ((), (), s32[]{:S(2)}) async-start(), calls=%async_computation.8 | async-start | bytes 12582912 | tf_op jit(solution)/shard_map/psum | solution.py:111
  450.7 2.6 copy-start.8
  476.1 0.7 copy-start.7
  566.4 18.6 %all-to-all-start.4 = ((f32[32,1,16]{2,1,0:T(1,128)}), f32[32,1,16]{2,1,0:T(1,128)S(1)}, u32[]{:S(2)}, u32[]{:S(2)}) async-start(f32[32,1,16]{2,1,0:T(1,128)} %bitcast.15), calls=%async_computation.5 | async-start | bytes 32768 | tf_op jit(solution)/shard_map/all_to_all | solution.py:123
  576.5 4.6 copy-start.2
  576.5 4.6 copy-start.3
  576.5 4.6 copy-start.9
  583.8 54.2 %copy-start.4 = (f32[32,896]{1,0:T(8,128)S(1)}, f32[32,896]{1,0:T(8,128)}, u32[]{:S(2)}) copy-start(f32[32,896]{1,0:T(8,128)} %reduce-scatter.2.cloned.1.call-done) | copy-start | bytes 344068
  585.1 52.9 %all-to-all-start.3 = ((f32[32,16,896]{2,1,0:T(8,128)}), f32[32,16,896]{2,1,0:T(8,128)}, u32[]{:S(2)}, u32[]{:S(2)}) async-start(f32[32,16,896]{2,1,0:T(8,128)} %bitcast.61), calls=%async_computation.4 | async-start | bytes 3670016 | tf_op jit(solution)/shard_map/all_to_all | solution.py:116
Sparse Core Ops, SparseCore 0:
  172.6 31.5 all-gather.2
  214.4 225.8 reduce-scatter.1
  476.2 85.9 all-reduce.2
where the time goes:
time: 648 us
  waiting for transfers between devices  373 us (58%)
  blocking collectives  172 us (27%)
  starting transfers between devices  37 us (6%)
  matrix products  35.8 us (6%)
  between operations  14 us (2%)
  other arithmetic  11.1 us (2%)
    reduce_scatter x1, waiting for transfers between devices, local(): lax.psum_scatter(jnp.dot(gathered, head_weight, preferred_element_type=jn...  212 us
    psum x1, blocking collectives, local(): lax.psum(jnp.sum(jnp.exp(scores - row_max[:, None]), axis=1), 'exp')  74 us
    pmax x1, blocking collectives, local(): row_max = lax.pmax(local_max, 'exp')  73.7 us
    psum x1, waiting for transfers between devices, local(): lax.psum((part_gate, part_up, part_back), 'ctx')  71.3 us
    all_to_all x1, waiting for transfers between devices, local(): lax.all_to_all(input_grad.reshape(exp_count, item_count, feature_width),...  40.3 us
    all_gather x1, waiting for transfers between devices, local(): gathered = lax.all_gather(logit_grads, 'ctx', axis=0, tiled=True)  31.6 us
    all_to_all x1, waiting for transfers between devices, local(): lax.all_to_all(send_upstream, 'exp', split_axis=0, concat_axis=0, tiled=T...  15.8 us
    all_to_all x1, blocking collectives, local(): lax.all_to_all(send_prob, 'exp', split_axis=0, concat_axis=0, tiled=True)  13.5 us
  transfers between devices with their start and end apart: 7, of which 6 were waited for; matrix products, arithmetic and copies ran while one was open for 3% of the time, Pallas kernels for 0%

commit v1 on v0

v1 whole, which is shorter than its diff:
```python
import jax
import jax.numpy as jnp
from jax import lax
from jax.sharding import PartitionSpec as P

SLAB = 64
NY, NZ = 4, 8
Y_GROUPS = [[y * NZ + z for y in range(NY)] for z in range(NZ)]
Z_GROUPS = [[y * NZ + z for z in range(NZ)] for y in range(NY)]
PAIR_GROUPS = [[2 * c, 2 * c + 1] for c in range(4)]
X_GROUPS = [[2 * c + p for c in range(4)] for p in range(2)]
CONTRACT_LAST = (((1,), (1,)), ((), ()))


def exchange(x, axis, groups=None):
    return lax.all_to_all(x, axis, 0, 0, tiled=True, axis_index_groups=groups)


def exchange_sum(x, axis, groups, parts):
    rows, width = x.shape
    got = exchange(x, axis, groups).reshape(parts, rows // parts, width)
    return jnp.sum(got.astype(jnp.float32), axis=0)


def sum_over_ctx(x):
    half = exchange_sum(x.astype(jnp.float16), "ctx", PAIR_GROUPS, 2).astype(jnp.float16)
    own = exchange_sum(half, "ctx", X_GROUPS, 4).astype(jnp.float16)
    rows, width = own.shape
    spread = jnp.broadcast_to(own[None], (4, rows, width)).reshape(4 * rows, width)
    half = exchange(spread, "ctx", X_GROUPS)
    other = lax.ppermute(half, "ctx", [(i, i ^ 1) for i in range(8)])
    core = lax.axis_index("ctx") % 2
    first = jnp.where(core == 0, half, other)
    second = jnp.where(core == 0, other, half)
    return jnp.concatenate([first, second], axis=0).astype(jnp.float32)


def unit_backward(gate_sum, up_sum, back_sum, slot_prob):
    gate_sigmoid = jax.nn.sigmoid(gate_sum)
    gate_silu = gate_sum * gate_sigmoid
    prob_part = jnp.sum(gate_silu * up_sum * back_sum, axis=1)
    scaled_back = slot_prob[:, None] * back_sum
    gate_grad = (
        scaled_back * up_sum * gate_sigmoid * (1.0 + gate_sum * (1.0 - gate_sigmoid))
    ).astype(jnp.bfloat16)
    up_grad = (scaled_back * gate_silu).astype(jnp.bfloat16)
    return (gate_grad, up_grad, prob_part)


def local(
    logits,
    head_weight,
    token_ids,
    slab_order,
    token_weights,
    moe_input,
    routes,
    probs,
    w_gate,
    w_up,
    w_down,
):
    ctx_count = lax.axis_size("ctx")
    exp_count = lax.axis_size("exp")
    row_count, vocab_width = logits.shape
    seq_length = row_count * ctx_count
    all_logits = lax.all_gather(logits, "ctx", axis=0, tiled=True)

    token_count, route_count = routes.shape
    feature_width = moe_input.shape[1]
    capacity = min(token_count, 2 * token_count * route_count // exp_count)
    slot_count = exp_count * capacity
    route_list = routes.reshape(-1)
    expert_match = (route_list[:, None] == jnp.arange(exp_count, dtype=jnp.int32)[None, :]).astype(
        jnp.int32
    )
    route_rank = jnp.sum((jnp.cumsum(expert_match, axis=0) - 1) * expert_match, axis=1)
    slot_of_route = route_list * capacity + route_rank
    chosen = (jnp.arange(slot_count, dtype=jnp.int32)[:, None] == slot_of_route[None, :]).astype(
        jnp.float32
    )
    slot_owner = jnp.sum(chosen.reshape(slot_count, token_count, route_count), axis=2).astype(
        jnp.bfloat16
    )

    scores = logits.astype(jnp.float32)
    local_max = jnp.max(scores, axis=1)
    local_sum = jnp.sum(jnp.exp(scores - local_max[:, None]), axis=1)
    send_prob = jnp.dot(
        chosen, probs.reshape(-1).astype(jnp.float32), precision=lax.Precision.HIGHEST
    ).reshape(exp_count, capacity)
    packed = jnp.concatenate(
        [
            jnp.broadcast_to(local_max[None], (exp_count, row_count)),
            jnp.broadcast_to(local_sum[None], (exp_count, row_count)),
            jnp.pad(send_prob, ((0, 0), (0, 128 - capacity))),
        ],
        axis=1,
    )
    packed = exchange(packed, "exp")
    all_max = packed[:, :row_count]
    row_max = jnp.max(all_max, axis=0)
    row_total = jnp.sum(packed[:, row_count : 2 * row_count] * jnp.exp(all_max - row_max), axis=0)
    flat_prob = packed[:, 2 * row_count : 2 * row_count + capacity].reshape(-1)
    rows = jnp.stack([row_max, row_total, token_weights, token_ids.astype(jnp.float32)])
    rows = lax.all_gather(rows, "ctx", axis=1, tiled=True)
    row_max, row_total, weights = rows[0], rows[1], rows[2]
    all_ids = rows[3].astype(jnp.int32)

    send_input = jnp.dot(slot_owner, moe_input, preferred_element_type=jnp.float32).astype(
        jnp.bfloat16
    )
    flat_inputs = exchange(send_input, "exp")
    gate_w = w_gate[0]
    up_w = w_up[0]
    down_w = w_down[0]
    part_gate = jnp.dot(flat_inputs, gate_w, preferred_element_type=jnp.float32)
    part_up = jnp.dot(flat_inputs, up_w, preferred_element_type=jnp.float32)
    gate_sum, up_sum = lax.psum((part_gate, part_up), "ctx")

    storage = jnp.arange(seq_length, dtype=jnp.int32)
    slab_match = (
        jnp.arange(slab_order.shape[0], dtype=jnp.int32)[None, :] == (storage // SLAB)[:, None]
    )
    placed_slab = jnp.sum(jnp.where(slab_match, slab_order[None, :], 0), axis=1)
    position = placed_slab * SLAB + storage % SLAB
    has_target = position < seq_length - 1
    target = jnp.take(all_ids, jnp.minimum(position + 1, seq_length - 1))
    local_target = target - lax.axis_index("exp") * vocab_width
    weighting = jnp.where(has_target, weights, 0.0)
    is_target = jnp.arange(vocab_width, dtype=jnp.int32)[None, :] == local_target[:, None]
    logit_grads = (
        weighting[:, None]
        * (
            jnp.exp(all_logits.astype(jnp.float32) - row_max[:, None]) / row_total[:, None]
            - is_target.astype(jnp.float32)
        )
    ).astype(jnp.bfloat16)
    partial = jnp.dot(logit_grads, head_weight, preferred_element_type=jnp.float32)
    over_y = exchange_sum((partial * 4096.0).astype(jnp.float16), "exp", Y_GROUPS, NY)
    upstream = exchange_sum(over_y.astype(jnp.float16), "exp", Z_GROUPS, NZ) * (1.0 / 4096.0)
    upstream_sent = upstream.astype(jnp.bfloat16)

    send_upstream = jnp.dot(slot_owner, upstream_sent, preferred_element_type=jnp.float32).astype(
        jnp.bfloat16
    )
    flat_upstream = exchange(send_upstream, "exp")
    part_back = lax.dot_general(
        flat_upstream, down_w, CONTRACT_LAST, preferred_element_type=jnp.float32
    )
    back_sum = sum_over_ctx(part_back)
    gate_grad, up_grad, prob_grad = unit_backward(gate_sum, up_sum, back_sum, flat_prob)
    input_grad = lax.dot_general(
        gate_grad, gate_w, CONTRACT_LAST, preferred_element_type=jnp.float32
    ) + lax.dot_general(up_grad, up_w, CONTRACT_LAST, preferred_element_type=jnp.float32)
    prob_high = lax.reduce_precision(prob_grad, 8, 7)
    prob_low = prob_grad - prob_high
    lane = jnp.arange(128, dtype=jnp.int32)[None, :]
    prob_block = jnp.where(
        lane == 0, prob_high[:, None], jnp.where(lane == 1, prob_low[:, None], 0)
    ).astype(jnp.bfloat16)
    back = exchange(
        jnp.concatenate([input_grad.astype(jnp.bfloat16), prob_block], axis=1), "exp"
    )
    back_input = back[:, :feature_width]
    back_prob = back[:, feature_width].astype(jnp.float32) + back[:, feature_width + 1].astype(
        jnp.float32
    )
    d_x = upstream + lax.dot_general(
        slot_owner, back_input, (((0,), (0,)), ((), ())), preferred_element_type=jnp.float32
    )
    d_prob = jnp.dot(back_prob, chosen, precision=lax.Precision.HIGHEST).reshape(
        token_count, route_count
    )
    return (d_x, d_prob)


def solution(mesh):
    placed = (
        P("ctx", "exp"),
        P("exp", "ctx"),
        P("ctx"),
        P(),
        P("ctx"),
        P("exp", "ctx"),
        P("exp", None),
        P("exp", None),
        P("exp", "ctx", None),
        P("exp", "ctx", None),
        P("exp", None, "ctx"),
    )
    return jax.shard_map(
        local,
        mesh=mesh,
        in_specs=placed,
        out_specs=(P("exp", "ctx"), P("exp", None)),
        check_vma=False,
    )
```

time: 648 us -> 298 us (0.46)
  waiting for transfers between devices: 373 us -> 95 us
  blocking collectives: 172 us -> 108 us
  starting transfers between devices: 37 us -> 29 us
  matrix products: 35.8 us -> 29.1 us
    reduce_scatter x1 -> x0, waiting for transfers between devices: 212 us -> none  [local(): lax.psum_scatter(jnp.dot(gathered, head_weight, preferred_element_type=jn...]
    all_to_all x1 -> x5, blocking collectives: 13.5 us -> 96.3 us  [exchange(): return lax.all_to_all(x, axis, 0, 0, tiled=True, axis_index_groups=groups)]
    psum x1 -> x0, blocking collectives: 74 us -> none  [local(): lax.psum(jnp.sum(jnp.exp(scores - row_max[:, None]), axis=1), 'exp')]
    pmax x1 -> x0, blocking collectives: 73.7 us -> none  [local(): row_max = lax.pmax(local_max, 'exp')]
    psum x1, waiting for transfers between devices: 71.3 us -> 32.8 us  [local(): gate_sum, up_sum = lax.psum((part_gate, part_up), 'ctx')]
    all_gather x1, waiting for transfers between devices: 31.6 us -> 0.15 us  [local(): all_logits = lax.all_gather(logits, 'ctx', axis=0, tiled=True)]
    dot_general x6, matrix products: 26.9 us -> 18.8 us  [the longest x1 10 us: local(): jnp.dot(logit_grads, head_weight, preferred_element_type=jnp.float32)]
    all_to_all x4, starting transfers between devices: 36.9 us -> 28.9 us  [exchange(): return lax.all_to_all(x, axis, 0, 0, tiled=True, axis_index_groups=groups)]
  transfers between devices with their start and end apart: 7 -> 7, of which waited for: 6 -> 7; matrix products, arithmetic and copies ran while one was open for 3% -> 9% of each run, Pallas kernels for 0% -> 0%
where the time goes in v1:
time: 298 us; the launch traced here: 297 us
  blocking collectives  108 us (36%)
  waiting for transfers between devices  95 us (32%)
  matrix products  29.1 us (10%)
  starting transfers between devices  29 us (10%)
  between operations  14.4 us (5%)
  other arithmetic  11.1 us (4%)
  local copies, waits for them, and re-layouts  10.3 us (3%)
    all_to_all x5, blocking collectives, exchange(): return lax.all_to_all(x, axis, 0, 0, tiled=True, axis_index_groups=groups)  96.3 us
    all_to_all x4, waiting for transfers between devices, exchange(): return lax.all_to_all(x, axis, 0, 0, tiled=True, axis_index_groups=groups)  60.5 us
    psum x1, waiting for transfers between devices, local(): gate_sum, up_sum = lax.psum((part_gate, part_up), 'ctx')  32.8 us
    all_to_all x4, starting transfers between devices, exchange(): return lax.all_to_all(x, axis, 0, 0, tiled=True, axis_index_groups=groups)  28.9 us
    all_gather x1, blocking collectives, local(): rows = lax.all_gather(rows, 'ctx', axis=1, tiled=True)  11.9 us
    dot_general x1, matrix products, local(): jnp.dot(logit_grads, head_weight, preferred_element_type=jnp.float32)  10 us
  transfers between devices with their start and end apart: 7, of which 7 were waited for; matrix products, arithmetic and copies ran while one was open for 9% of the time, Pallas kernels for 0%

profile of v1, /device:TPU:32, one launch (start us, length us, event | category | flops | bytes accessed | tf_op | source)
XLA Modules:
  0.0 297.2 jit_solution(11782930849626184385)
XLA Ops:
  7.3 0.7 all-gather.2.cloned.1.call-update
  7.9 0.8 copy.30
  8.9 1.3 reduce_max.23
  10.2 0.8 copy.33
  11.0 0.6 reduce-window.6
  11.9 1.5 exponential_reduce_fusion
  13.5 0.5 fusion.30
  14.0 0.7 all_to_all.58
  14.6 11.4 %all-to-all-start = ((f32[32,1,384]{2,1,0:T(1,128)}), f32[32,1,384]{2,1,0:T(1,128)S(1)}, u32[]{:S(2)}, u32[]{:S(2)}) async-start(f32[32,1,384]{2,1,0:T(1,128)} %all_to_all.58), calls=%async_computation | async-start | bytes 98304 | tf_op jit(solution)/shard_map/all_to_all | solution.py:16
  26.2 8.8 %all-to-all-done = f32[32,1,384]{2,1,0:T(1,128)S(1)} async-done(((f32[32,1,384]{2,1,0:T(1,128)}), f32[32,1,384]{2,1,0:T(1,128)S(1)}, u32[]{:S(2)}, u32[]{:S(2)}) %all-to-all-start) | async-done | bytes 49184 | tf_op jit(solution)/shard_map/all_to_all | solution.py:16
  35.0 11.9 %all_gather.6 = f32[4,1024]{1,0:T(4,128)S(1)} all-gather(f32[4,128]{1,0:T(4,128)S(1)} %pad_maximum_fusion.5), channel_id=1, replica_groups=mesh['ctx'=8,'exp'=32] {'ctx'}, dimensions={1}, use_global_device_ids=true | all-gather | bytes 18432 | tf_op jit(solution)/shard_map/all_gather | solution.py:106
  47.0 4.5 %gather_fusion = s32[1024]{0:T(1024)S(1)} fusion(s32[1024]{0:T(1024)S(1)} %bitcast.76, s32[1024]{0:T(1024)S(1)} %broadcast_clamp_fusion), kind=kCustom, calls=%fused_computation | custom fusion | bytes 12288 | tf_op jit(solution)/shard_map/jit(_take)/gather | solution.py:128
  51.7 10.0 %multiply_convert_fusion.2 = f16[1024,896]{1,0:T(8,128)(2,1)S(1)} fusion(bf16[2560,896]{1,0:T(8,128)(2,1)} %param.12, bf16[1024,2560]{1,0:T(8,128)(2,1)} %all-gather.2.cloned.1.call-done, s32[1024]{0:T(1024)S(1)} %select_subtract_fusion, f32[1024]{0:T(1024)S(1)} %bitcast.96, f32[1024]{0:T(1024)S(1)} %bitcast.97, f32[1024]{0:T(1024)S(1)} %compare_select_fusion.2), kind=kOutput, calls=%fused_computation.5 | convolution fusion | flops 4720427008 | bytes 11681792 | tf_op jit(solution)/shard_map/dot_general | solution.py:139
  61.7 28.0 %all_to_all.87 = f16[4,256,896]{2,1,0:T(8,128)(2,1)S(1)} all-to-all(f16[4,256,896]{2,1,0:T(8,128)(2,1)S(1)} %bitcast.82), channel_id=1, replica_groups={{0,8,16,24},{1,9,17,25},{2,10,18,26},{3,11,19,27},{4,12,20,28},{5,13,21..., dimensions={0} | all-to-all | bytes 3670016 | tf_op jit(solution)/shard_map/all_to_all | solution.py:16
  89.7 0.3 convert_reduce_fusion
  90.0 0.8 convert_element_type.119
  90.8 7.5 %all-to-all-start.2 = ((f16[8,32,896]{2,1,0:T(8,128)(2,1)}), f16[8,32,896]{2,1,0:T(8,128)(2,1)S(1)}, u32[]{:S(2)}, u32[]{:S(2)}) async-start(f16[8,32,896]{2,1,0:T(8,128)(2,1)} %bitcast.14), calls=%async_computation.2 | async-start | bytes 917504 | tf_op jit(solution)/shard_map/all_to_all | solution.py:16
  98.4 0.2 convert_reduce_fusion.4
  98.7 1.3 convolution_convert_fusion
  100.0 12.2 %all-to-all-done.2 = f16[8,32,896]{2,1,0:T(8,128)(2,1)S(1)} async-done(((f16[8,32,896]{2,1,0:T(8,128)(2,1)}), f16[8,32,896]{2,1,0:T(8,128)(2,1)S(1)}, u32[]{:S(2)}, u32[]{:S(2)}) %all-to-all-start.2) | async-done | bytes 458784 | tf_op jit(solution)/shard_map/all_to_all | solution.py:16
  112.2 5.0 %all-to-all-start.7 = ((bf16[32,16,896]{2,1,0:T(8,128)(2,1)}), bf16[32,16,896]{2,1,0:T(8,128)(2,1)S(1)}, u32[]{:S(2)}, u32[]{:S(2)}) async-start(bf16[32,16,896]{2,1,0:T(8,128)(2,1)} %bitcast.21), calls=%async_computation.7 | async-start | bytes 1835008 | tf_op jit(solution)/shard_map/all_to_all | solution.py:16
  117.3 1.4 convolution_convert_fusion.1
  118.8 22.9 %all-to-all-done.7 = bf16[32,16,896]{2,1,0:T(8,128)(2,1)S(1)} async-done(((bf16[32,16,896]{2,1,0:T(8,128)(2,1)}), bf16[32,16,896]{2,1,0:T(8,128)(2,1)S(1)}, u32[]{:S(2)}, u32[]{:S(2)}) %all-to-all-start.7) | async-done | bytes 917536 | tf_op jit(solution)/shard_map/all_to_all | solution.py:16
  141.7 0.9 copy-done.3
  142.6 5.1 %all-to-all-start.3 = ((bf16[32,16,896]{2,1,0:T(8,128)(2,1)}), bf16[32,16,896]{2,1,0:T(8,128)(2,1)S(1)}, u32[]{:S(2)}, u32[]{:S(2)}) async-start(bf16[32,16,896]{2,1,0:T(8,128)(2,1)} %bitcast.15), calls=%async_computation.3 | async-start | bytes 1835008 | tf_op jit(solution)/shard_map/all_to_all | solution.py:16
  147.8 4.5 %fusion.11 = f32[512,1024]{1,0:T(8,128)} fusion(bf16[512,896]{1,0:T(8,128)(2,1)} %bitcast.85, bf16[1,896,1024]{2,1,0:T(8,128)(2,1)} %param.19), kind=kOutput, calls=%fused_computation.20 | convolution fusion | flops 939524096 | bytes 4849664 | tf_op jit(solution)/shard_map/dot_general | solution.py:117
  152.2 2.6 fusion.15
  154.8 16.5 %all-to-all-done.3 = bf16[32,16,896]{2,1,0:T(8,128)(2,1)S(1)} async-done(((bf16[32,16,896]{2,1,0:T(8,128)(2,1)}), bf16[32,16,896]{2,1,0:T(8,128)(2,1)S(1)}, u32[]{:S(2)}, u32[]{:S(2)}) %all-to-all-start.3) | async-done | bytes 917536 | tf_op jit(solution)/shard_map/all_to_all | solution.py:16
  171.4 2.8 fusion.19
  174.2 4.7 %all_to_all.88 = f16[2,256,1024]{2,1,0:T(8,128)(2,1)S(1)} all-to-all(f16[2,256,1024]{2,1,0:T(8,128)(2,1)S(1)} %bitcast.83), channel_id=1, replica_groups={{0,32},{64,96},{128,160},{192,224},{1,33},{65,97},{129,161},{193,225},{..., dimensions={0} | all-to-all | bytes 2097152 | tf_op jit(solution)/shard_map/all_to_all | solution.py:16
  178.9 0.3 convert_reduce_fusion.1
  179.2 15.8 %all_to_all.89 = f16[4,64,1024]{2,1,0:T(8,128)(2,1)S(1)} all-to-all(f16[4,64,1024]{2,1,0:T(8,128)(2,1)S(1)} %bitcast.81), channel_id=1, replica_groups={{0,64,128,192},{32,96,160,224},{1,65,129,193},{33,97,161,225},{2,66,130..., dimensions={0} | all-to-all | bytes 1048576 | tf_op jit(solution)/shard_map/all_to_all | solution.py:16
  195.2 11.0 %all_to_all.90 = f16[4,64,1024]{2,1,0:T(8,128)(2,1)S(1)} all-to-all(f16[4,64,1024]{2,1,0:T(8,128)(2,1)S(1)} %broadcast_in_dim.96), channel_id=1, replica_groups={{0,64,128,192},{32,96,160,224},{1,65,129,193},{33,97,161,225},{2,66,130..., dimensions={0} | all-to-all | bytes 1048576 | tf_op jit(solution)/shard_map/all_to_all | solution.py:16
  206.2 0.5 iota_compare_fusion.7
  206.7 0.7 mul.115
  207.4 0.8 collective-permute-done
  208.2 1.3 broadcast_select_fusion.1
  209.5 32.8 %all-reduce.4.cloned.1.call-done = (f32[512,1024]{1,0:T(8,128)}, f32[512,1024]{1,0:T(8,128)}) async-done(((f32[512,1024]{1,0:T(8,128)}, f32[512,1024]{1,0:T(8,128)}), (f32[512,1024]{1,0:T(8,128)}, f32[512,1024]{1,0:T(8,128)})) %all-reduce.4.cloned.1.call-update) | async-done | bytes 4194320 | tf_op jit(solution)/shard_map/psum | solution.py:119
  242.4 3.1 %fusion.7 = f32[512]{0:T(512)S(1)} fusion(f32[512,1024]{1,0:T(8,128)} %get-tuple-element.2, f32[512,1024]{1,0:T(8,128)} %get-tuple-element.3, f16[256,1024]{1,0:T(8,128)(2,1)S(1)} %get-tuple-element.5, f16[256,1024]{1,0:T(8,128)(2,1)S(1)} %get-tuple-element.4), kind=kLoop, calls=%fused_computation.14 | loop fusion | flops 4718080 | bytes 5244928 | tf_op jit(solution)/shard_map/reduce_sum | solution.py:41
  245.6 1.4 fusion.13
  247.1 0.5 copy-done.13
  247.7 1.7 add_convert_fusion
  249.4 0.2 select_convert_fusion
  249.8 36.9 %all_to_all.91 = bf16[32,16,1024]{2,1,0:T(8,128)(2,1)S(1)} all-to-all(bf16[32,16,1024]{2,1,0:T(8,128)(2,1)S(1)} %bitcast.79), channel_id=1, replica_groups=mesh['ctx'=8,'exp'=32] {'exp'}, dimensions={0} | all-to-all | bytes 2097152 | tf_op jit(solution)/shard_map/all_to_all | solution.py:16
  286.7 0.9 convolution_add_fusion
  287.6 0.2 add_reduce_fusion
  287.8 1.9 fusion.32
  289.7 0.7 copy.36
  (69 shorter events, 1.8 us)
Async XLA Ops:
  7.2 145.1 %copy-start = (bf16[1,896,1024]{2,1,0:T(8,128)(2,1)S(1)}, bf16[1,896,1024]{2,1,0:T(8,128)(2,1)}, u32[]{:S(2)}) copy-start(bf16[1,896,1024]{2,1,0:T(8,128)(2,1)} %param.20) | copy-start | bytes 5505028
  7.2 18.8 %copy-start.11 = (s32[16]{0:T(128)S(1)}, s32[16]{0:T(128)}, u32[]{:S(2)}) copy-start(s32[16]{0:T(128)} %param.14) | copy-start | bytes 196
  7.2 19.0 %copy-start.14 = (s32[128]{0:T(128)S(1)}, s32[128]{0:T(128)}, u32[]{:S(2)}) copy-start(s32[128]{0:T(128)} %param.13) | copy-start | bytes 1540
  7.2 27.8 %copy-start.12 = (f32[128]{0:T(128)S(1)}, f32[128]{0:T(128)}, u32[]{:S(2)}) copy-start(f32[128]{0:T(128)} %param.15) | copy-start | bytes 1540
  7.2 44.5 %all-gather.2.cloned.1.call-start = ((), (), s32[]{:S(2)}) async-start(), calls=%async_computation.9 | async-start | bytes 5898240 | tf_op jit(solution)/shard_map/all_gather | solution.py:67
  13.4 1.2 copy-start.7
  14.6 20.3 %all-to-all-start = ((f32[32,1,384]{2,1,0:T(1,128)}), f32[32,1,384]{2,1,0:T(1,128)S(1)}, u32[]{:S(2)}, u32[]{:S(2)}) async-start(f32[32,1,384]{2,1,0:T(1,128)} %all_to_all.58), calls=%async_computation | async-start | bytes 98304 | tf_op jit(solution)/shard_map/all_to_all | solution.py:16
  89.7 8.9 %copy-start.5 = (bf16[32,896]{1,0:T(8,128)(2,1)S(1)}, bf16[32,896]{1,0:T(8,128)(2,1)}, u32[]{:S(2)}) copy-start(bf16[32,896]{1,0:T(8,128)(2,1)} %param.16) | copy-start | bytes 172036
  90.8 21.4 %all-to-all-start.2 = ((f16[8,32,896]{2,1,0:T(8,128)(2,1)}), f16[8,32,896]{2,1,0:T(8,128)(2,1)S(1)}, u32[]{:S(2)}, u32[]{:S(2)}) async-start(f16[8,32,896]{2,1,0:T(8,128)(2,1)} %bitcast.14), calls=%async_computation.2 | async-start | bytes 917504 | tf_op jit(solution)/shard_map/all_to_all | solution.py:16
  112.2 29.5 %all-to-all-start.7 = ((bf16[32,16,896]{2,1,0:T(8,128)(2,1)}), bf16[32,16,896]{2,1,0:T(8,128)(2,1)S(1)}, u32[]{:S(2)}, u32[]{:S(2)}) async-start(bf16[32,16,896]{2,1,0:T(8,128)(2,1)} %bitcast.21), calls=%async_computation.7 | async-start | bytes 1835008 | tf_op jit(solution)/shard_map/all_to_all | solution.py:16
  141.7 0.9 copy-start.3
  142.6 28.7 %all-to-all-start.3 = ((bf16[32,16,896]{2,1,0:T(8,128)(2,1)}), bf16[32,16,896]{2,1,0:T(8,128)(2,1)S(1)}, u32[]{:S(2)}, u32[]{:S(2)}) async-start(bf16[32,16,896]{2,1,0:T(8,128)(2,1)} %bitcast.15), calls=%async_computation.3 | async-start | bytes 1835008 | tf_op jit(solution)/shard_map/all_to_all | solution.py:16
  147.7 94.7 %all-reduce.4.cloned.1.call-start = ((), (), s32[]{:S(2)}) async-start(), calls=%async_computation.10 | async-start | bytes 8388608 | tf_op jit(solution)/shard_map/psum | solution.py:119
  147.7 4.5 %copy-start.4 = (bf16[32,16,896]{2,1,0:T(8,128)(2,1)S(1)}, bf16[32,16,896]{2,1,0:T(8,128)(2,1)}, u32[]{:S(2)}) copy-start(bf16[32,16,896]{2,1,0:T(8,128)(2,1)} %copy-done.3) | copy-start | bytes 2752516
  206.2 2.0 collective-permute-start
  242.4 3.1 %copy-start.2 = (f32[512,1024]{1,0:T(8,128)S(1)}, f32[512,1024]{1,0:T(8,128)}, u32[]{:S(2)}) copy-start(f32[512,1024]{1,0:T(8,128)} %get-tuple-element.3) | copy-start | bytes 6291460
  242.4 3.2 %copy-start.6 = (f32[512]{0:T(512)S(1)}, f32[512]{0:T(512)}, u32[]{:S(2)}) copy-start(f32[512]{0:T(512)} %mul.115) | copy-start | bytes 6148
  245.5 1.6 copy-start.1
  245.5 2.1 copy-start.13
  247.7 1.7 copy-start.9
  247.7 1.8 copy-start.10
  249.8 38.0 %copy-start.8 = (s32[256]{0:T(256)S(1)}, s32[256]{0:T(256)}, u32[]{:S(2)}) copy-start(s32[256]{0:T(256)} %copy-done.7) | copy-start | bytes 3076
Sparse Core Ops, SparseCore 0:
  9.9 41.7 all-gather.1
  155.0 87.3 all-reduce.3

commit v2 on v1

--- a/solution.py
+++ b/solution.py
@@ -5,10 +5,7 @@
 
 SLAB = 64
 NY, NZ = 4, 8
-Y_GROUPS = [[y * NZ + z for y in range(NY)] for z in range(NZ)]
 Z_GROUPS = [[y * NZ + z for z in range(NZ)] for y in range(NY)]
-PAIR_GROUPS = [[2 * c, 2 * c + 1] for c in range(4)]
-X_GROUPS = [[2 * c + p for c in range(4)] for p in range(2)]
 CONTRACT_LAST = (((1,), (1,)), ((), ()))
 
 
@@ -22,17 +19,73 @@
     return jnp.sum(got.astype(jnp.float32), axis=0)
 
 
+def split_high(x):
+    high = lax.reduce_precision(x, 8, 7)
+    return high, x - high
+
+
+def ctx_shift(x, shift):
+    return lax.ppermute(x, "ctx", [(i, (i + 2 * shift) % 8) for i in range(8)])
+
+
+def ctx_swap(x):
+    return lax.ppermute(x, "ctx", [(i, i ^ 1) for i in range(8)])
+
+
+def rows_at(x, index, count):
+    return lax.dynamic_slice_in_dim(x, index * count, count, axis=0)
+
+
 def sum_over_ctx(x):
-    half = exchange_sum(x.astype(jnp.float16), "ctx", PAIR_GROUPS, 2).astype(jnp.float16)
-    own = exchange_sum(half, "ctx", X_GROUPS, 4).astype(jnp.float16)
-    rows, width = own.shape
-    spread = jnp.broadcast_to(own[None], (4, rows, width)).reshape(4 * rows, width)
-    half = exchange(spread, "ctx", X_GROUPS)
-    other = lax.ppermute(half, "ctx", [(i, i ^ 1) for i in range(8)])
     core = lax.axis_index("ctx") % 2
-    first = jnp.where(core == 0, half, other)
-    second = jnp.where(core == 0, other, half)
-    return jnp.concatenate([first, second], axis=0).astype(jnp.float32)
+    chip = lax.axis_index("ctx") // 2
+    half_rows = x.shape[0] // 2
+    own_rows = half_rows // 4
+    x = x.astype(jnp.float16)
+    other = ctx_swap(rows_at(x, 1 - core, half_rows))
+    pair = (
+        rows_at(x, core, half_rows).astype(jnp.float32) + other.astype(jnp.float32)
+    ).astype(jnp.float16)
+    got = [ctx_shift(rows_at(pair, (chip + shift) % 4, own_rows), shift) for shift in (1, 3, 2)]
+    own = rows_at(pair, chip, own_rows).astype(jnp.float32)
+    for piece in got:
+        own = own + piece.astype(jnp.float32)
+    own = own.astype(jnp.float16)
+    from_one, from_three, from_two = [ctx_shift(own, shift) for shift in (1, 3, 2)]
+    half = jnp.zeros((half_rows, x.shape[1]), jnp.float16)
+    for piece, shift in ((own, 0), (from_one, 1), (from_three, 3), (from_two, 2)):
+        half = lax.dynamic_update_slice_in_dim(half, piece, (chip + 4 - shift) % 4 * own_rows, axis=0)
+    other = ctx_swap(half)
+    first = jnp.where(core == 0, half, other).astype(jnp.float32)
+    second = jnp.where(core == 0, other, half).astype(jnp.float32)
+    return jnp.concatenate([first, second], axis=0)
+
+
+def y_shift(x, shift):
+    return lax.ppermute(
+        x, "exp", [(i, (i + NZ * shift) % (NY * NZ)) for i in range(NY * NZ)]
+    )
+
+
+def ring_sum_over_y(x):
+    y = lax.axis_index("exp") // NZ
+    count = x.shape[0] // NY
+    split = 512
+    far = rows_at(x, (y + 2) % NY, count)
+    up = rows_at(x, (y + 1) % NY, count)
+    down = rows_at(x, (y + 3) % NY, count)
+    from_down = y_shift(far[:, :split], 1)
+    from_up = y_shift(far[:, split:], 3)
+    up_sum = (up[:, :split].astype(jnp.float32) + from_down.astype(jnp.float32)).astype(x.dtype)
+    down_sum = (down[:, split:].astype(jnp.float32) + from_up.astype(jnp.float32)).astype(x.dtype)
+    up_late = y_shift(up[:, split:], 1)
+    down_late = y_shift(down[:, :split], 3)
+    up_sum = y_shift(up_sum, 1)
+    down_sum = y_shift(down_sum, 3)
+    own = rows_at(x, y, count).astype(jnp.float32)
+    left = own[:, :split] + up_sum.astype(jnp.float32) + down_late.astype(jnp.float32)
+    right = own[:, split:] + up_late.astype(jnp.float32) + down_sum.astype(jnp.float32)
+    return jnp.concatenate([left, right], axis=1)
 
 
 def unit_backward(gate_sum, up_sum, back_sum, slot_prob):
@@ -89,6 +142,9 @@
     send_prob = jnp.dot(
         chosen, probs.reshape(-1).astype(jnp.float32), precision=lax.Precision.HIGHEST
     ).reshape(exp_count, capacity)
+    send_input = jnp.dot(slot_owner, moe_input, preferred_element_type=jnp.float32).astype(
+        jnp.bfloat16
+    )
     packed = jnp.concatenate(
         [
             jnp.broadcast_to(local_max[None], (exp_count, row_count)),
@@ -102,30 +158,30 @@
     row_max = jnp.max(all_max, axis=0)
     row_total = jnp.sum(packed[:, row_count : 2 * row_count] * jnp.exp(all_max - row_max), axis=0)
     flat_prob = packed[:, 2 * row_count : 2 * row_count + capacity].reshape(-1)
-    rows = jnp.stack([row_max, row_total, token_weights, token_ids.astype(jnp.float32)])
-    rows = lax.all_gather(rows, "ctx", axis=1, tiled=True)
-    row_max, row_total, weights = rows[0], rows[1], rows[2]
-    all_ids = rows[3].astype(jnp.int32)
-
-    send_input = jnp.dot(slot_owner, moe_input, preferred_element_type=jnp.float32).astype(
-        jnp.bfloat16
-    )
+    rows = jnp.concatenate([row_max, row_total, token_weights, token_ids.astype(jnp.float32)])
+    rows = exchange(jnp.broadcast_to(rows[None], (ctx_count, 4 * row_count)), "ctx")
+    rows = rows.reshape(ctx_count, 4, row_count).transpose(1, 0, 2).reshape(4, seq_length)
+    rows, send_input, all_logits = lax.optimization_barrier((rows, send_input, all_logits))
     flat_inputs = exchange(send_input, "exp")
+
     gate_w = w_gate[0]
     up_w = w_up[0]
     down_w = w_down[0]
     part_gate = jnp.dot(flat_inputs, gate_w, preferred_element_type=jnp.float32)
     part_up = jnp.dot(flat_inputs, up_w, preferred_element_type=jnp.float32)
-    gate_sum, up_sum = lax.psum((part_gate, part_up), "ctx")
-
-    storage = jnp.arange(seq_length, dtype=jnp.int32)
-    slab_match = (
-        jnp.arange(slab_order.shape[0], dtype=jnp.int32)[None, :] == (storage // SLAB)[:, None]
-    )
-    placed_slab = jnp.sum(jnp.where(slab_match, slab_order[None, :], 0), axis=1)
-    position = placed_slab * SLAB + storage % SLAB
+    part_both = jnp.concatenate(
+        [part_gate.astype(jnp.float16), part_up.astype(jnp.float16)], axis=1
+    )
+    both_sum = sum_over_ctx(part_both)
+    row_max, row_total, weights = rows[0], rows[1], rows[2]
+    all_ids = rows[3].astype(jnp.int32)
+
+    slab_count = slab_order.shape[0]
+    next_ids = jnp.concatenate([all_ids[1:], all_ids[-1:]]).reshape(slab_count, SLAB)
+    slab_match = slab_order[:, None] == jnp.arange(slab_count, dtype=jnp.int32)[None, :]
+    target = jnp.sum(jnp.where(slab_match[:, :, None], next_ids[None], 0), axis=1).reshape(-1)
+    position = (slab_order[:, None] * SLAB + jnp.arange(SLAB, dtype=jnp.int32)).reshape(-1)
     has_target = position < seq_length - 1
-    target = jnp.take(all_ids, jnp.minimum(position + 1, seq_length - 1))
     local_target = target - lax.axis_index("exp") * vocab_width
     weighting = jnp.where(has_target, weights, 0.0)
     is_target = jnp.arange(vocab_width, dtype=jnp.int32)[None, :] == local_target[:, None]
@@ -137,7 +193,7 @@
         )
     ).astype(jnp.bfloat16)
     partial = jnp.dot(logit_grads, head_weight, preferred_element_type=jnp.float32)
-    over_y = exchange_sum((partial * 4096.0).astype(jnp.float16), "exp", Y_GROUPS, NY)
+    over_y = ring_sum_over_y((partial * 4096.0).astype(jnp.float16))
     upstream = exchange_sum(over_y.astype(jnp.float16), "exp", Z_GROUPS, NZ) * (1.0 / 4096.0)
     upstream_sent = upstream.astype(jnp.bfloat16)
 
@@ -145,6 +201,9 @@
         jnp.bfloat16
     )
     flat_upstream = exchange(send_upstream, "exp")
+    flat_upstream, both_sum = lax.optimization_barrier((flat_upstream, both_sum))
+    gate_sum = both_sum[:, : gate_w.shape[1]]
+    up_sum = both_sum[:, gate_w.shape[1] :]
     part_back = lax.dot_general(
         flat_upstream, down_w, CONTRACT_LAST, preferred_element_type=jnp.float32
     )
@@ -153,8 +212,7 @@
     input_grad = lax.dot_general(
         gate_grad, gate_w, CONTRACT_LAST, preferred_element_type=jnp.float32
     ) + lax.dot_general(up_grad, up_w, CONTRACT_LAST, preferred_element_type=jnp.float32)
-    prob_high = lax.reduce_precision(prob_grad, 8, 7)
-    prob_low = prob_grad - prob_high
+    prob_high, prob_low = split_high(prob_grad)
     lane = jnp.arange(128, dtype=jnp.int32)[None, :]
     prob_block = jnp.where(
         lane == 0, prob_high[:, None], jnp.where(lane == 1, prob_low[:, None], 0)

time: 298 us -> 256 us (0.86)
  blocking collectives: 108 us -> 34 us
  starting transfers between devices: 29 us -> 61.3 us
  waiting for transfers between devices: 95 us -> 84.8 us
  other arithmetic: 11.1 us -> 20.5 us
    all_to_all x5 -> x1, blocking collectives: 96.3 us -> 34 us  [exchange(): return lax.all_to_all(x, axis, 0, 0, tiled=True, axis_index_groups=groups)]
    ppermute x1 -> x22, waiting for transfers between devices: 0.83 us -> 34.2 us  [the longest x12 23.9 us: ctx_shift(): return lax.ppermute(x, 'ctx', [(i, (i + 2 * shift) % 8) for i in range(8)])]
    psum x1 -> x0, waiting for transfers between devices: 32.8 us -> none  [local(): gate_sum, up_sum = lax.psum((part_gate, part_up), 'ctx')]
    ppermute x1 -> x22, starting transfers between devices: 0.01 us -> 24.6 us  [the longest x12 16 us: ctx_shift(): return lax.ppermute(x, 'ctx', [(i, (i + 2 * shift) % 8) for i in range(8)])]
    all_to_all x4 -> x5, waiting for transfers between devices: 60.5 us -> 43.7 us  [exchange(): return lax.all_to_all(x, axis, 0, 0, tiled=True, axis_index_groups=groups)]
    all_gather x1 -> x0, blocking collectives: 11.9 us -> none  [local(): rows = lax.all_gather(rows, 'ctx', axis=1, tiled=True)]
    all_to_all x4 -> x5, starting transfers between devices: 28.9 us -> 36.7 us  [exchange(): return lax.all_to_all(x, axis, 0, 0, tiled=True, axis_index_groups=groups)]
    all_gather x1, waiting for transfers between devices: 0.15 us -> 6.3 us  [local(): all_logits = lax.all_gather(logits, 'ctx', axis=0, tiled=True)]
  transfers between devices with their start and end apart: 7 -> 28, of which waited for: 7 -> 21; matrix products, arithmetic and copies ran while one was open for 9% -> 15% of each run, Pallas kernels for 0% -> 0%
where the time goes in v2:
time: 256 us; the launch traced here: 255 us
  waiting for transfers between devices  84.8 us (33%)
  starting transfers between devices  61.3 us (24%)
  blocking collectives  34 us (13%)
  matrix products  26.6 us (10%)
  other arithmetic  20.5 us (8%)
  between operations  14.6 us (6%)
  local copies, waits for them, and re-layouts  12.8 us (5%)
    all_to_all x5, waiting for transfers between devices, exchange(): return lax.all_to_all(x, axis, 0, 0, tiled=True, axis_index_groups=groups)  43.7 us
    all_to_all x5, starting transfers between devices, exchange(): return lax.all_to_all(x, axis, 0, 0, tiled=True, axis_index_groups=groups)  36.7 us
    all_to_all x1, blocking collectives, exchange(): return lax.all_to_all(x, axis, 0, 0, tiled=True, axis_index_groups=groups)  34 us
    ppermute x12, waiting for transfers between devices, ctx_shift(): return lax.ppermute(x, 'ctx', [(i, (i + 2 * shift) % 8) for i in range(8)])  23.9 us
    ppermute x12, starting transfers between devices, ctx_shift(): return lax.ppermute(x, 'ctx', [(i, (i + 2 * shift) % 8) for i in range(8)])  16 us
    dot_general x1, matrix products, local(): jnp.dot(logit_grads, head_weight, preferred_element_type=jnp.float32)  10.2 us
    ppermute x6, starting transfers between devices, y_shift(): lax.ppermute(x, 'exp', [(i, (i + NZ * shift) % (NY * NZ)) for i in range(...  8.31 us
    ppermute x6, waiting for transfers between devices, y_shift(): lax.ppermute(x, 'exp', [(i, (i + NZ * shift) % (NY * NZ)) for i in range(...  6.59 us
  transfers between devices with their start and end apart: 28, of which 21 were waited for; matrix products, arithmetic and copies ran while one was open for 15% of the time, Pallas kernels for 0%

profile of v2, /device:TPU:32, one launch (start us, length us, event | category | flops | bytes accessed | tf_op | source)
XLA Modules:
  0.0 254.7 jit_solution(15461884064766667386)
XLA Ops:
  10.6 1.3 reduce_max.23
  11.9 1.5 exponential_reduce_fusion
  14.6 11.4 %all-to-all-start = ((f32[32,1,384]{2,1,0:T(1,128)}), f32[32,1,384]{2,1,0:T(1,128)S(1)}, u32[]{:S(2)}, u32[]{:S(2)}) async-start(f32[32,1,384]{2,1,0:T(1,128)} %all_to_all.40), calls=%async_computation | async-start | bytes 98304 | tf_op jit(solution)/shard_map/all_to_all | solution.py:13
  26.4 1.4 convolution_convert_fusion.1
  27.8 7.1 %all-to-all-done = f32[32,1,384]{2,1,0:T(1,128)S(1)} async-done(((f32[32,1,384]{2,1,0:T(1,128)}), f32[32,1,384]{2,1,0:T(1,128)S(1)}, u32[]{:S(2)}, u32[]{:S(2)}) %all-to-all-start) | async-done | bytes 49184 | tf_op jit(solution)/shard_map/all_to_all | solution.py:13
  35.6 4.3 %all-to-all-start.1 = ((f32[8,1,512]{2,1,0:T(1,128)}), f32[8,1,512]{2,1,0:T(1,128)S(1)}, u32[]{:S(2)}, u32[]{:S(2)}) async-start(f32[8,1,512]{2,1,0:T(1,128)} %broadcast_in_dim.104), calls=%async_computation.1 | async-start | bytes 32768 | tf_op jit(solution)/shard_map/all_to_all | solution.py:13
  40.2 5.3 %all-to-all-done.1 = f32[8,1,512]{2,1,0:T(1,128)S(1)} async-done(((f32[8,1,512]{2,1,0:T(1,128)}), f32[8,1,512]{2,1,0:T(1,128)S(1)}, u32[]{:S(2)}, u32[]{:S(2)}) %all-to-all-start.1) | async-done | bytes 16416 | tf_op jit(solution)/shard_map/all_to_all | solution.py:13
  45.4 6.3 %all-gather.2.cloned.1.call-done = bf16[1024,2560]{1,0:T(8,128)(2,1)} async-done(((bf16[128,2560]{1,0:T(8,128)(2,1)}), bf16[1024,2560]{1,0:T(8,128)(2,1)}) %all-gather.2.cloned.1.call-update) | async-done | bytes 5242896 | tf_op jit(solution)/shard_map/all_gather | solution.py:120
  53.4 10.1 %all-to-all-start.4 = ((bf16[32,16,896]{2,1,0:T(8,128)(2,1)}), bf16[32,16,896]{2,1,0:T(8,128)(2,1)S(1)}, u32[]{:S(2)}, u32[]{:S(2)}) async-start(bf16[32,16,896]{2,1,0:T(8,128)(2,1)} %bitcast.15), calls=%async_computation.4 | async-start | bytes 1835008 | tf_op jit(solution)/shard_map/all_to_all | solution.py:13
  63.5 10.2 %multiply_convert_fusion.2 = f16[1024,896]{1,0:T(8,128)(2,1)S(1)} fusion(bf16[2560,896]{1,0:T(8,128)(2,1)} %param.12, bf16[1024,2560]{1,0:T(8,128)(2,1)} %all-gather.2.cloned.1.call-done, s32[1024]{0:T(1024)S(1)} %sub.90, f32[1024]{0:T(1024)S(1)} %bitcast.90, f32[1024]{0:T(1024)S(1)} %bitcast.91, f32[1024]{0:T(1024)S(1)} %broadcast_select_fusion.4), kind=kOutput, calls=%fused_computation.3 | convolution fusion | flops 4720427008 | bytes 11681792 | tf_op jit(solution)/shard_map/dot_general | solution.py:195
  74.7 2.7 %collective-permute-start.4 = (f16[256,384]{1,0:T(8,128)(2,1)}, f16[256,384]{1,0:T(8,128)(2,1)}, u32[]{:S(2)}, u32[]{:S(2)}) collective-permute-start(f16[256,384]{1,0:T(8,128)(2,1)} %get-tuple-element.21), channel_id=1, source_target_pairs={{0,24},{1,25},{2,26},{3,27},{4,28},{5,29},{6,30},{7,31},{8,0},{9,1... | collective-permute-start | bytes 589832 | tf_op jit(solution)/shard_map/ppermute | solution.py:65
  78.2 3.2 %collective-permute-start.2 = (f16[256,512]{1,0:T(8,128)(2,1)S(1)}, f16[256,512]{1,0:T(8,128)(2,1)S(1)}, u32[]{:S(2)}, u32[]{:S(2)}) collective-permute-start(f16[256,512]{1,0:T(8,128)(2,1)S(1)} %get-tuple-element.19), channel_id=1, source_target_pairs={{0,24},{1,25},{2,26},{3,27},{4,28},{5,29},{6,30},{7,31},{8,0},{9,1... | collective-permute-start | bytes 786440 | tf_op jit(solution)/shard_map/ppermute | solution.py:65
  81.5 8.3 %all-to-all-done.4 = bf16[32,16,896]{2,1,0:T(8,128)(2,1)S(1)} async-done(((bf16[32,16,896]{2,1,0:T(8,128)(2,1)}), bf16[32,16,896]{2,1,0:T(8,128)(2,1)S(1)}, u32[]{:S(2)}, u32[]{:S(2)}) %all-to-all-start.4) | async-done | bytes 917536 | tf_op jit(solution)/shard_map/all_to_all | solution.py:13
  89.8 2.7 %fusion.19 = f16[512,1024]{1,0:T(8,128)(2,1)S(1)} fusion(bf16[512,896]{1,0:T(8,128)(2,1)S(1)} %bitcast.79, bf16[1,896,1024]{2,1,0:T(8,128)(2,1)} %param.19), kind=kOutput, calls=%fused_computation.32 | convolution fusion | flops 940048384 | bytes 3801088 | tf_op jit(solution)/shard_map/dot_general | solution.py:170
  92.5 1.3 fusion.22
  96.3 1.4 collective-permute-start.5
  99.8 3.0 %collective-permute-done.5 = f16[256,384]{1,0:T(8,128)(2,1)S(1)} collective-permute-done((f16[256,384]{1,0:T(8,128)(2,1)S(1)}, f16[256,384]{1,0:T(8,128)(2,1)S(1)}, u32[]{:S(2)}, u32[]{:S(2)}) %collective-permute-start.5) | collective-permute-done | bytes 196640 | tf_op jit(solution)/shard_map/ppermute | solution.py:65
  103.7 3.6 %collective-permute-done.1 = f16[256,512]{1,0:T(8,128)(2,1)S(1)} collective-permute-done((f16[256,512]{1,0:T(8,128)(2,1)S(1)}, f16[256,512]{1,0:T(8,128)(2,1)S(1)}, u32[]{:S(2)}, u32[]{:S(2)}) %collective-permute-start.1) | collective-permute-done | bytes 262176 | tf_op jit(solution)/shard_map/ppermute | solution.py:65
  108.9 1.7 collective-permute-start.9
  110.7 1.5 collective-permute-start.8
  113.6 4.0 %all-to-all-start.2 = ((f16[8,32,896]{2,1,0:T(8,128)(2,1)}), f16[8,32,896]{2,1,0:T(8,128)(2,1)S(1)}, u32[]{:S(2)}, u32[]{:S(2)}) async-start(f16[8,32,896]{2,1,0:T(8,128)(2,1)} %pad_maximum_fusion.2), calls=%async_computation.2 | async-start | bytes 917504 | tf_op jit(solution)/shard_map/all_to_all | solution.py:13
  117.6 2.4 collective-permute-done.9
  120.9 1.8 collective-permute-done.7
  122.9 2.0 constant_dynamic-update-slice_fusion.7
  126.2 3.0 %collective-permute-start.11 = (f16[64,2048]{1,0:T(8,128)(2,1)}, f16[64,2048]{1,0:T(8,128)(2,1)S(1)}, u32[]{:S(2)}, u32[]{:S(2)}) collective-permute-start(f16[64,2048]{1,0:T(8,128)(2,1)} %get-tuple-element.15), channel_id=1, source_target_pairs={{0,192},{32,224},{64,0},{96,32},{128,64},{160,96},{192,128},{224,1... | collective-permute-start | bytes 786440 | tf_op jit(solution)/shard_map/ppermute | solution.py:28
  130.4 1.9 collective-permute-start.12
  132.3 3.3 %collective-permute-done.10 = f16[64,2048]{1,0:T(8,128)(2,1)S(1)} collective-permute-done((f16[64,2048]{1,0:T(8,128)(2,1)}, f16[64,2048]{1,0:T(8,128)(2,1)S(1)}, u32[]{:S(2)}, u32[]{:S(2)}) %collective-permute-start.10) | collective-permute-done | bytes 262176 | tf_op jit(solution)/shard_map/ppermute | solution.py:28
  136.4 2.7 %collective-permute-done.11 = f16[64,2048]{1,0:T(8,128)(2,1)S(1)} collective-permute-done((f16[64,2048]{1,0:T(8,128)(2,1)}, f16[64,2048]{1,0:T(8,128)(2,1)S(1)}, u32[]{:S(2)}, u32[]{:S(2)}) %collective-permute-start.11) | collective-permute-done | bytes 262176 | tf_op jit(solution)/shard_map/ppermute | solution.py:28
  140.6 1.4 convolution_convert_fusion
  142.0 6.9 %all-to-all-start.3 = ((bf16[32,16,896]{2,1,0:T(8,128)(2,1)}), bf16[32,16,896]{2,1,0:T(8,128)(2,1)}, u32[]{:S(2)}, u32[]{:S(2)}) async-start(bf16[32,16,896]{2,1,0:T(8,128)(2,1)} %bitcast.77), calls=%async_computation.3 | async-start | bytes 1835008 | tf_op jit(solution)/shard_map/all_to_all | solution.py:13
  149.0 2.0 broadcast_select_fusion.1
  150.9 2.4 maximum_convert_fusion
  153.4 21.7 %all-to-all-done.3 = bf16[32,16,896]{2,1,0:T(8,128)(2,1)} async-done(((bf16[32,16,896]{2,1,0:T(8,128)(2,1)}), bf16[32,16,896]{2,1,0:T(8,128)(2,1)}, u32[]{:S(2)}, u32[]{:S(2)}) %all-to-all-start.3) | async-done | bytes 917536 | tf_op jit(solution)/shard_map/all_to_all | solution.py:13
  175.1 3.1 %fusion.25 = f16[512,1024]{1,0:T(8,128)(2,1)S(1)} fusion(bf16[512,896]{1,0:T(8,128)(2,1)} %bitcast.14, bf16[1,1024,896]{2,1,0:T(8,128)(2,1)} %param.21), kind=kOutput, calls=%fused_computation.34 | convolution fusion | flops 940048384 | bytes 3801088 | tf_op jit(solution)/shard_map/dot_general | solution.py:207
  178.4 1.9 collective-permute-done.14
  180.6 1.4 collective-permute-start.17
  184.0 4.5 %collective-permute-done.17 = f16[64,1024]{1,0:T(8,128)(2,1)S(1)} collective-permute-done((f16[64,1024]{1,0:T(8,128)(2,1)S(1)}, f16[64,1024]{1,0:T(8,128)(2,1)S(1)}, u32[]{:S(2)}, u32[]{:S(2)}) %collective-permute-start.17) | collective-permute-done | bytes 131104 | tf_op jit(solution)/shard_map/ppermute | solution.py:28
  188.5 1.6 collective-permute-done.16
  190.8 3.2 %collective-permute-start.19 = (f16[64,1024]{1,0:T(8,128)(2,1)S(1)}, f16[64,1024]{1,0:T(8,128)(2,1)S(1)}, u32[]{:S(2)}, u32[]{:S(2)}) collective-permute-start(f16[64,1024]{1,0:T(8,128)(2,1)S(1)} %get-tuple-element.13), channel_id=1, source_target_pairs={{0,192},{32,224},{64,0},{96,32},{128,64},{160,96},{192,128},{224,1... | collective-permute-start | bytes 393224 | tf_op jit(solution)/shard_map/ppermute | solution.py:28
  194.5 2.5 collective-permute-done.18
  197.0 2.1 collective-permute-done.19
  199.1 1.5 collective-permute-done.20
  200.9 1.8 collective-permute-done.21
  203.0 3.2 %fusion.7 = f32[512]{0:T(512)S(1)} fusion(f32[512,2048]{1,0:T(8,128)} %maximum_convert_fusion, f16[256,1024]{1,0:T(8,128)(2,1)S(1)} %get-tuple-element.23, f16[256,1024]{1,0:T(8,128)(2,1)S(1)} %get-tuple-element.22), kind=kLoop, calls=%fused_computation.16 | loop fusion | flops 4718080 | bytes 5244928 | tf_op jit(solution)/shard_map/reduce_sum | solution.py:94
  206.4 1.5 fusion.11
  208.0 1.8 add_convert_fusion.1
  210.1 34.0 %all_to_all.60 = bf16[32,16,1024]{2,1,0:T(8,128)(2,1)S(1)} all-to-all(bf16[32,16,1024]{2,1,0:T(8,128)(2,1)S(1)} %bitcast.76), channel_id=1, replica_groups=mesh['ctx'=8,'exp'=32] {'exp'}, dimensions={0} | all-to-all | bytes 2097152 | tf_op jit(solution)/shard_map/all_to_all | solution.py:13
  245.3 1.9 fusion.42
  (121 shorter events, 30.3 us)
Async XLA Ops:
  7.2 85.4 %copy-start = (bf16[1,896,1024]{2,1,0:T(8,128)(2,1)S(1)}, bf16[1,896,1024]{2,1,0:T(8,128)(2,1)}, u32[]{:S(2)}) copy-start(bf16[1,896,1024]{2,1,0:T(8,128)(2,1)} %param.20) | copy-start | bytes 5505028
  7.2 19.1 %copy-start.7 = (s32[16]{0:T(128)S(1)}, s32[16]{0:T(128)}, u32[]{:S(2)}) copy-start(s32[16]{0:T(128)} %param.14) | copy-start | bytes 196
  7.2 19.2 %copy-start.6 = (bf16[32,896]{1,0:T(8,128)(2,1)S(1)}, bf16[32,896]{1,0:T(8,128)(2,1)}, u32[]{:S(2)}) copy-start(bf16[32,896]{1,0:T(8,128)(2,1)} %param.16) | copy-start | bytes 172036
  7.2 20.6 %copy-start.10 = (s32[128]{0:T(128)S(1)}, s32[128]{0:T(128)}, u32[]{:S(2)}) copy-start(s32[128]{0:T(128)} %param.13) | copy-start | bytes 1540
  7.2 27.8 %copy-start.8 = (f32[128]{0:T(128)S(1)}, f32[128]{0:T(128)}, u32[]{:S(2)}) copy-start(f32[128]{0:T(128)} %param.15) | copy-start | bytes 1540
  7.2 44.5 %all-gather.2.cloned.1.call-start = ((), (), s32[]{:S(2)}) async-start(), calls=%async_computation.6 | async-start | bytes 5898240 | tf_op jit(solution)/shard_map/all_gather | solution.py:120
  14.6 20.3 %all-to-all-start = ((f32[32,1,384]{2,1,0:T(1,128)}), f32[32,1,384]{2,1,0:T(1,128)S(1)}, u32[]{:S(2)}, u32[]{:S(2)}) async-start(f32[32,1,384]{2,1,0:T(1,128)} %all_to_all.40), calls=%async_computation | async-start | bytes 98304 | tf_op jit(solution)/shard_map/all_to_all | solution.py:13
  35.6 9.8 %all-to-all-start.1 = ((f32[8,1,512]{2,1,0:T(1,128)}), f32[8,1,512]{2,1,0:T(1,128)S(1)}, u32[]{:S(2)}, u32[]{:S(2)}) async-start(f32[8,1,512]{2,1,0:T(1,128)} %broadcast_in_dim.104), calls=%async_computation.1 | async-start | bytes 32768 | tf_op jit(solution)/shard_map/all_to_all | solution.py:13
  53.4 36.3 %all-to-all-start.4 = ((bf16[32,16,896]{2,1,0:T(8,128)(2,1)}), bf16[32,16,896]{2,1,0:T(8,128)(2,1)S(1)}, u32[]{:S(2)}, u32[]{:S(2)}) async-start(bf16[32,16,896]{2,1,0:T(8,128)(2,1)} %bitcast.15), calls=%async_computation.4 | async-start | bytes 1835008 | tf_op jit(solution)/shard_map/all_to_all | solution.py:13
  73.7 3.7 %copy-start.4 = (f16[1024,896]{1,0:T(8,128)(2,1)}, f16[1024,896]{1,0:T(8,128)(2,1)S(1)}, u32[]{:S(2)}) copy-start(f16[1024,896]{1,0:T(8,128)(2,1)S(1)} %multiply_convert_fusion.2) | copy-start | bytes 5505028
  74.7 19.5 %collective-permute-start.4 = (f16[256,384]{1,0:T(8,128)(2,1)}, f16[256,384]{1,0:T(8,128)(2,1)}, u32[]{:S(2)}, u32[]{:S(2)}) collective-permute-start(f16[256,384]{1,0:T(8,128)(2,1)} %get-tuple-element.21), channel_id=1, source_target_pairs={{0,24},{1,25},{2,26},{3,27},{4,28},{5,29},{6,30},{7,31},{8,0},{9,1... | collective-permute-start | bytes 589832 | tf_op jit(solution)/shard_map/ppermute | solution.py:65
  77.4 22.3 %collective-permute-start.3 = (f16[256,384]{1,0:T(8,128)(2,1)}, f16[256,384]{1,0:T(8,128)(2,1)}, u32[]{:S(2)}, u32[]{:S(2)}) collective-permute-start(f16[256,384]{1,0:T(8,128)(2,1)} %get-tuple-element.20), channel_id=1, source_target_pairs={{0,8},{1,9},{2,10},{3,11},{4,12},{5,13},{6,14},{7,15},{8,16},{9,17... | collective-permute-start | bytes 589832 | tf_op jit(solution)/shard_map/ppermute | solution.py:65
  78.2 25.5 %collective-permute-start.2 = (f16[256,512]{1,0:T(8,128)(2,1)S(1)}, f16[256,512]{1,0:T(8,128)(2,1)S(1)}, u32[]{:S(2)}, u32[]{:S(2)}) collective-permute-start(f16[256,512]{1,0:T(8,128)(2,1)S(1)} %get-tuple-element.19), channel_id=1, source_target_pairs={{0,24},{1,25},{2,26},{3,27},{4,28},{5,29},{6,30},{7,31},{8,0},{9,1... | collective-permute-start | bytes 786440 | tf_op jit(solution)/shard_map/ppermute | solution.py:65
  81.5 16.3 %collective-permute-start = (f16[256,512]{1,0:T(8,128)(2,1)}, f16[256,512]{1,0:T(8,128)(2,1)}, u32[]{:S(2)}, u32[]{:S(2)}) collective-permute-start(f16[256,512]{1,0:T(8,128)(2,1)} %get-tuple-element.18), channel_id=1, source_target_pairs={{0,8},{1,9},{2,10},{3,11},{4,12},{5,13},{6,14},{7,15},{8,16},{9,17... | collective-permute-start | bytes 786440 | tf_op jit(solution)/shard_map/ppermute | solution.py:65
  93.8 1.5 copy-start.5
  94.1 13.4 %collective-permute-start.6 = (f16[256,2048]{1,0:T(8,128)(2,1)S(1)}, f16[256,2048]{1,0:T(8,128)(2,1)S(1)}, u32[]{:S(2)}, u32[]{:S(2)}) collective-permute-start(f16[256,2048]{1,0:T(8,128)(2,1)S(1)} %fusion.31), channel_id=1, source_target_pairs={{0,32},{32,0},{64,96},{96,64},{128,160},{160,128},{192,224},{224,1... | collective-permute-start | bytes 3145736 | tf_op jit(solution)/shard_map/ppermute | solution.py:32
  96.3 6.4 %collective-permute-start.5 = (f16[256,384]{1,0:T(8,128)(2,1)S(1)}, f16[256,384]{1,0:T(8,128)(2,1)S(1)}, u32[]{:S(2)}, u32[]{:S(2)}) collective-permute-start(f16[256,384]{1,0:T(8,128)(2,1)S(1)} %add_convert_fusion.5), channel_id=1, source_target_pairs={{0,24},{1,25},{2,26},{3,27},{4,28},{5,29},{6,30},{7,31},{8,0},{9,1... | collective-permute-start | bytes 589832 | tf_op jit(solution)/shard_map/ppermute | solution.py:65
  98.8 8.6 %collective-permute-start.1 = (f16[256,512]{1,0:T(8,128)(2,1)S(1)}, f16[256,512]{1,0:T(8,128)(2,1)S(1)}, u32[]{:S(2)}, u32[]{:S(2)}) collective-permute-start(f16[256,512]{1,0:T(8,128)(2,1)S(1)} %add_convert_fusion.4), channel_id=1, source_target_pairs={{0,8},{1,9},{2,10},{3,11},{4,12},{5,13},{6,14},{7,15},{8,16},{9,17... | collective-permute-start | bytes 786440 | tf_op jit(solution)/shard_map/ppermute | solution.py:65
  108.9 11.0 %collective-permute-start.9 = (f16[64,2048]{1,0:T(8,128)(2,1)}, f16[64,2048]{1,0:T(8,128)(2,1)}, u32[]{:S(2)}, u32[]{:S(2)}) collective-permute-start(f16[64,2048]{1,0:T(8,128)(2,1)} %get-tuple-element.25), channel_id=1, source_target_pairs={{0,128},{32,160},{64,192},{96,224},{128,0},{160,32},{192,64},{224,... | collective-permute-start | bytes 786440 | tf_op jit(solution)/shard_map/ppermute | solution.py:28
  110.7 10.3 %collective-permute-start.8 = (f16[64,2048]{1,0:T(8,128)(2,1)}, f16[64,2048]{1,0:T(8,128)(2,1)}, u32[]{:S(2)}, u32[]{:S(2)}) collective-permute-start(f16[64,2048]{1,0:T(8,128)(2,1)} %get-tuple-element.26), channel_id=1, source_target_pairs={{0,192},{32,224},{64,0},{96,32},{128,64},{160,96},{192,128},{224,1... | collective-permute-start | bytes 786440 | tf_op jit(solution)/shard_map/ppermute | solution.py:28
  112.1 10.6 %collective-permute-start.7 = (f16[64,2048]{1,0:T(8,128)(2,1)}, f16[64,2048]{1,0:T(8,128)(2,1)}, u32[]{:S(2)}, u32[]{:S(2)}) collective-permute-start(f16[64,2048]{1,0:T(8,128)(2,1)} %get-tuple-element.24), channel_id=1, source_target_pairs={{0,64},{32,96},{64,128},{96,160},{128,192},{160,224},{192,0},{224,... | collective-permute-start | bytes 786440 | tf_op jit(solution)/shard_map/ppermute | solution.py:28
  113.6 16.8 %all-to-all-start.2 = ((f16[8,32,896]{2,1,0:T(8,128)(2,1)}), f16[8,32,896]{2,1,0:T(8,128)(2,1)S(1)}, u32[]{:S(2)}, u32[]{:S(2)}) async-start(f16[8,32,896]{2,1,0:T(8,128)(2,1)} %pad_maximum_fusion.2), calls=%async_computation.2 | async-start | bytes 917504 | tf_op jit(solution)/shard_map/all_to_all | solution.py:13
  124.9 1.0 copy-start.2
  125.9 9.7 %collective-permute-start.10 = (f16[64,2048]{1,0:T(8,128)(2,1)}, f16[64,2048]{1,0:T(8,128)(2,1)S(1)}, u32[]{:S(2)}, u32[]{:S(2)}) collective-permute-start(f16[64,2048]{1,0:T(8,128)(2,1)} %get-tuple-element.15), channel_id=1, source_target_pairs={{0,64},{32,96},{64,128},{96,160},{128,192},{160,224},{192,0},{224,... | collective-permute-start | bytes 786440 | tf_op jit(solution)/shard_map/ppermute | solution.py:28
  126.2 13.0 %collective-permute-start.11 = (f16[64,2048]{1,0:T(8,128)(2,1)}, f16[64,2048]{1,0:T(8,128)(2,1)S(1)}, u32[]{:S(2)}, u32[]{:S(2)}) collective-permute-start(f16[64,2048]{1,0:T(8,128)(2,1)} %get-tuple-element.15), channel_id=1, source_target_pairs={{0,192},{32,224},{64,0},{96,32},{128,64},{160,96},{192,128},{224,1... | collective-permute-start | bytes 786440 | tf_op jit(solution)/shard_map/ppermute | solution.py:28
  130.4 9.4 %collective-permute-start.12 = (f16[64,2048]{1,0:T(8,128)(2,1)}, f16[64,2048]{1,0:T(8,128)(2,1)S(1)}, u32[]{:S(2)}, u32[]{:S(2)}) collective-permute-start(f16[64,2048]{1,0:T(8,128)(2,1)} %get-tuple-element.15), channel_id=1, source_target_pairs={{0,128},{32,160},{64,192},{96,224},{128,0},{160,32},{192,64},{224,... | collective-permute-start | bytes 786440 | tf_op jit(solution)/shard_map/ppermute | solution.py:28
  140.6 8.3 %copy-start.3 = (f16[256,2048]{1,0:T(8,128)(2,1)S(1)}, f16[256,2048]{1,0:T(8,128)(2,1)}, u32[]{:S(2)}) copy-start(f16[256,2048]{1,0:T(8,128)(2,1)} %constant_dynamic-update-slice_fusion.4) | copy-start | bytes 3145732
  140.6 8.3 %collective-permute-start.13 = (f16[256,2048]{1,0:T(8,128)(2,1)}, f16[256,2048]{1,0:T(8,128)(2,1)}, u32[]{:S(2)}, u32[]{:S(2)}) collective-permute-start(f16[256,2048]{1,0:T(8,128)(2,1)} %constant_dynamic-update-slice_fusion.4), channel_id=1, source_target_pairs={{0,32},{32,0},{64,96},{96,64},{128,160},{160,128},{192,224},{224,1... | collective-permute-start | bytes 3145736 | tf_op jit(solution)/shard_map/ppermute | solution.py:32
  142.0 33.1 %all-to-all-start.3 = ((bf16[32,16,896]{2,1,0:T(8,128)(2,1)}), bf16[32,16,896]{2,1,0:T(8,128)(2,1)}, u32[]{:S(2)}, u32[]{:S(2)}) async-start(bf16[32,16,896]{2,1,0:T(8,128)(2,1)} %bitcast.77), calls=%async_computation.3 | async-start | bytes 1835008 | tf_op jit(solution)/shard_map/all_to_all | solution.py:13
  178.3 2.0 collective-permute-start.14
  180.6 7.9 %collective-permute-start.17 = (f16[64,1024]{1,0:T(8,128)(2,1)S(1)}, f16[64,1024]{1,0:T(8,128)(2,1)S(1)}, u32[]{:S(2)}, u32[]{:S(2)}) collective-permute-start(f16[64,1024]{1,0:T(8,128)(2,1)S(1)} %get-tuple-element.28), channel_id=1, source_target_pairs={{0,128},{32,160},{64,192},{96,224},{128,0},{160,32},{192,64},{224,... | collective-permute-start | bytes 393224 | tf_op jit(solution)/shard_map/ppermute | solution.py:28
  182.0 8.1 %collective-permute-start.16 = (f16[64,1024]{1,0:T(8,128)(2,1)S(1)}, f16[64,1024]{1,0:T(8,128)(2,1)S(1)}, u32[]{:S(2)}, u32[]{:S(2)}) collective-permute-start(f16[64,1024]{1,0:T(8,128)(2,1)S(1)} %get-tuple-element.29), channel_id=1, source_target_pairs={{0,192},{32,224},{64,0},{96,32},{128,64},{160,96},{192,128},{224,1... | collective-permute-start | bytes 393224 | tf_op jit(solution)/shard_map/ppermute | solution.py:28
  183.2 7.3 %collective-permute-start.15 = (f16[64,1024]{1,0:T(8,128)(2,1)S(1)}, f16[64,1024]{1,0:T(8,128)(2,1)S(1)}, u32[]{:S(2)}, u32[]{:S(2)}) collective-permute-start(f16[64,1024]{1,0:T(8,128)(2,1)S(1)} %get-tuple-element.27), channel_id=1, source_target_pairs={{0,64},{32,96},{64,128},{96,160},{128,192},{160,224},{192,0},{224,... | collective-permute-start | bytes 393224 | tf_op jit(solution)/shard_map/ppermute | solution.py:28
  190.7 6.3 %collective-permute-start.18 = (f16[64,1024]{1,0:T(8,128)(2,1)S(1)}, f16[64,1024]{1,0:T(8,128)(2,1)S(1)}, u32[]{:S(2)}, u32[]{:S(2)}) collective-permute-start(f16[64,1024]{1,0:T(8,128)(2,1)S(1)} %get-tuple-element.13), channel_id=1, source_target_pairs={{0,64},{32,96},{64,128},{96,160},{128,192},{160,224},{192,0},{224,... | collective-permute-start | bytes 393224 | tf_op jit(solution)/shard_map/ppermute | solution.py:28
  190.8 8.3 %collective-permute-start.19 = (f16[64,1024]{1,0:T(8,128)(2,1)S(1)}, f16[64,1024]{1,0:T(8,128)(2,1)S(1)}, u32[]{:S(2)}, u32[]{:S(2)}) collective-permute-start(f16[64,1024]{1,0:T(8,128)(2,1)S(1)} %get-tuple-element.13), channel_id=1, source_target_pairs={{0,192},{32,224},{64,0},{96,32},{128,64},{160,96},{192,128},{224,1... | collective-permute-start | bytes 393224 | tf_op jit(solution)/shard_map/ppermute | solution.py:28
  194.0 6.7 %collective-permute-start.20 = (f16[64,1024]{1,0:T(8,128)(2,1)S(1)}, f16[64,1024]{1,0:T(8,128)(2,1)S(1)}, u32[]{:S(2)}, u32[]{:S(2)}) collective-permute-start(f16[64,1024]{1,0:T(8,128)(2,1)S(1)} %get-tuple-element.13), channel_id=1, source_target_pairs={{0,128},{32,160},{64,192},{96,224},{128,0},{160,32},{192,64},{224,... | collective-permute-start | bytes 393224 | tf_op jit(solution)/shard_map/ppermute | solution.py:28
  200.7 2.0 collective-permute-start.21
  203.0 3.5 %copy-start.1 = (f32[512,2048]{1,0:T(8,128)S(1)}, f32[512,2048]{1,0:T(8,128)}, u32[]{:S(2)}) copy-start(f32[512,2048]{1,0:T(8,128)} %maximum_convert_fusion) | copy-start | bytes 12582916
  206.4 1.5 copy-start.9
Sparse Core Ops, SparseCore 0:
  9.9 41.8 all-gather.1

commit v3 on v2

--- a/solution.py
+++ b/solution.py
@@ -36,7 +36,7 @@
     return lax.dynamic_slice_in_dim(x, index * count, count, axis=0)
 
 
-def sum_over_ctx(x):
+def ctx_scatter(x):
     core = lax.axis_index("ctx") % 2
     chip = lax.axis_index("ctx") // 2
     half_rows = x.shape[0] // 2
@@ -50,14 +50,20 @@
     own = rows_at(pair, chip, own_rows).astype(jnp.float32)
     for piece in got:
         own = own + piece.astype(jnp.float32)
-    own = own.astype(jnp.float16)
+    return own
+
+
+def ctx_gather(own):
+    core = lax.axis_index("ctx") % 2
+    chip = lax.axis_index("ctx") // 2
+    own_rows, width = own.shape
     from_one, from_three, from_two = [ctx_shift(own, shift) for shift in (1, 3, 2)]
-    half = jnp.zeros((half_rows, x.shape[1]), jnp.float16)
+    half = jnp.zeros((4 * own_rows, width), own.dtype)
     for piece, shift in ((own, 0), (from_one, 1), (from_three, 3), (from_two, 2)):
         half = lax.dynamic_update_slice_in_dim(half, piece, (chip + 4 - shift) % 4 * own_rows, axis=0)
     other = ctx_swap(half)
-    first = jnp.where(core == 0, half, other).astype(jnp.float32)
-    second = jnp.where(core == 0, other, half).astype(jnp.float32)
+    first = jnp.where(core == 0, half, other)
+    second = jnp.where(core == 0, other, half)
     return jnp.concatenate([first, second], axis=0)
 
 
@@ -67,25 +73,23 @@
     )
 
 
-def ring_sum_over_y(x):
+def ring_sum_over_y(block, far):
     y = lax.axis_index("exp") // NZ
-    count = x.shape[0] // NY
     split = 512
-    far = rows_at(x, (y + 2) % NY, count)
-    up = rows_at(x, (y + 1) % NY, count)
-    down = rows_at(x, (y + 3) % NY, count)
     from_down = y_shift(far[:, :split], 1)
     from_up = y_shift(far[:, split:], 3)
-    up_sum = (up[:, :split].astype(jnp.float32) + from_down.astype(jnp.float32)).astype(x.dtype)
-    down_sum = (down[:, split:].astype(jnp.float32) + from_up.astype(jnp.float32)).astype(x.dtype)
+    up = block((y + 1) % NY)
     up_late = y_shift(up[:, split:], 1)
+    down = block((y + 3) % NY)
     down_late = y_shift(down[:, :split], 3)
+    up_sum = (up[:, :split].astype(jnp.float32) + from_down.astype(jnp.float32)).astype(up.dtype)
     up_sum = y_shift(up_sum, 1)
+    down_sum = (down[:, split:].astype(jnp.float32) + from_up.astype(jnp.float32)).astype(up.dtype)
     down_sum = y_shift(down_sum, 3)
-    own = rows_at(x, y, count).astype(jnp.float32)
+    own = block(y).astype(jnp.float32)
     left = own[:, :split] + up_sum.astype(jnp.float32) + down_late.astype(jnp.float32)
     right = own[:, split:] + up_late.astype(jnp.float32) + down_sum.astype(jnp.float32)
-    return jnp.concatenate([left, right], axis=1)
+    return jnp.concatenate([left, right], axis=1).astype(up.dtype)
 
 
 def unit_backward(gate_sum, up_sum, back_sum, slot_prob):
@@ -161,18 +165,10 @@
     rows = jnp.concatenate([row_max, row_total, token_weights, token_ids.astype(jnp.float32)])
     rows = exchange(jnp.broadcast_to(rows[None], (ctx_count, 4 * row_count)), "ctx")
     rows = rows.reshape(ctx_count, 4, row_count).transpose(1, 0, 2).reshape(4, seq_length)
-    rows, send_input, all_logits = lax.optimization_barrier((rows, send_input, all_logits))
-    flat_inputs = exchange(send_input, "exp")
-
-    gate_w = w_gate[0]
-    up_w = w_up[0]
+    rows, all_logits = lax.optimization_barrier((rows, all_logits))
+
+    both_w = jnp.concatenate([w_gate[0], w_up[0]], axis=1)
     down_w = w_down[0]
-    part_gate = jnp.dot(flat_inputs, gate_w, preferred_element_type=jnp.float32)
-    part_up = jnp.dot(flat_inputs, up_w, preferred_element_type=jnp.float32)
-    part_both = jnp.concatenate(
-        [part_gate.astype(jnp.float16), part_up.astype(jnp.float16)], axis=1
-    )
-    both_sum = sum_over_ctx(part_both)
     row_max, row_total, weights = rows[0], rows[1], rows[2]
     all_ids = rows[3].astype(jnp.int32)
 
@@ -184,48 +180,69 @@
     has_target = position < seq_length - 1
     local_target = target - lax.axis_index("exp") * vocab_width
     weighting = jnp.where(has_target, weights, 0.0)
-    is_target = jnp.arange(vocab_width, dtype=jnp.int32)[None, :] == local_target[:, None]
-    logit_grads = (
-        weighting[:, None]
-        * (
-            jnp.exp(all_logits.astype(jnp.float32) - row_max[:, None]) / row_total[:, None]
-            - is_target.astype(jnp.float32)
-        )
-    ).astype(jnp.bfloat16)
-    partial = jnp.dot(logit_grads, head_weight, preferred_element_type=jnp.float32)
-    over_y = ring_sum_over_y((partial * 4096.0).astype(jnp.float16))
-    upstream = exchange_sum(over_y.astype(jnp.float16), "exp", Z_GROUPS, NZ) * (1.0 / 4096.0)
+    columns = jnp.arange(vocab_width, dtype=jnp.int32)[None, :]
+    per_row = jnp.stack([row_max, row_total, weighting, local_target.astype(jnp.float32)])
+
+    def upstream_block(q):
+        count = seq_length // NY
+        top, total, weight, aim = lax.dynamic_slice_in_dim(per_row, q * count, count, axis=1)
+        is_target = columns == aim.astype(jnp.int32)[:, None]
+        logit_grads = (
+            weight[:, None]
+            * (
+                jnp.exp(rows_at(all_logits, q, count).astype(jnp.float32) - top[:, None])
+                / total[:, None]
+                - is_target.astype(jnp.float32)
+            )
+        ).astype(jnp.bfloat16)
+        partial = jnp.dot(logit_grads, head_weight, preferred_element_type=jnp.float32)
+        return (partial * 4096.0).astype(jnp.float16)
+
+    far = upstream_block((lax.axis_index("exp") // NZ + 2) % NY)
+    far, send_input = lax.optimization_barrier((far, send_input))
+    flat_inputs = exchange(send_input, "exp")
+    over_y = ring_sum_over_y(upstream_block, far)
+    part_both = jnp.dot(flat_inputs, both_w, preferred_element_type=jnp.float32)
+    over_y, part_both = lax.optimization_barrier((over_y, part_both.astype(jnp.float16)))
+    upstream = exchange_sum(over_y, "exp", Z_GROUPS, NZ) * (1.0 / 4096.0)
     upstream_sent = upstream.astype(jnp.bfloat16)
 
-    send_upstream = jnp.dot(slot_owner, upstream_sent, preferred_element_type=jnp.float32).astype(
-        jnp.bfloat16
-    )
-    flat_upstream = exchange(send_upstream, "exp")
+    send_upstream = jnp.dot(slot_owner, upstream_sent, preferred_element_type=jnp.float32)
+    flat_upstream = exchange(send_upstream.astype(jnp.bfloat16), "exp")
+    both_sum = ctx_scatter(part_both)
     flat_upstream, both_sum = lax.optimization_barrier((flat_upstream, both_sum))
-    gate_sum = both_sum[:, : gate_w.shape[1]]
-    up_sum = both_sum[:, gate_w.shape[1] :]
     part_back = lax.dot_general(
         flat_upstream, down_w, CONTRACT_LAST, preferred_element_type=jnp.float32
     )
-    back_sum = sum_over_ctx(part_back)
-    gate_grad, up_grad, prob_grad = unit_backward(gate_sum, up_sum, back_sum, flat_prob)
-    input_grad = lax.dot_general(
-        gate_grad, gate_w, CONTRACT_LAST, preferred_element_type=jnp.float32
-    ) + lax.dot_general(up_grad, up_w, CONTRACT_LAST, preferred_element_type=jnp.float32)
+    back_sum = ctx_scatter(part_back)
+
+    hidden = w_gate.shape[2]
+    own_count = slot_count // ctx_count
+    ctx_index = lax.axis_index("ctx")
+    own_prob = rows_at(flat_prob, ctx_index % 2 * 4 + ctx_index // 2, own_count)
+    gate_grad, up_grad, prob_grad = unit_backward(
+        both_sum[:, :hidden], both_sum[:, hidden:], back_sum, own_prob
+    )
     prob_high, prob_low = split_high(prob_grad)
     lane = jnp.arange(128, dtype=jnp.int32)[None, :]
     prob_block = jnp.where(
         lane == 0, prob_high[:, None], jnp.where(lane == 1, prob_low[:, None], 0)
     ).astype(jnp.bfloat16)
+    grads = ctx_gather(jnp.concatenate([gate_grad, up_grad, prob_block], axis=1))
+    input_grad = lax.dot_general(
+        grads[:, : 2 * hidden], both_w, CONTRACT_LAST, preferred_element_type=jnp.float32
+    )
     back = exchange(
-        jnp.concatenate([input_grad.astype(jnp.bfloat16), prob_block], axis=1), "exp"
-    )
-    back_input = back[:, :feature_width]
+        jnp.concatenate([input_grad.astype(jnp.bfloat16), grads[:, 2 * hidden :]], axis=1), "exp"
+    )
+    d_x = upstream + lax.dot_general(
+        slot_owner,
+        back[:, :feature_width],
+        (((0,), (0,)), ((), ())),
+        preferred_element_type=jnp.float32,
+    )
     back_prob = back[:, feature_width].astype(jnp.float32) + back[:, feature_width + 1].astype(
         jnp.float32
-    )
-    d_x = upstream + lax.dot_general(
-        slot_owner, back_input, (((0,), (0,)), ((), ())), preferred_element_type=jnp.float32
     )
     d_prob = jnp.dot(back_prob, chosen, precision=lax.Precision.HIGHEST).reshape(
         token_count, route_count

time: 256 us -> 249 us (0.973)
  waiting for transfers between devices: 84.8 us -> 78.9 us
  matrix products: 26.6 us -> 32.2 us
  starting transfers between devices: 61.3 us -> 56.9 us
  other arithmetic: 20.5 us -> 16.2 us
  local copies, waits for them, and re-layouts: 12.8 us -> 15.4 us
    all_to_all x5, waiting for transfers between devices: 43.7 us -> 36.7 us  [exchange(): return lax.all_to_all(x, axis, 0, 0, tiled=True, axis_index_groups=groups)]
    dot_general x6 -> x7, matrix products: 18.4 us -> 24.6 us  [the longest x4 15.6 us: upstream_block(): jnp.dot(logit_grads, head_weight, preferred_element_type=jnp.float32)]
    reduce_sum x1 -> x0, other arithmetic: 3.17 us -> none  [unit_backward(): prob_part = jnp.sum(gate_silu * up_sum * back_sum, axis=1)]
    ppermute x12 -> x9, starting transfers between devices: 16 us -> 12.9 us  [ctx_shift(): return lax.ppermute(x, 'ctx', [(i, (i + 2 * shift) % 8) for i in range(8)])]
    dynamic_slice x3 -> x5, local copies, waits for them, and re-layouts: 1.15 us -> 3.97 us  [rows_at(): return lax.dynamic_slice_in_dim(x, index * count, count, axis=0)]
    concatenate x4 -> x3, other arithmetic: 3.72 us -> 1.09 us  [the longest x1 0.9 us: ring_sum_over_y(): return jnp.concatenate([left, right], axis=1).astype(up.dtype)]
    ppermute x12 -> x9, waiting for transfers between devices: 23.9 us -> 24.1 us  [ctx_shift(): return lax.ppermute(x, 'ctx', [(i, (i + 2 * shift) % 8) for i in range(8)])]
  transfers between devices with their start and end apart: 28 -> 24, of which waited for: 21 -> 17; matrix products, arithmetic and copies ran while one was open for 15% -> 12% of each run, Pallas kernels for 0% -> 0%
where the time goes in v3:
time: 249 us; the launch traced here: 248 us
  waiting for transfers between devices  78.9 us (32%)
  starting transfers between devices  56.9 us (23%)
  blocking collectives  33.6 us (13%)
  matrix products  32.2 us (13%)
  other arithmetic  16.2 us (7%)
  local copies, waits for them, and re-layouts  15.4 us (6%)
  between operations  14.6 us (6%)
    all_to_all x5, waiting for transfers between devices, exchange(): return lax.all_to_all(x, axis, 0, 0, tiled=True, axis_index_groups=groups)  36.7 us
    all_to_all x5, starting transfers between devices, exchange(): return lax.all_to_all(x, axis, 0, 0, tiled=True, axis_index_groups=groups)  36 us
    all_to_all x1, blocking collectives, exchange(): return lax.all_to_all(x, axis, 0, 0, tiled=True, axis_index_groups=groups)  33.6 us
    ppermute x9, waiting for transfers between devices, ctx_shift(): return lax.ppermute(x, 'ctx', [(i, (i + 2 * shift) % 8) for i in range(8)])  24.1 us
    dot_general x4, matrix products, upstream_block(): jnp.dot(logit_grads, head_weight, preferred_element_type=jnp.float32)  15.6 us
    ppermute x9, starting transfers between devices, ctx_shift(): return lax.ppermute(x, 'ctx', [(i, (i + 2 * shift) % 8) for i in range(8)])  12.9 us
    ppermute x6, starting transfers between devices, y_shift(): lax.ppermute(x, 'exp', [(i, (i + NZ * shift) % (NY * NZ)) for i in range(...  7.67 us
    ppermute x6, waiting for transfers between devices, y_shift(): lax.ppermute(x, 'exp', [(i, (i + NZ * shift) % (NY * NZ)) for i in range(...  6.92 us
  transfers between devices with their start and end apart: 24, of which 17 were waited for; matrix products, arithmetic and copies ran while one was open for 12% of the time, Pallas kernels for 0%

profile of v3, /device:TPU:32, one launch (start us, length us, event | category | flops | bytes accessed | tf_op | source)
XLA Modules:
  0.0 247.9 jit_solution(2030052327316932007)
XLA Ops:
  8.9 1.3 reduce_max.23
  11.9 1.5 exponential_reduce_fusion
  14.6 11.4 %all-to-all-start = ((f32[32,1,384]{2,1,0:T(1,128)}), f32[32,1,384]{2,1,0:T(1,128)S(1)}, u32[]{:S(2)}, u32[]{:S(2)}) async-start(f32[32,1,384]{2,1,0:T(1,128)} %all_to_all.42), calls=%async_computation | async-start | bytes 98304 | tf_op jit(solution)/shard_map/all_to_all | solution.py:13
  26.4 1.4 convolution_convert_fusion.2
  27.8 7.1 %all-to-all-done = f32[32,1,384]{2,1,0:T(1,128)S(1)} async-done(((f32[32,1,384]{2,1,0:T(1,128)}), f32[32,1,384]{2,1,0:T(1,128)S(1)}, u32[]{:S(2)}, u32[]{:S(2)}) %all-to-all-start) | async-done | bytes 49184 | tf_op jit(solution)/shard_map/all_to_all | solution.py:13
  36.2 4.3 %all-to-all-start.1 = ((f32[8,1,512]{2,1,0:T(1,128)}), f32[8,1,512]{2,1,0:T(1,128)S(1)}, u32[]{:S(2)}, u32[]{:S(2)}) async-start(f32[8,1,512]{2,1,0:T(1,128)} %broadcast_in_dim.66), calls=%async_computation.1 | async-start | bytes 32768 | tf_op jit(solution)/shard_map/all_to_all | solution.py:13
  40.7 5.3 %all-to-all-done.1 = f32[8,1,512]{2,1,0:T(1,128)S(1)} async-done(((f32[8,1,512]{2,1,0:T(1,128)}), f32[8,1,512]{2,1,0:T(1,128)S(1)}, u32[]{:S(2)}, u32[]{:S(2)}) %all-to-all-start.1) | async-done | bytes 16416 | tf_op jit(solution)/shard_map/all_to_all | solution.py:13
  46.0 5.7 %all-gather.2.cloned.1.call-done = bf16[1024,2560]{1,0:T(8,128)(2,1)} async-done(((bf16[128,2560]{1,0:T(8,128)(2,1)}), bf16[1024,2560]{1,0:T(8,128)(2,1)}) %all-gather.2.cloned.1.call-update) | async-done | bytes 5242896 | tf_op jit(solution)/shard_map/all_gather | solution.py:124
  53.6 4.6 %fusion.36 = f16[256,896]{1,0:T(8,128)(2,1)S(1)} fusion(bf16[2560,896]{1,0:T(8,128)(2,1)} %param.12, s32[256]{0:T(256)S(1)} %bitcast.102, f32[256]{0:T(256)S(1)} %bitcast.99, f32[256]{0:T(256)S(1)} %bitcast.100, bf16[1024,2560]{1,0:T(8,128)(2,1)} %all-gather.2.cloned.1.call-done, s32[]{:T(128)S(6)} %select_n.149, f32[256]{0:T(256)S(1)} %bitcast.101), kind=kOutput, calls=%fused_computation.52 | convolution fusion | flops 1180106752 | bytes 6361092 | tf_op jit(solution)/shard_map/dot_general | solution.py:198
  59.7 4.6 %fusion.37 = f16[256,896]{1,0:T(8,128)(2,1)S(1)} fusion(bf16[2560,896]{1,0:T(8,128)(2,1)} %param.12, s32[256]{0:T(256)S(1)} %bitcast.98, f32[256]{0:T(256)S(1)} %bitcast.95, f32[256]{0:T(256)S(1)} %bitcast.96, bf16[1024,2560]{1,0:T(8,128)(2,1)S(1)} %copy-done.8, s32[]{:T(128)S(6)} %select_n.151, f32[256]{0:T(256)S(1)} %bitcast.97), kind=kOutput, calls=%fused_computation.53 | convolution fusion | flops 1180106752 | bytes 6361092 | tf_op jit(solution)/shard_map/dot_general | solution.py:198
  65.1 2.7 %collective-permute-start.2 = (f16[256,512]{1,0:T(8,128)(2,1)}, f16[256,512]{1,0:T(8,128)(2,1)S(1)}, u32[]{:S(2)}, u32[]{:S(2)}) collective-permute-start(f16[256,512]{1,0:T(8,128)(2,1)} %slice.117), channel_id=1, source_target_pairs={{0,24},{1,25},{2,26},{3,27},{4,28},{5,29},{6,30},{7,31},{8,0},{9,1... | collective-permute-start | bytes 786440 | tf_op jit(solution)/shard_map/ppermute | solution.py:71
  68.7 1.2 collective-permute-start
  69.9 1.9 fusion.35
  72.5 10.6 %all-to-all-start.2 = ((bf16[32,16,896]{2,1,0:T(8,128)(2,1)}), bf16[32,16,896]{2,1,0:T(8,128)(2,1)S(1)}, u32[]{:S(2)}, u32[]{:S(2)}) async-start(bf16[32,16,896]{2,1,0:T(8,128)(2,1)} %bitcast.24), calls=%async_computation.2 | async-start | bytes 1835008 | tf_op jit(solution)/shard_map/all_to_all | solution.py:13
  84.2 2.8 %collective-permute-start.5 = (f16[256,384]{1,0:T(8,128)(2,1)S(1)}, f16[256,384]{1,0:T(8,128)(2,1)S(1)}, u32[]{:S(2)}, u32[]{:S(2)}) collective-permute-start(f16[256,384]{1,0:T(8,128)(2,1)S(1)} %add_convert_fusion.3), channel_id=1, source_target_pairs={{0,24},{1,25},{2,26},{3,27},{4,28},{5,29},{6,30},{7,31},{8,0},{9,1... | collective-permute-start | bytes 589832 | tf_op jit(solution)/shard_map/ppermute | solution.py:71
  88.1 4.5 %fusion.34 = f32[256,896]{1,0:T(8,128)S(1)} fusion(bf16[2560,896]{1,0:T(8,128)(2,1)} %param.12, s32[256]{0:T(256)S(1)} %bitcast.90, f32[256]{0:T(256)S(1)} %bitcast.87, f32[256]{0:T(256)S(1)} %bitcast.88, bf16[1024,2560]{1,0:T(8,128)(2,1)} %all-gather.2.cloned.1.call-done, s32[]{:T(128)S(6)} %select_n.145, f32[256]{0:T(256)S(1)} %bitcast.89), kind=kOutput, calls=%fused_computation.50 | convolution fusion | flops 1180336128 | bytes 6819844 | tf_op jit(solution)/shard_map/dot_general | solution.py:198
  92.6 1.3 collective-permute-done.5
  95.0 5.6 %collective-permute-done.1 = f16[256,512]{1,0:T(8,128)(2,1)S(1)} collective-permute-done((f16[256,512]{1,0:T(8,128)(2,1)S(1)}, f16[256,512]{1,0:T(8,128)(2,1)S(1)}, u32[]{:S(2)}, u32[]{:S(2)}) %collective-permute-start.1) | collective-permute-done | bytes 262176 | tf_op jit(solution)/shard_map/ppermute | solution.py:71
  101.6 6.6 %all-to-all-done.2 = bf16[32,16,896]{2,1,0:T(8,128)(2,1)S(1)} async-done(((bf16[32,16,896]{2,1,0:T(8,128)(2,1)}), bf16[32,16,896]{2,1,0:T(8,128)(2,1)S(1)}, u32[]{:S(2)}, u32[]{:S(2)}) %all-to-all-start.2) | async-done | bytes 917536 | tf_op jit(solution)/shard_map/all_to_all | solution.py:13
  108.2 5.7 %convolution_convert_fusion = f16[512,2048]{1,0:T(8,128)(2,1)} fusion(bf16[512,896]{1,0:T(8,128)(2,1)S(1)} %bitcast.77, bf16[896,1024]{1,0:T(8,128)(2,1)} %bitcast.105, bf16[896,1024]{1,0:T(8,128)(2,1)} %bitcast.107), kind=kOutput, calls=%fused_computation.1 | convolution fusion | flops 1887436800 | bytes 6684672 | tf_op jit(solution)/shard_map/dot_general | solution.py:205
  114.0 3.9 %all-to-all-start.3 = ((f16[8,32,896]{2,1,0:T(8,128)(2,1)}), f16[8,32,896]{2,1,0:T(8,128)(2,1)S(1)}, u32[]{:S(2)}, u32[]{:S(2)}) async-start(f16[8,32,896]{2,1,0:T(8,128)(2,1)} %bitcast.28), calls=%async_computation.3 | async-start | bytes 917504 | tf_op jit(solution)/shard_map/all_to_all | solution.py:13
  117.9 1.4 constant_dynamic-slice_fusion.7
  119.5 11.0 %all-to-all-done.3 = f16[8,32,896]{2,1,0:T(8,128)(2,1)S(1)} async-done(((f16[8,32,896]{2,1,0:T(8,128)(2,1)}), f16[8,32,896]{2,1,0:T(8,128)(2,1)S(1)}, u32[]{:S(2)}, u32[]{:S(2)}) %all-to-all-start.3) | async-done | bytes 458784 | tf_op jit(solution)/shard_map/all_to_all | solution.py:13
  130.6 1.4 convolution_convert_fusion.1
  131.9 5.8 %all-to-all-start.4 = ((bf16[32,16,896]{2,1,0:T(8,128)(2,1)}), bf16[32,16,896]{2,1,0:T(8,128)(2,1)}, u32[]{:S(2)}, u32[]{:S(2)}) async-start(bf16[32,16,896]{2,1,0:T(8,128)(2,1)} %bitcast.29), calls=%async_computation.4 | async-start | bytes 1835008 | tf_op jit(solution)/shard_map/all_to_all | solution.py:13
  137.8 2.0 add_convert_fusion
  141.3 1.8 collective-permute-start.9
  143.1 2.1 collective-permute-start.8
  145.1 9.3 %collective-permute-done.7 = f16[64,2048]{1,0:T(8,128)(2,1)} collective-permute-done((f16[64,2048]{1,0:T(8,128)(2,1)}, f16[64,2048]{1,0:T(8,128)(2,1)}, u32[]{:S(2)}, u32[]{:S(2)}) %collective-permute-start.7) | collective-permute-done | bytes 262176 | tf_op jit(solution)/shard_map/ppermute | solution.py:28
  154.8 1.2 convert_add_fusion
  156.1 6.6 %all-to-all-done.4 = bf16[32,16,896]{2,1,0:T(8,128)(2,1)} async-done(((bf16[32,16,896]{2,1,0:T(8,128)(2,1)}), bf16[32,16,896]{2,1,0:T(8,128)(2,1)}, u32[]{:S(2)}, u32[]{:S(2)}) %all-to-all-start.4) | async-done | bytes 917536 | tf_op jit(solution)/shard_map/all_to_all | solution.py:13
  162.7 2.5 fusion.7
  165.4 1.9 collective-permute-done.10
  168.8 1.8 collective-permute-start.13
  170.6 2.1 collective-permute-start.12
  173.2 1.3 slice.121
  174.5 1.4 reshape.257
  176.7 1.4 collective-permute-done.11
  179.9 1.2 collective-permute-start.14
  181.1 2.1 collective-permute-start.15
  184.1 5.4 %collective-permute-done.14 = bf16[64,2176]{1,0:T(8,128)(2,1)S(1)} collective-permute-done((bf16[64,2176]{1,0:T(8,128)(2,1)S(1)}, bf16[64,2176]{1,0:T(8,128)(2,1)S(1)}, u32[]{:S(2)}, u32[]{:S(2)}) %collective-permute-start.14) | collective-permute-done | bytes 278560 | tf_op jit(solution)/shard_map/ppermute | solution.py:28
  189.5 5.3 %collective-permute-done.15 = bf16[64,2176]{1,0:T(8,128)(2,1)S(1)} collective-permute-done((bf16[64,2176]{1,0:T(8,128)(2,1)S(1)}, bf16[64,2176]{1,0:T(8,128)(2,1)S(1)}, u32[]{:S(2)}, u32[]{:S(2)}) %collective-permute-start.15) | collective-permute-done | bytes 278560 | tf_op jit(solution)/shard_map/ppermute | solution.py:28
  194.9 1.8 collective-permute-done.16
  196.8 2.8 %collective-permute-done.17 = bf16[256,2176]{1,0:T(8,128)(2,1)} collective-permute-done((bf16[256,2176]{1,0:T(8,128)(2,1)S(1)}, bf16[256,2176]{1,0:T(8,128)(2,1)}, u32[]{:S(2)}, u32[]{:S(2)}) %collective-permute-start.17) | collective-permute-done | bytes 1114144 | tf_op jit(solution)/shard_map/ppermute | solution.py:32
  199.6 1.4 broadcast_select_fusion.1
  201.1 2.4 fusion.10
  203.6 33.6 %all_to_all.63 = bf16[32,16,1024]{2,1,0:T(8,128)(2,1)S(1)} all-to-all(bf16[32,16,1024]{2,1,0:T(8,128)(2,1)S(1)} %bitcast.76), channel_id=1, replica_groups=mesh['ctx'=8,'exp'=32] {'exp'}, dimensions={0} | all-to-all | bytes 2097152 | tf_op jit(solution)/shard_map/all_to_all | solution.py:13
  238.4 1.9 fusion.46
  (120 shorter events, 26.3 us)
Async XLA Ops:
  7.2 155.5 %copy-start = (bf16[1,1024,896]{2,1,0:T(8,128)(2,1)S(1)}, bf16[1,1024,896]{2,1,0:T(8,128)(2,1)}, u32[]{:S(2)}) copy-start(bf16[1,1024,896]{2,1,0:T(8,128)(2,1)} %param.21) | copy-start | bytes 5505028
  7.2 19.2 %copy-start.6 = (s32[16]{0:T(128)S(1)}, s32[16]{0:T(128)}, u32[]{:S(2)}) copy-start(s32[16]{0:T(128)} %param.14) | copy-start | bytes 196
  7.2 19.2 %copy-start.3 = (bf16[32,896]{1,0:T(8,128)(2,1)S(1)}, bf16[32,896]{1,0:T(8,128)(2,1)}, u32[]{:S(2)}) copy-start(bf16[32,896]{1,0:T(8,128)(2,1)} %param.16) | copy-start | bytes 172036
  7.2 20.6 %copy-start.11 = (s32[128]{0:T(128)S(1)}, s32[128]{0:T(128)}, u32[]{:S(2)}) copy-start(s32[128]{0:T(128)} %param.13) | copy-start | bytes 1540
  7.2 28.4 %copy-start.7 = (f32[128]{0:T(128)S(1)}, f32[128]{0:T(128)}, u32[]{:S(2)}) copy-start(f32[128]{0:T(128)} %param.15) | copy-start | bytes 1540
  7.2 44.5 %all-gather.2.cloned.1.call-start = ((), (), s32[]{:S(2)}) async-start(), calls=%async_computation.6 | async-start | bytes 5898240 | tf_op jit(solution)/shard_map/all_gather | solution.py:124
  13.5 12.6 %copy-start.4 = (s32[256]{0:T(256)}, s32[256]{0:T(256)S(1)}, u32[]{:S(2)}) copy-start(s32[256]{0:T(256)S(1)} %multiply_add_fusion.2) | copy-start | bytes 3076
  14.6 20.3 %all-to-all-start = ((f32[32,1,384]{2,1,0:T(1,128)}), f32[32,1,384]{2,1,0:T(1,128)S(1)}, u32[]{:S(2)}, u32[]{:S(2)}) async-start(f32[32,1,384]{2,1,0:T(1,128)} %all_to_all.42), calls=%async_computation | async-start | bytes 98304 | tf_op jit(solution)/shard_map/all_to_all | solution.py:13
  35.0 0.6 copy-start.2
  36.2 9.8 %all-to-all-start.1 = ((f32[8,1,512]{2,1,0:T(1,128)}), f32[8,1,512]{2,1,0:T(1,128)S(1)}, u32[]{:S(2)}, u32[]{:S(2)}) async-start(f32[8,1,512]{2,1,0:T(1,128)} %broadcast_in_dim.66), calls=%async_computation.1 | async-start | bytes 32768 | tf_op jit(solution)/shard_map/all_to_all | solution.py:13
  53.6 6.1 %copy-start.8 = (bf16[1024,2560]{1,0:T(8,128)(2,1)S(1)}, bf16[1024,2560]{1,0:T(8,128)(2,1)}, u32[]{:S(2)}) copy-start(bf16[1024,2560]{1,0:T(8,128)(2,1)} %all-gather.2.cloned.1.call-done) | copy-start | bytes 15728644
  58.9 11.0 %slice-start = ((s8[4587520]{0:T(1024)(128)(4,1)}), s8[4194304]{0:T(1024)(128)(4,1)S(1)}, s32[]{:S(2)}) async-start(s8[4587520]{0:T(1024)(128)(4,1)} %bitcast.103), calls=%async_computation.7 | async-start | bytes 8388608
  59.7 10.2 %slice-start.1 = ((s8[4587520]{0:T(1024)(128)(4,1)}), s8[393216]{0:T(1024)(128)(4,1)S(1)}, s32[]{:S(2)}) async-start(s8[4587520]{0:T(1024)(128)(4,1)} %bitcast.103), calls=%async_computation.8 | async-start | bytes 786432
  64.3 7.5 %copy-start.1 = (f16[256,896]{1,0:T(8,128)(2,1)}, f16[256,896]{1,0:T(8,128)(2,1)S(1)}, u32[]{:S(2)}) copy-start(f16[256,896]{1,0:T(8,128)(2,1)S(1)} %fusion.37) | copy-start | bytes 1376260
  65.1 29.8 %collective-permute-start.2 = (f16[256,512]{1,0:T(8,128)(2,1)}, f16[256,512]{1,0:T(8,128)(2,1)S(1)}, u32[]{:S(2)}, u32[]{:S(2)}) collective-permute-start(f16[256,512]{1,0:T(8,128)(2,1)} %slice.117), channel_id=1, source_target_pairs={{0,24},{1,25},{2,26},{3,27},{4,28},{5,29},{6,30},{7,31},{8,0},{9,1... | collective-permute-start | bytes 786440 | tf_op jit(solution)/shard_map/ppermute | solution.py:71
  67.9 15.2 %collective-permute-start.4 = (f16[256,384]{1,0:T(8,128)(2,1)}, f16[256,384]{1,0:T(8,128)(2,1)}, u32[]{:S(2)}, u32[]{:S(2)}) collective-permute-start(f16[256,384]{1,0:T(8,128)(2,1)} %slice.101), channel_id=1, source_target_pairs={{0,24},{1,25},{2,26},{3,27},{4,28},{5,29},{6,30},{7,31},{8,0},{9,1... | collective-permute-start | bytes 589832 | tf_op jit(solution)/shard_map/ppermute | solution.py:71
  68.7 18.3 %collective-permute-start = (f16[256,512]{1,0:T(8,128)(2,1)}, f16[256,512]{1,0:T(8,128)(2,1)}, u32[]{:S(2)}, u32[]{:S(2)}) collective-permute-start(f16[256,512]{1,0:T(8,128)(2,1)} %slice.96), channel_id=1, source_target_pairs={{0,8},{1,9},{2,10},{3,11},{4,12},{5,13},{6,14},{7,15},{8,16},{9,17... | collective-permute-start | bytes 786440 | tf_op jit(solution)/shard_map/ppermute | solution.py:71
  72.5 20.1 %collective-permute-start.3 = (f16[256,384]{1,0:T(8,128)(2,1)}, f16[256,384]{1,0:T(8,128)(2,1)}, u32[]{:S(2)}, u32[]{:S(2)}) collective-permute-start(f16[256,384]{1,0:T(8,128)(2,1)} %slice.119), channel_id=1, source_target_pairs={{0,8},{1,9},{2,10},{3,11},{4,12},{5,13},{6,14},{7,15},{8,16},{9,17... | collective-permute-start | bytes 589832 | tf_op jit(solution)/shard_map/ppermute | solution.py:71
  72.5 35.7 %all-to-all-start.2 = ((bf16[32,16,896]{2,1,0:T(8,128)(2,1)}), bf16[32,16,896]{2,1,0:T(8,128)(2,1)S(1)}, u32[]{:S(2)}, u32[]{:S(2)}) async-start(bf16[32,16,896]{2,1,0:T(8,128)(2,1)} %bitcast.24), calls=%async_computation.2 | async-start | bytes 1835008 | tf_op jit(solution)/shard_map/all_to_all | solution.py:13
  84.2 9.7 %collective-permute-start.5 = (f16[256,384]{1,0:T(8,128)(2,1)S(1)}, f16[256,384]{1,0:T(8,128)(2,1)S(1)}, u32[]{:S(2)}, u32[]{:S(2)}) collective-permute-start(f16[256,384]{1,0:T(8,128)(2,1)S(1)} %add_convert_fusion.3), channel_id=1, source_target_pairs={{0,24},{1,25},{2,26},{3,27},{4,28},{5,29},{6,30},{7,31},{8,0},{9,1... | collective-permute-start | bytes 589832 | tf_op jit(solution)/shard_map/ppermute | solution.py:71
  88.0 12.5 %collective-permute-start.1 = (f16[256,512]{1,0:T(8,128)(2,1)S(1)}, f16[256,512]{1,0:T(8,128)(2,1)S(1)}, u32[]{:S(2)}, u32[]{:S(2)}) collective-permute-start(f16[256,512]{1,0:T(8,128)(2,1)S(1)} %add_convert_fusion.2), channel_id=1, source_target_pairs={{0,8},{1,9},{2,10},{3,11},{4,12},{5,13},{6,14},{7,15},{8,16},{9,17... | collective-permute-start | bytes 786440 | tf_op jit(solution)/shard_map/ppermute | solution.py:71
  114.0 16.5 %all-to-all-start.3 = ((f16[8,32,896]{2,1,0:T(8,128)(2,1)}), f16[8,32,896]{2,1,0:T(8,128)(2,1)S(1)}, u32[]{:S(2)}, u32[]{:S(2)}) async-start(f16[8,32,896]{2,1,0:T(8,128)(2,1)} %bitcast.28), calls=%async_computation.3 | async-start | bytes 917504 | tf_op jit(solution)/shard_map/all_to_all | solution.py:13
  119.4 18.5 %collective-permute-start.6 = (f16[256,2048]{1,0:T(8,128)(2,1)S(1)}, f16[256,2048]{1,0:T(8,128)(2,1)}, u32[]{:S(2)}, u32[]{:S(2)}) collective-permute-start(f16[256,2048]{1,0:T(8,128)(2,1)S(1)} %constant_dynamic-slice_fusion.7), channel_id=1, source_target_pairs={{0,32},{32,0},{64,96},{96,64},{128,160},{160,128},{192,224},{224,1... | collective-permute-start | bytes 3145736 | tf_op jit(solution)/shard_map/ppermute | solution.py:32
  131.9 30.8 %all-to-all-start.4 = ((bf16[32,16,896]{2,1,0:T(8,128)(2,1)}), bf16[32,16,896]{2,1,0:T(8,128)(2,1)}, u32[]{:S(2)}, u32[]{:S(2)}) async-start(bf16[32,16,896]{2,1,0:T(8,128)(2,1)} %bitcast.29), calls=%async_computation.4 | async-start | bytes 1835008 | tf_op jit(solution)/shard_map/all_to_all | solution.py:13
  140.8 13.7 %collective-permute-start.7 = (f16[64,2048]{1,0:T(8,128)(2,1)}, f16[64,2048]{1,0:T(8,128)(2,1)}, u32[]{:S(2)}, u32[]{:S(2)}) collective-permute-start(f16[64,2048]{1,0:T(8,128)(2,1)} %get-tuple-element.22), channel_id=1, source_target_pairs={{0,64},{32,96},{64,128},{96,160},{128,192},{160,224},{192,0},{224,... | collective-permute-start | bytes 786440 | tf_op jit(solution)/shard_map/ppermute | solution.py:28
  141.3 13.2 %collective-permute-start.9 = (f16[64,2048]{1,0:T(8,128)(2,1)S(1)}, f16[64,2048]{1,0:T(8,128)(2,1)}, u32[]{:S(2)}, u32[]{:S(2)}) collective-permute-start(f16[64,2048]{1,0:T(8,128)(2,1)S(1)} %get-tuple-element.23), channel_id=1, source_target_pairs={{0,128},{32,160},{64,192},{96,224},{128,0},{160,32},{192,64},{224,... | collective-permute-start | bytes 786440 | tf_op jit(solution)/shard_map/ppermute | solution.py:28
  143.1 11.8 %collective-permute-start.8 = (f16[64,2048]{1,0:T(8,128)(2,1)S(1)}, f16[64,2048]{1,0:T(8,128)(2,1)}, u32[]{:S(2)}, u32[]{:S(2)}) collective-permute-start(f16[64,2048]{1,0:T(8,128)(2,1)S(1)} %get-tuple-element.24), channel_id=1, source_target_pairs={{0,192},{32,224},{64,0},{96,32},{128,64},{160,96},{192,128},{224,1... | collective-permute-start | bytes 786440 | tf_op jit(solution)/shard_map/ppermute | solution.py:28
  165.3 2.0 collective-permute-start.10
  168.3 9.8 %collective-permute-start.11 = (f16[64,1024]{1,0:T(8,128)(2,1)}, f16[64,1024]{1,0:T(8,128)(2,1)S(1)}, u32[]{:S(2)}, u32[]{:S(2)}) collective-permute-start(f16[64,1024]{1,0:T(8,128)(2,1)} %get-tuple-element.27), channel_id=1, source_target_pairs={{0,64},{32,96},{64,128},{96,160},{128,192},{160,224},{192,0},{224,... | collective-permute-start | bytes 393224 | tf_op jit(solution)/shard_map/ppermute | solution.py:28
  168.8 9.3 %collective-permute-start.13 = (f16[64,1024]{1,0:T(8,128)(2,1)}, f16[64,1024]{1,0:T(8,128)(2,1)S(1)}, u32[]{:S(2)}, u32[]{:S(2)}) collective-permute-start(f16[64,1024]{1,0:T(8,128)(2,1)} %get-tuple-element.28), channel_id=1, source_target_pairs={{0,128},{32,160},{64,192},{96,224},{128,0},{160,32},{192,64},{224,... | collective-permute-start | bytes 393224 | tf_op jit(solution)/shard_map/ppermute | solution.py:28
  170.6 8.1 %collective-permute-start.12 = (f16[64,1024]{1,0:T(8,128)(2,1)S(1)}, f16[64,1024]{1,0:T(8,128)(2,1)S(1)}, u32[]{:S(2)}, u32[]{:S(2)}) collective-permute-start(f16[64,1024]{1,0:T(8,128)(2,1)S(1)} %get-tuple-element.29), channel_id=1, source_target_pairs={{0,192},{32,224},{64,0},{96,32},{128,64},{160,96},{192,128},{224,1... | collective-permute-start | bytes 393224 | tf_op jit(solution)/shard_map/ppermute | solution.py:28
  179.9 9.6 %collective-permute-start.14 = (bf16[64,2176]{1,0:T(8,128)(2,1)S(1)}, bf16[64,2176]{1,0:T(8,128)(2,1)S(1)}, u32[]{:S(2)}, u32[]{:S(2)}) collective-permute-start(bf16[64,2176]{1,0:T(8,128)(2,1)S(1)} %get-tuple-element.30), channel_id=1, source_target_pairs={{0,64},{32,96},{64,128},{96,160},{128,192},{160,224},{192,0},{224,... | collective-permute-start | bytes 835592 | tf_op jit(solution)/shard_map/ppermute | solution.py:28
  181.1 13.7 %collective-permute-start.15 = (bf16[64,2176]{1,0:T(8,128)(2,1)S(1)}, bf16[64,2176]{1,0:T(8,128)(2,1)S(1)}, u32[]{:S(2)}, u32[]{:S(2)}) collective-permute-start(bf16[64,2176]{1,0:T(8,128)(2,1)S(1)} %get-tuple-element.30), channel_id=1, source_target_pairs={{0,192},{32,224},{64,0},{96,32},{128,64},{160,96},{192,128},{224,1... | collective-permute-start | bytes 835592 | tf_op jit(solution)/shard_map/ppermute | solution.py:28
  183.2 13.4 %collective-permute-start.16 = (bf16[64,2176]{1,0:T(8,128)(2,1)S(1)}, bf16[64,2176]{1,0:T(8,128)(2,1)S(1)}, u32[]{:S(2)}, u32[]{:S(2)}) collective-permute-start(bf16[64,2176]{1,0:T(8,128)(2,1)S(1)} %get-tuple-element.30), channel_id=1, source_target_pairs={{0,128},{32,160},{64,192},{96,224},{128,0},{160,32},{192,64},{224,... | collective-permute-start | bytes 835592 | tf_op jit(solution)/shard_map/ppermute | solution.py:28
  196.7 3.0 %collective-permute-start.17 = (bf16[256,2176]{1,0:T(8,128)(2,1)S(1)}, bf16[256,2176]{1,0:T(8,128)(2,1)}, u32[]{:S(2)}, u32[]{:S(2)}) collective-permute-start(bf16[256,2176]{1,0:T(8,128)(2,1)S(1)} %constant_dynamic-update-slice_fusion), channel_id=1, source_target_pairs={{0,32},{32,0},{64,96},{96,64},{128,160},{160,128},{192,224},{224,1... | collective-permute-start | bytes 3342344 | tf_op jit(solution)/shard_map/ppermute | solution.py:32
  196.8 4.3 %copy-start.9 = (bf16[1,896,1024]{2,1,0:T(8,128)(2,1)S(1)}, bf16[1,896,1024]{2,1,0:T(8,128)(2,1)}, u32[]{:S(2)}) copy-start(bf16[1,896,1024]{2,1,0:T(8,128)(2,1)} %param.20) | copy-start | bytes 5505028
  196.8 4.3 %copy-start.10 = (bf16[1,896,1024]{2,1,0:T(8,128)(2,1)S(1)}, bf16[1,896,1024]{2,1,0:T(8,128)(2,1)}, u32[]{:S(2)}) copy-start(bf16[1,896,1024]{2,1,0:T(8,128)(2,1)} %param.19) | copy-start | bytes 5505028
  203.6 34.8 %copy-start.5 = (s32[256]{0:T(256)S(1)}, s32[256]{0:T(256)}, u32[]{:S(2)}) copy-start(s32[256]{0:T(256)} %copy-done.4) | copy-start | bytes 3076
Sparse Core Ops, SparseCore 0:
  9.9 41.8 all-gather.1

commit v4 on v3

--- a/solution.py
+++ b/solution.py
@@ -73,23 +73,24 @@
     )
 
 
-def ring_sum_over_y(block, far):
+def ring_sum_over_y(block, far, per_row):
     y = lax.axis_index("exp") // NZ
-    split = 512
-    from_down = y_shift(far[:, :split], 1)
-    from_up = y_shift(far[:, split:], 3)
-    up = block((y + 1) % NY)
-    up_late = y_shift(up[:, split:], 1)
-    down = block((y + 3) % NY)
-    down_late = y_shift(down[:, :split], 3)
-    up_sum = (up[:, :split].astype(jnp.float32) + from_down.astype(jnp.float32)).astype(up.dtype)
+    split = far.shape[0] // 2
+    from_down = y_shift(far[:split], 1)
+    from_up = y_shift(far[split:], 3)
+    from_down, from_up, per_row = lax.optimization_barrier((from_down, from_up, per_row))
+    up = block((y + 1) % NY, per_row)
+    up_late = y_shift(up[split:], 1)
+    down = block((y + 3) % NY, per_row)
+    down_late = y_shift(down[:split], 3)
+    up_sum = (up[:split].astype(jnp.float32) + from_down.astype(jnp.float32)).astype(up.dtype)
     up_sum = y_shift(up_sum, 1)
-    down_sum = (down[:, split:].astype(jnp.float32) + from_up.astype(jnp.float32)).astype(up.dtype)
+    down_sum = (down[split:].astype(jnp.float32) + from_up.astype(jnp.float32)).astype(up.dtype)
     down_sum = y_shift(down_sum, 3)
-    own = block(y).astype(jnp.float32)
-    left = own[:, :split] + up_sum.astype(jnp.float32) + down_late.astype(jnp.float32)
-    right = own[:, split:] + up_late.astype(jnp.float32) + down_sum.astype(jnp.float32)
-    return jnp.concatenate([left, right], axis=1).astype(up.dtype)
+    own = block(y, per_row).astype(jnp.float32)
+    first = own[:split] + up_sum.astype(jnp.float32) + down_late.astype(jnp.float32)
+    second = own[split:] + up_late.astype(jnp.float32) + down_sum.astype(jnp.float32)
+    return jnp.concatenate([first, second], axis=0).astype(up.dtype)
 
 
 def unit_backward(gate_sum, up_sum, back_sum, slot_prob):
@@ -167,7 +168,8 @@
     rows = rows.reshape(ctx_count, 4, row_count).transpose(1, 0, 2).reshape(4, seq_length)
     rows, all_logits = lax.optimization_barrier((rows, all_logits))
 
-    both_w = jnp.concatenate([w_gate[0], w_up[0]], axis=1)
+    gate_w = w_gate[0]
+    up_w = w_up[0]
     down_w = w_down[0]
     row_max, row_total, weights = rows[0], rows[1], rows[2]
     all_ids = rows[3].astype(jnp.int32)
@@ -183,7 +185,7 @@
     columns = jnp.arange(vocab_width, dtype=jnp.int32)[None, :]
     per_row = jnp.stack([row_max, row_total, weighting, local_target.astype(jnp.float32)])
 
-    def upstream_block(q):
+    def upstream_block(q, per_row):
         count = seq_length // NY
         top, total, weight, aim = lax.dynamic_slice_in_dim(per_row, q * count, count, axis=1)
         is_target = columns == aim.astype(jnp.int32)[:, None]
@@ -198,17 +200,26 @@
         partial = jnp.dot(logit_grads, head_weight, preferred_element_type=jnp.float32)
         return (partial * 4096.0).astype(jnp.float16)
 
-    far = upstream_block((lax.axis_index("exp") // NZ + 2) % NY)
+    far = upstream_block((lax.axis_index("exp") // NZ + 2) % NY, per_row)
     far, send_input = lax.optimization_barrier((far, send_input))
     flat_inputs = exchange(send_input, "exp")
-    over_y = ring_sum_over_y(upstream_block, far)
-    part_both = jnp.dot(flat_inputs, both_w, preferred_element_type=jnp.float32)
-    over_y, part_both = lax.optimization_barrier((over_y, part_both.astype(jnp.float16)))
+    over_y = ring_sum_over_y(upstream_block, far, per_row)
+    flat_inputs, over_y = lax.optimization_barrier((flat_inputs, over_y))
+    part_both = jnp.concatenate(
+        [
+            jnp.dot(flat_inputs, weight, preferred_element_type=jnp.float32).astype(jnp.float16)
+            for weight in (gate_w, up_w)
+        ],
+        axis=1,
+    )
     upstream = exchange_sum(over_y, "exp", Z_GROUPS, NZ) * (1.0 / 4096.0)
     upstream_sent = upstream.astype(jnp.bfloat16)
 
-    send_upstream = jnp.dot(slot_owner, upstream_sent, preferred_element_type=jnp.float32)
-    flat_upstream = exchange(send_upstream.astype(jnp.bfloat16), "exp")
+    send_upstream = jnp.dot(slot_owner, upstream_sent, preferred_element_type=jnp.float32).astype(
+        jnp.bfloat16
+    )
+    send_upstream, part_both = lax.optimization_barrier((send_upstream, part_both))
+    flat_upstream = exchange(send_upstream, "exp")
     both_sum = ctx_scatter(part_both)
     flat_upstream, both_sum = lax.optimization_barrier((flat_upstream, both_sum))
     part_back = lax.dot_general(
@@ -230,7 +241,9 @@
     ).astype(jnp.bfloat16)
     grads = ctx_gather(jnp.concatenate([gate_grad, up_grad, prob_block], axis=1))
     input_grad = lax.dot_general(
-        grads[:, : 2 * hidden], both_w, CONTRACT_LAST, preferred_element_type=jnp.float32
+        grads[:, :hidden], gate_w, CONTRACT_LAST, preferred_element_type=jnp.float32
+    ) + lax.dot_general(
+        grads[:, hidden : 2 * hidden], up_w, CONTRACT_LAST, preferred_element_type=jnp.float32
     )
     back = exchange(
         jnp.concatenate([input_grad.astype(jnp.bfloat16), grads[:, 2 * hidden :]], axis=1), "exp"
@@ -241,12 +254,15 @@
         (((0,), (0,)), ((), ())),
         preferred_element_type=jnp.float32,
     )
-    back_prob = back[:, feature_width].astype(jnp.float32) + back[:, feature_width + 1].astype(
-        jnp.float32
-    )
-    d_prob = jnp.dot(back_prob, chosen, precision=lax.Precision.HIGHEST).reshape(
-        token_count, route_count
-    )
+    d_prob = jnp.sum(
+        lax.dot_general(
+            back[:, feature_width : feature_width + 2],
+            chosen.astype(jnp.bfloat16),
+            (((0,), (0,)), ((), ())),
+            preferred_element_type=jnp.float32,
+        ),
+        axis=0,
+    ).reshape(token_count, route_count)
     return (d_x, d_prob)
 
 

time: 249 us -> 241 us (0.968)
  waiting for transfers between devices: 78.9 us -> 72.6 us
  starting transfers between devices: 56.9 us -> 59.7 us
  local copies, waits for them, and re-layouts: 15.4 us -> 12.8 us
    all_to_all x5, waiting for transfers between devices: 36.7 us -> 27.2 us  [exchange(): return lax.all_to_all(x, axis, 0, 0, tiled=True, axis_index_groups=groups)]
    dot_general x3 -> x5, matrix products: 9.99 us -> 6.79 us  [the longest x2 4 us: local(): jnp.dot(flat_inputs, weight, preferred_element_type=jnp.float32)]
    slice x5 -> x4, local copies, waits for them, and re-layouts: 3.18 us -> 0.35 us  [the longest x1 0.81 us: ring_sum_over_y(): down_late = y_shift(down[:, :split], 3)]
  transfers between devices with their start and end apart: 24 -> 24, of which waited for: 17 -> 15; matrix products, arithmetic and copies ran while one was open for 12% -> 16% of each run, Pallas kernels for 0% -> 0%
where the time goes in v4:
time: 241 us; the launch traced here: 240 us
  waiting for transfers between devices  72.6 us (30%)
  starting transfers between devices  59.7 us (25%)
  blocking collectives  34 us (14%)
  matrix products  30.7 us (13%)
  other arithmetic  15.4 us (6%)
  between operations  14.6 us (6%)
  local copies, waits for them, and re-layouts  12.8 us (5%)
    all_to_all x5, starting transfers between devices, exchange(): return lax.all_to_all(x, axis, 0, 0, tiled=True, axis_index_groups=groups)  37.5 us
    all_to_all x1, blocking collectives, exchange(): return lax.all_to_all(x, axis, 0, 0, tiled=True, axis_index_groups=groups)  34 us
    all_to_all x5, waiting for transfers between devices, exchange(): return lax.all_to_all(x, axis, 0, 0, tiled=True, axis_index_groups=groups)  27.2 us
    ppermute x9, waiting for transfers between devices, ctx_shift(): return lax.ppermute(x, 'ctx', [(i, (i + 2 * shift) % 8) for i in range(8)])  25.5 us
    dot_general x4, matrix products, upstream_block(): jnp.dot(logit_grads, head_weight, preferred_element_type=jnp.float32)  16.7 us
    ppermute x9, starting transfers between devices, ctx_shift(): return lax.ppermute(x, 'ctx', [(i, (i + 2 * shift) % 8) for i in range(8)])  12.1 us
    ppermute x6, starting transfers between devices, y_shift(): lax.ppermute(x, 'exp', [(i, (i + NZ * shift) % (NY * NZ)) for i in range(...  9.68 us
    ppermute x6, waiting for transfers between devices, y_shift(): lax.ppermute(x, 'exp', [(i, (i + NZ * shift) % (NY * NZ)) for i in range(...  8.66 us
  transfers between devices with their start and end apart: 24, of which 15 were waited for; matrix products, arithmetic and copies ran while one was open for 16% of the time, Pallas kernels for 0%

profile of v4, /device:TPU:32, one launch (start us, length us, event | category | flops | bytes accessed | tf_op | source)
XLA Modules:
  0.0 239.9 jit_solution(17088434669582099822)
XLA Ops:
  10.6 1.3 reduce_max.23
  11.9 1.5 exponential_reduce_fusion
  14.6 11.4 %all-to-all-start = ((f32[32,1,384]{2,1,0:T(1,128)}), f32[32,1,384]{2,1,0:T(1,128)S(1)}, u32[]{:S(2)}, u32[]{:S(2)}) async-start(f32[32,1,384]{2,1,0:T(1,128)} %all_to_all.42), calls=%async_computation | async-start | bytes 98304 | tf_op jit(solution)/shard_map/all_to_all | solution.py:13
  26.4 1.4 convolution_convert_fusion.1
  27.8 7.2 %all-to-all-done = f32[32,1,384]{2,1,0:T(1,128)S(1)} async-done(((f32[32,1,384]{2,1,0:T(1,128)}), f32[32,1,384]{2,1,0:T(1,128)S(1)}, u32[]{:S(2)}, u32[]{:S(2)}) %all-to-all-start) | async-done | bytes 49184 | tf_op jit(solution)/shard_map/all_to_all | solution.py:13
  36.2 4.3 %all-to-all-start.1 = ((f32[8,1,512]{2,1,0:T(1,128)}), f32[8,1,512]{2,1,0:T(1,128)S(1)}, u32[]{:S(2)}, u32[]{:S(2)}) async-start(f32[8,1,512]{2,1,0:T(1,128)} %broadcast_in_dim.66), calls=%async_computation.1 | async-start | bytes 32768 | tf_op jit(solution)/shard_map/all_to_all | solution.py:13
  40.7 5.3 %all-to-all-done.1 = f32[8,1,512]{2,1,0:T(1,128)S(1)} async-done(((f32[8,1,512]{2,1,0:T(1,128)}), f32[8,1,512]{2,1,0:T(1,128)S(1)}, u32[]{:S(2)}, u32[]{:S(2)}) %all-to-all-start.1) | async-done | bytes 16416 | tf_op jit(solution)/shard_map/all_to_all | solution.py:13
  46.0 5.7 %all-gather.2.cloned.1.call-done = bf16[1024,2560]{1,0:T(8,128)(2,1)} async-done(((bf16[128,2560]{1,0:T(8,128)(2,1)}), bf16[1024,2560]{1,0:T(8,128)(2,1)}) %all-gather.2.cloned.1.call-update) | async-done | bytes 5242896 | tf_op jit(solution)/shard_map/all_gather | solution.py:125
  53.5 4.5 %fusion.43 = f16[256,896]{1,0:T(8,128)(2,1)S(1)} fusion(bf16[2560,896]{1,0:T(8,128)(2,1)} %param.12, s32[256]{0:T(256)S(1)} %bitcast.110, f32[256]{0:T(256)S(1)} %bitcast.108, f32[256]{0:T(256)S(1)} %bitcast.109, bf16[1024,2560]{1,0:T(8,128)(2,1)} %all-gather.2.cloned.1.call-done, s32[]{:T(128)S(6)} %select_n.146, f32[256]{0:T(256)S(1)} %bitcast.107), kind=kOutput, calls=%fused_computation.58 | convolution fusion | flops 1180106752 | bytes 6361092 | tf_op jit(solution)/shard_map/dot_general | solution.py:200
  58.1 1.6 collective-permute-start
  59.7 1.8 collective-permute-start.1
  61.4 8.9 %all-to-all-start.2 = ((bf16[32,16,896]{2,1,0:T(8,128)(2,1)}), bf16[32,16,896]{2,1,0:T(8,128)(2,1)S(1)}, u32[]{:S(2)}, u32[]{:S(2)}) async-start(bf16[32,16,896]{2,1,0:T(8,128)(2,1)} %bitcast.12), calls=%async_computation.2 | async-start | bytes 1835008 | tf_op jit(solution)/shard_map/all_to_all | solution.py:13
  70.4 4.5 %fusion.47 = f16[256,896]{1,0:T(8,128)(2,1)S(1)} fusion(bf16[2560,896]{1,0:T(8,128)(2,1)} %param.12, s32[256]{0:T(256)S(1)} %bitcast.106, f32[256]{0:T(256)S(1)} %bitcast.103, f32[256]{0:T(256)S(1)} %bitcast.104, bf16[1024,2560]{1,0:T(8,128)(2,1)} %all-gather.2.cloned.1.call-done, s32[]{:T(128)S(6)} %select_n.151, f32[256]{0:T(256)S(1)} %bitcast.105), kind=kOutput, calls=%fused_computation.62 | convolution fusion | flops 1180106752 | bytes 6361092 | tf_op jit(solution)/shard_map/dot_general | solution.py:200
  76.2 2.8 %collective-permute-start.5 = (f16[128,896]{1,0:T(8,128)(2,1)S(1)}, f16[128,896]{1,0:T(8,128)(2,1)S(1)}, u32[]{:S(2)}, u32[]{:S(2)}) collective-permute-start(f16[128,896]{1,0:T(8,128)(2,1)S(1)} %add_convert_fusion.3), channel_id=1, source_target_pairs={{0,24},{1,25},{2,26},{3,27},{4,28},{5,29},{6,30},{7,31},{8,0},{9,1... | collective-permute-start | bytes 688136 | tf_op jit(solution)/shard_map/ppermute | solution.py:71
  79.0 4.5 %fusion.46 = f16[256,896]{1,0:T(8,128)(2,1)S(1)} fusion(bf16[2560,896]{1,0:T(8,128)(2,1)} %param.12, s32[256]{0:T(256)S(1)} %bitcast.102, f32[256]{0:T(256)S(1)} %bitcast.100, f32[256]{0:T(256)S(1)} %bitcast.101, bf16[1024,2560]{1,0:T(8,128)(2,1)} %all-gather.2.cloned.1.call-done, s32[]{:T(128)S(6)} %select_n.149, f32[256]{0:T(256)S(1)} %bitcast.99), kind=kOutput, calls=%fused_computation.61 | convolution fusion | flops 1180106752 | bytes 6361092 | tf_op jit(solution)/shard_map/dot_general | solution.py:200
  84.7 2.6 %collective-permute-start.3 = (f16[128,896]{1,0:T(8,128)(2,1)S(1)}, f16[128,896]{1,0:T(8,128)(2,1)S(1)}, u32[]{:S(2)}, u32[]{:S(2)}) collective-permute-start(f16[128,896]{1,0:T(8,128)(2,1)S(1)} %slice.117), channel_id=1, source_target_pairs={{0,24},{1,25},{2,26},{3,27},{4,28},{5,29},{6,30},{7,31},{8,0},{9,1... | collective-permute-start | bytes 688136 | tf_op jit(solution)/shard_map/ppermute | solution.py:71
  87.2 3.2 %fusion.45 = f32[256,896]{1,0:T(8,128)S(1)} fusion(bf16[2560,896]{1,0:T(8,128)(2,1)S(1)} %bitcast.112, s32[256]{0:T(256)S(1)} %bitcast.98, f32[256]{0:T(256)S(1)} %bitcast.95, f32[256]{0:T(256)S(1)} %bitcast.96, bf16[1024,2560]{1,0:T(8,128)(2,1)} %all-gather.2.cloned.1.call-done, s32[]{:T(128)S(6)} %select_n.147, f32[256]{0:T(256)S(1)} %bitcast.97), kind=kOutput, calls=%fused_computation.60 | convolution fusion | flops 1180336128 | bytes 6819844 | tf_op jit(solution)/shard_map/dot_general | solution.py:200
  90.4 5.0 %collective-permute-done.2 = f16[128,896]{1,0:T(8,128)(2,1)S(1)} collective-permute-done((f16[128,896]{1,0:T(8,128)(2,1)S(1)}, f16[128,896]{1,0:T(8,128)(2,1)S(1)}, u32[]{:S(2)}, u32[]{:S(2)}) %collective-permute-start.2) | collective-permute-done | bytes 229408 | tf_op jit(solution)/shard_map/ppermute | solution.py:71
  95.4 3.6 %collective-permute-done.4 = f16[128,896]{1,0:T(8,128)(2,1)S(1)} collective-permute-done((f16[128,896]{1,0:T(8,128)(2,1)S(1)}, f16[128,896]{1,0:T(8,128)(2,1)S(1)}, u32[]{:S(2)}, u32[]{:S(2)}) %collective-permute-start.4) | collective-permute-done | bytes 229408 | tf_op jit(solution)/shard_map/ppermute | solution.py:71
  100.2 7.2 %all-to-all-start.3 = ((f16[8,32,896]{2,1,0:T(8,128)(2,1)}), f16[8,32,896]{2,1,0:T(8,128)(2,1)S(1)}, u32[]{:S(2)}, u32[]{:S(2)}) async-start(f16[8,32,896]{2,1,0:T(8,128)(2,1)} %bitcast.26), calls=%async_computation.3 | async-start | bytes 917504 | tf_op jit(solution)/shard_map/all_to_all | solution.py:13
  107.4 2.7 %fusion.12 = f16[512,1024]{1,0:T(8,128)(2,1)S(1)} fusion(bf16[512,896]{1,0:T(8,128)(2,1)S(1)} %bitcast.86, bf16[1,896,1024]{2,1,0:T(8,128)(2,1)} %param.19), kind=kOutput, calls=%fused_computation.28 | convolution fusion | flops 940048384 | bytes 3801088 | tf_op jit(solution)/shard_map/dot_general | solution.py:210
  110.2 1.3 fusion.15
  111.4 1.9 pad_maximum_fusion
  113.3 8.0 %all-to-all-done.3 = f16[8,32,896]{2,1,0:T(8,128)(2,1)S(1)} async-done(((f16[8,32,896]{2,1,0:T(8,128)(2,1)}), f16[8,32,896]{2,1,0:T(8,128)(2,1)S(1)}, u32[]{:S(2)}, u32[]{:S(2)}) %all-to-all-start.3) | async-done | bytes 458784 | tf_op jit(solution)/shard_map/all_to_all | solution.py:13
  121.3 1.4 convolution_convert_fusion
  122.7 1.4 constant_dynamic-slice_fusion.7
  124.3 5.7 %all-to-all-start.4 = ((bf16[32,16,896]{2,1,0:T(8,128)(2,1)}), bf16[32,16,896]{2,1,0:T(8,128)(2,1)}, u32[]{:S(2)}, u32[]{:S(2)}) async-start(bf16[32,16,896]{2,1,0:T(8,128)(2,1)} %bitcast.29), calls=%async_computation.4 | async-start | bytes 1835008 | tf_op jit(solution)/shard_map/all_to_all | solution.py:13
  130.1 2.0 add_convert_fusion
  133.5 2.7 %collective-permute-start.8 = (f16[64,2048]{1,0:T(8,128)(2,1)S(1)}, f16[64,2048]{1,0:T(8,128)(2,1)}, u32[]{:S(2)}, u32[]{:S(2)}) collective-permute-start(f16[64,2048]{1,0:T(8,128)(2,1)S(1)} %get-tuple-element.40), channel_id=1, source_target_pairs={{0,192},{32,224},{64,0},{96,32},{128,64},{160,96},{192,128},{224,1... | collective-permute-start | bytes 786440 | tf_op jit(solution)/shard_map/ppermute | solution.py:28
  136.8 11.8 %collective-permute-done.7 = f16[64,2048]{1,0:T(8,128)(2,1)} collective-permute-done((f16[64,2048]{1,0:T(8,128)(2,1)}, f16[64,2048]{1,0:T(8,128)(2,1)}, u32[]{:S(2)}, u32[]{:S(2)}) %collective-permute-start.7) | collective-permute-done | bytes 262176 | tf_op jit(solution)/shard_map/ppermute | solution.py:28
  148.6 1.2 convert_add_fusion
  149.8 6.7 %all-to-all-done.4 = bf16[32,16,896]{2,1,0:T(8,128)(2,1)} async-done(((bf16[32,16,896]{2,1,0:T(8,128)(2,1)}), bf16[32,16,896]{2,1,0:T(8,128)(2,1)}, u32[]{:S(2)}, u32[]{:S(2)}) %all-to-all-start.4) | async-done | bytes 917536 | tf_op jit(solution)/shard_map/all_to_all | solution.py:13
  156.6 3.1 %fusion.18 = f16[512,1024]{1,0:T(8,128)(2,1)S(1)} fusion(bf16[512,896]{1,0:T(8,128)(2,1)} %bitcast.30, bf16[1,1024,896]{2,1,0:T(8,128)(2,1)} %param.21), kind=kOutput, calls=%fused_computation.30 | convolution fusion | flops 940048384 | bytes 3801088 | tf_op jit(solution)/shard_map/dot_general | solution.py:225
  160.1 1.9 collective-permute-done.10
  163.5 2.7 %collective-permute-start.12 = (f16[64,1024]{1,0:T(8,128)(2,1)}, f16[64,1024]{1,0:T(8,128)(2,1)S(1)}, u32[]{:S(2)}, u32[]{:S(2)}) collective-permute-start(f16[64,1024]{1,0:T(8,128)(2,1)} %get-tuple-element.47), channel_id=1, source_target_pairs={{0,192},{32,224},{64,0},{96,32},{128,64},{160,96},{192,128},{224,1... | collective-permute-start | bytes 393224 | tf_op jit(solution)/shard_map/ppermute | solution.py:28
  167.3 1.3 slice.121
  168.6 1.4 reshape.233
  170.8 1.4 collective-permute-done.12
  174.3 2.4 collective-permute-start.15
  176.7 1.2 collective-permute-start.16
  177.9 5.2 %collective-permute-done.14 = bf16[64,2176]{1,0:T(8,128)(2,1)S(1)} collective-permute-done((bf16[64,2176]{1,0:T(8,128)(2,1)S(1)}, bf16[64,2176]{1,0:T(8,128)(2,1)S(1)}, u32[]{:S(2)}, u32[]{:S(2)}) %collective-permute-start.14) | collective-permute-done | bytes 278560 | tf_op jit(solution)/shard_map/ppermute | solution.py:28
  183.1 4.8 %collective-permute-done.15 = bf16[64,2176]{1,0:T(8,128)(2,1)S(1)} collective-permute-done((bf16[64,2176]{1,0:T(8,128)(2,1)S(1)}, bf16[64,2176]{1,0:T(8,128)(2,1)S(1)}, u32[]{:S(2)}, u32[]{:S(2)}) %collective-permute-start.15) | collective-permute-done | bytes 278560 | tf_op jit(solution)/shard_map/ppermute | solution.py:28
  187.9 1.8 collective-permute-done.16
  189.8 2.9 %collective-permute-done.17 = bf16[256,2176]{1,0:T(8,128)(2,1)} collective-permute-done((bf16[256,2176]{1,0:T(8,128)(2,1)S(1)}, bf16[256,2176]{1,0:T(8,128)(2,1)}, u32[]{:S(2)}, u32[]{:S(2)}) %collective-permute-start.17) | collective-permute-done | bytes 1114144 | tf_op jit(solution)/shard_map/ppermute | solution.py:32
  192.7 1.4 broadcast_select_fusion.1
  194.2 1.3 fusion.4
  195.7 1.3 add_convert_fusion.1
  197.1 34.0 %all_to_all.63 = bf16[32,16,1024]{2,1,0:T(8,128)(2,1)S(1)} all-to-all(bf16[32,16,1024]{2,1,0:T(8,128)(2,1)S(1)} %bitcast.83), channel_id=1, replica_groups=mesh['ctx'=8,'exp'=32] {'exp'}, dimensions={0} | all-to-all | bytes 2097152 | tf_op jit(solution)/shard_map/all_to_all | solution.py:13
  (120 shorter events, 22.3 us)
Async XLA Ops:
  7.2 103.0 %copy-start = (bf16[1,896,1024]{2,1,0:T(8,128)(2,1)S(1)}, bf16[1,896,1024]{2,1,0:T(8,128)(2,1)}, u32[]{:S(2)}) copy-start(bf16[1,896,1024]{2,1,0:T(8,128)(2,1)} %param.20) | copy-start | bytes 5505028
  7.2 19.2 %copy-start.5 = (s32[16]{0:T(128)S(1)}, s32[16]{0:T(128)}, u32[]{:S(2)}) copy-start(s32[16]{0:T(128)} %param.14) | copy-start | bytes 196
  7.2 19.2 %copy-start.2 = (bf16[32,896]{1,0:T(8,128)(2,1)S(1)}, bf16[32,896]{1,0:T(8,128)(2,1)}, u32[]{:S(2)}) copy-start(bf16[32,896]{1,0:T(8,128)(2,1)} %param.16) | copy-start | bytes 172036
  7.2 20.6 %copy-start.10 = (s32[128]{0:T(128)S(1)}, s32[128]{0:T(128)}, u32[]{:S(2)}) copy-start(s32[128]{0:T(128)} %param.13) | copy-start | bytes 1540
  7.2 28.4 %copy-start.8 = (f32[128]{0:T(128)S(1)}, f32[128]{0:T(128)}, u32[]{:S(2)}) copy-start(f32[128]{0:T(128)} %param.15) | copy-start | bytes 1540
  7.2 44.5 %all-gather.2.cloned.1.call-start = ((), (), s32[]{:S(2)}) async-start(), calls=%async_computation.6 | async-start | bytes 5898240 | tf_op jit(solution)/shard_map/all_gather | solution.py:125
  13.5 12.6 %copy-start.3 = (s32[256]{0:T(256)}, s32[256]{0:T(256)S(1)}, u32[]{:S(2)}) copy-start(s32[256]{0:T(256)S(1)} %multiply_add_fusion.2) | copy-start | bytes 3076
  14.6 20.3 %all-to-all-start = ((f32[32,1,384]{2,1,0:T(1,128)}), f32[32,1,384]{2,1,0:T(1,128)S(1)}, u32[]{:S(2)}, u32[]{:S(2)}) async-start(f32[32,1,384]{2,1,0:T(1,128)} %all_to_all.42), calls=%async_computation | async-start | bytes 98304 | tf_op jit(solution)/shard_map/all_to_all | solution.py:13
  35.0 0.6 copy-start.1
  36.2 9.8 %all-to-all-start.1 = ((f32[8,1,512]{2,1,0:T(1,128)}), f32[8,1,512]{2,1,0:T(1,128)S(1)}, u32[]{:S(2)}, u32[]{:S(2)}) async-start(f32[8,1,512]{2,1,0:T(1,128)} %broadcast_in_dim.66), calls=%async_computation.1 | async-start | bytes 32768 | tf_op jit(solution)/shard_map/all_to_all | solution.py:13
  58.1 12.2 %collective-permute-start = (f16[128,896]{1,0:T(8,128)(2,1)S(1)}, f16[128,896]{1,0:T(8,128)(2,1)S(1)}, u32[]{:S(2)}, u32[]{:S(2)}) collective-permute-start(f16[128,896]{1,0:T(8,128)(2,1)S(1)} %get-tuple-element.49), channel_id=1, source_target_pairs={{0,8},{1,9},{2,10},{3,11},{4,12},{5,13},{6,14},{7,15},{8,16},{9,17... | collective-permute-start | bytes 688136 | tf_op jit(solution)/shard_map/ppermute | solution.py:71
  59.7 10.6 %collective-permute-start.1 = (f16[128,896]{1,0:T(8,128)(2,1)S(1)}, f16[128,896]{1,0:T(8,128)(2,1)}, u32[]{:S(2)}, u32[]{:S(2)}) collective-permute-start(f16[128,896]{1,0:T(8,128)(2,1)S(1)} %get-tuple-element.48), channel_id=1, source_target_pairs={{0,24},{1,25},{2,26},{3,27},{4,28},{5,29},{6,30},{7,31},{8,0},{9,1... | collective-permute-start | bytes 688136 | tf_op jit(solution)/shard_map/ppermute | solution.py:71
  61.4 38.8 %all-to-all-start.2 = ((bf16[32,16,896]{2,1,0:T(8,128)(2,1)}), bf16[32,16,896]{2,1,0:T(8,128)(2,1)S(1)}, u32[]{:S(2)}, u32[]{:S(2)}) async-start(bf16[32,16,896]{2,1,0:T(8,128)(2,1)} %bitcast.12), calls=%async_computation.2 | async-start | bytes 1835008 | tf_op jit(solution)/shard_map/all_to_all | solution.py:13
  75.0 12.2 %slice-start = ((s8[4587520]{0:T(1024)(128)(4,1)}), s8[4194304]{0:T(1024)(128)(4,1)S(1)}, s32[]{:S(2)}) async-start(s8[4587520]{0:T(1024)(128)(4,1)} %bitcast.111), calls=%async_computation.7 | async-start | bytes 8388608
  76.2 14.2 %collective-permute-start.5 = (f16[128,896]{1,0:T(8,128)(2,1)S(1)}, f16[128,896]{1,0:T(8,128)(2,1)S(1)}, u32[]{:S(2)}, u32[]{:S(2)}) collective-permute-start(f16[128,896]{1,0:T(8,128)(2,1)S(1)} %add_convert_fusion.3), channel_id=1, source_target_pairs={{0,24},{1,25},{2,26},{3,27},{4,28},{5,29},{6,30},{7,31},{8,0},{9,1... | collective-permute-start | bytes 688136 | tf_op jit(solution)/shard_map/ppermute | solution.py:71
  79.0 8.3 %slice-start.1 = ((s8[4587520]{0:T(1024)(128)(4,1)}), s8[393216]{0:T(1024)(128)(4,1)S(1)}, s32[]{:S(2)}) async-start(s8[4587520]{0:T(1024)(128)(4,1)} %bitcast.111), calls=%async_computation.8 | async-start | bytes 786432
  83.6 11.8 %collective-permute-start.2 = (f16[128,896]{1,0:T(8,128)(2,1)S(1)}, f16[128,896]{1,0:T(8,128)(2,1)S(1)}, u32[]{:S(2)}, u32[]{:S(2)}) collective-permute-start(f16[128,896]{1,0:T(8,128)(2,1)S(1)} %add_convert_fusion.4), channel_id=1, source_target_pairs={{0,8},{1,9},{2,10},{3,11},{4,12},{5,13},{6,14},{7,15},{8,16},{9,17... | collective-permute-start | bytes 688136 | tf_op jit(solution)/shard_map/ppermute | solution.py:71
  83.9 15.2 %collective-permute-start.4 = (f16[128,896]{1,0:T(8,128)(2,1)S(1)}, f16[128,896]{1,0:T(8,128)(2,1)S(1)}, u32[]{:S(2)}, u32[]{:S(2)}) collective-permute-start(f16[128,896]{1,0:T(8,128)(2,1)S(1)} %slice.119), channel_id=1, source_target_pairs={{0,8},{1,9},{2,10},{3,11},{4,12},{5,13},{6,14},{7,15},{8,16},{9,17... | collective-permute-start | bytes 688136 | tf_op jit(solution)/shard_map/ppermute | solution.py:71
  84.7 14.4 %collective-permute-start.3 = (f16[128,896]{1,0:T(8,128)(2,1)S(1)}, f16[128,896]{1,0:T(8,128)(2,1)S(1)}, u32[]{:S(2)}, u32[]{:S(2)}) collective-permute-start(f16[128,896]{1,0:T(8,128)(2,1)S(1)} %slice.117), channel_id=1, source_target_pairs={{0,24},{1,25},{2,26},{3,27},{4,28},{5,29},{6,30},{7,31},{8,0},{9,1... | collective-permute-start | bytes 688136 | tf_op jit(solution)/shard_map/ppermute | solution.py:71
  100.2 21.1 %all-to-all-start.3 = ((f16[8,32,896]{2,1,0:T(8,128)(2,1)}), f16[8,32,896]{2,1,0:T(8,128)(2,1)S(1)}, u32[]{:S(2)}, u32[]{:S(2)}) async-start(f16[8,32,896]{2,1,0:T(8,128)(2,1)} %bitcast.26), calls=%async_computation.3 | async-start | bytes 917504 | tf_op jit(solution)/shard_map/all_to_all | solution.py:13
  124.2 5.9 %collective-permute-start.6 = (f16[256,2048]{1,0:T(8,128)(2,1)S(1)}, f16[256,2048]{1,0:T(8,128)(2,1)}, u32[]{:S(2)}, u32[]{:S(2)}) collective-permute-start(f16[256,2048]{1,0:T(8,128)(2,1)S(1)} %constant_dynamic-slice_fusion.7), channel_id=1, source_target_pairs={{0,32},{32,0},{64,96},{96,64},{128,160},{160,128},{192,224},{224,1... | collective-permute-start | bytes 3145736 | tf_op jit(solution)/shard_map/ppermute | solution.py:32
  124.3 32.3 %all-to-all-start.4 = ((bf16[32,16,896]{2,1,0:T(8,128)(2,1)}), bf16[32,16,896]{2,1,0:T(8,128)(2,1)}, u32[]{:S(2)}, u32[]{:S(2)}) async-start(bf16[32,16,896]{2,1,0:T(8,128)(2,1)} %bitcast.29), calls=%async_computation.4 | async-start | bytes 1835008 | tf_op jit(solution)/shard_map/all_to_all | solution.py:13
  133.0 15.6 %collective-permute-start.7 = (f16[64,2048]{1,0:T(8,128)(2,1)}, f16[64,2048]{1,0:T(8,128)(2,1)}, u32[]{:S(2)}, u32[]{:S(2)}) collective-permute-start(f16[64,2048]{1,0:T(8,128)(2,1)} %get-tuple-element.38), channel_id=1, source_target_pairs={{0,64},{32,96},{64,128},{96,160},{128,192},{160,224},{192,0},{224,... | collective-permute-start | bytes 786440 | tf_op jit(solution)/shard_map/ppermute | solution.py:28
  133.5 15.0 %collective-permute-start.8 = (f16[64,2048]{1,0:T(8,128)(2,1)S(1)}, f16[64,2048]{1,0:T(8,128)(2,1)}, u32[]{:S(2)}, u32[]{:S(2)}) collective-permute-start(f16[64,2048]{1,0:T(8,128)(2,1)S(1)} %get-tuple-element.40), channel_id=1, source_target_pairs={{0,192},{32,224},{64,0},{96,32},{128,64},{160,96},{192,128},{224,1... | collective-permute-start | bytes 786440 | tf_op jit(solution)/shard_map/ppermute | solution.py:28
  136.2 12.3 %collective-permute-start.9 = (f16[64,2048]{1,0:T(8,128)(2,1)S(1)}, f16[64,2048]{1,0:T(8,128)(2,1)}, u32[]{:S(2)}, u32[]{:S(2)}) collective-permute-start(f16[64,2048]{1,0:T(8,128)(2,1)S(1)} %get-tuple-element.39), channel_id=1, source_target_pairs={{0,128},{32,160},{64,192},{96,224},{128,0},{160,32},{192,64},{224,... | collective-permute-start | bytes 786440 | tf_op jit(solution)/shard_map/ppermute | solution.py:28
  159.7 2.2 collective-permute-start.10
  163.0 7.8 %collective-permute-start.11 = (f16[64,1024]{1,0:T(8,128)(2,1)}, f16[64,1024]{1,0:T(8,128)(2,1)S(1)}, u32[]{:S(2)}, u32[]{:S(2)}) collective-permute-start(f16[64,1024]{1,0:T(8,128)(2,1)} %get-tuple-element.45), channel_id=1, source_target_pairs={{0,64},{32,96},{64,128},{96,160},{128,192},{160,224},{192,0},{224,... | collective-permute-start | bytes 393224 | tf_op jit(solution)/shard_map/ppermute | solution.py:28
  163.5 8.7 %collective-permute-start.12 = (f16[64,1024]{1,0:T(8,128)(2,1)}, f16[64,1024]{1,0:T(8,128)(2,1)S(1)}, u32[]{:S(2)}, u32[]{:S(2)}) collective-permute-start(f16[64,1024]{1,0:T(8,128)(2,1)} %get-tuple-element.47), channel_id=1, source_target_pairs={{0,192},{32,224},{64,0},{96,32},{128,64},{160,96},{192,128},{224,1... | collective-permute-start | bytes 393224 | tf_op jit(solution)/shard_map/ppermute | solution.py:28
  166.2 6.5 %collective-permute-start.13 = (f16[64,1024]{1,0:T(8,128)(2,1)S(1)}, f16[64,1024]{1,0:T(8,128)(2,1)S(1)}, u32[]{:S(2)}, u32[]{:S(2)}) collective-permute-start(f16[64,1024]{1,0:T(8,128)(2,1)S(1)} %get-tuple-element.46), channel_id=1, source_target_pairs={{0,128},{32,160},{64,192},{96,224},{128,0},{160,32},{192,64},{224,... | collective-permute-start | bytes 393224 | tf_op jit(solution)/shard_map/ppermute | solution.py:28
  170.0 3.1 %copy-start.6 = (pred[128]{0:T(512)(128)(4,1)S(1)}, pred[128]{0:T(512)(128)(4,1)}, u32[]{:S(2)}) copy-start(pred[128]{0:T(512)(128)(4,1)} %get-tuple-element.72) | copy-start | bytes 388
  170.0 3.1 %copy-start.7 = (pred[128]{0:T(512)(128)(4,1)S(1)}, pred[128]{0:T(512)(128)(4,1)}, u32[]{:S(2)}) copy-start(pred[128]{0:T(512)(128)(4,1)} %get-tuple-element.73) | copy-start | bytes 388
  173.4 9.7 %collective-permute-start.14 = (bf16[64,2176]{1,0:T(8,128)(2,1)S(1)}, bf16[64,2176]{1,0:T(8,128)(2,1)S(1)}, u32[]{:S(2)}, u32[]{:S(2)}) collective-permute-start(bf16[64,2176]{1,0:T(8,128)(2,1)S(1)} %get-tuple-element.50), channel_id=1, source_target_pairs={{0,64},{32,96},{64,128},{96,160},{128,192},{160,224},{192,0},{224,... | collective-permute-start | bytes 835592 | tf_op jit(solution)/shard_map/ppermute | solution.py:28
  174.3 13.6 %collective-permute-start.15 = (bf16[64,2176]{1,0:T(8,128)(2,1)S(1)}, bf16[64,2176]{1,0:T(8,128)(2,1)S(1)}, u32[]{:S(2)}, u32[]{:S(2)}) collective-permute-start(bf16[64,2176]{1,0:T(8,128)(2,1)S(1)} %get-tuple-element.50), channel_id=1, source_target_pairs={{0,192},{32,224},{64,0},{96,32},{128,64},{160,96},{192,128},{224,1... | collective-permute-start | bytes 835592 | tf_op jit(solution)/shard_map/ppermute | solution.py:28
  176.7 13.0 %collective-permute-start.16 = (bf16[64,2176]{1,0:T(8,128)(2,1)S(1)}, bf16[64,2176]{1,0:T(8,128)(2,1)S(1)}, u32[]{:S(2)}, u32[]{:S(2)}) collective-permute-start(bf16[64,2176]{1,0:T(8,128)(2,1)S(1)} %get-tuple-element.50), channel_id=1, source_target_pairs={{0,128},{32,160},{64,192},{96,224},{128,0},{160,32},{192,64},{224,... | collective-permute-start | bytes 835592 | tf_op jit(solution)/shard_map/ppermute | solution.py:28
  189.7 3.0 %collective-permute-start.17 = (bf16[256,2176]{1,0:T(8,128)(2,1)S(1)}, bf16[256,2176]{1,0:T(8,128)(2,1)}, u32[]{:S(2)}, u32[]{:S(2)}) collective-permute-start(bf16[256,2176]{1,0:T(8,128)(2,1)S(1)} %constant_dynamic-update-slice_fusion), channel_id=1, source_target_pairs={{0,32},{32,0},{64,96},{96,64},{128,160},{160,128},{192,224},{224,1... | collective-permute-start | bytes 3342344 | tf_op jit(solution)/shard_map/ppermute | solution.py:32
  194.2 1.5 copy-start.9
  197.1 34.0 %copy-start.4 = (s32[256]{0:T(256)S(1)}, s32[256]{0:T(256)}, u32[]{:S(2)}) copy-start(s32[256]{0:T(256)} %copy-done.3) | copy-start | bytes 3076
Sparse Core Ops, SparseCore 0:
  9.9 41.8 all-gather.1

commit v5 on v4

--- a/solution.py
+++ b/solution.py
@@ -78,7 +78,6 @@
     split = far.shape[0] // 2
     from_down = y_shift(far[:split], 1)
     from_up = y_shift(far[split:], 3)
-    from_down, from_up, per_row = lax.optimization_barrier((from_down, from_up, per_row))
     up = block((y + 1) % NY, per_row)
     up_late = y_shift(up[split:], 1)
     down = block((y + 3) % NY, per_row)
@@ -145,24 +144,34 @@
     local_max = jnp.max(scores, axis=1)
     local_sum = jnp.sum(jnp.exp(scores - local_max[:, None]), axis=1)
     send_prob = jnp.dot(
-        chosen, probs.reshape(-1).astype(jnp.float32), precision=lax.Precision.HIGHEST
-    ).reshape(exp_count, capacity)
+        chosen.astype(jnp.bfloat16), probs.reshape(-1), preferred_element_type=jnp.float32
+    ).astype(jnp.bfloat16)
     send_input = jnp.dot(slot_owner, moe_input, preferred_element_type=jnp.float32).astype(
         jnp.bfloat16
     )
-    packed = jnp.concatenate(
+    sum_high, sum_rest = split_high(local_sum)
+    sum_mid, sum_low = split_high(sum_rest)
+    stats = jnp.stack([local_max, sum_high, sum_mid, sum_low]).astype(jnp.bfloat16)
+    extra = jnp.concatenate(
         [
-            jnp.broadcast_to(local_max[None], (exp_count, row_count)),
-            jnp.broadcast_to(local_sum[None], (exp_count, row_count)),
-            jnp.pad(send_prob, ((0, 0), (0, 128 - capacity))),
+            jnp.broadcast_to(stats[None], (exp_count, 4, row_count)),
+            jnp.pad(
+                send_prob.reshape(exp_count, 1, capacity),
+                ((0, 0), (0, capacity - 5), (0, row_count - capacity)),
+            ),
         ],
         axis=1,
-    )
-    packed = exchange(packed, "exp")
-    all_max = packed[:, :row_count]
+    ).reshape(slot_count, row_count)
+    got = exchange(jnp.concatenate([send_input, extra], axis=1), "exp")
+    flat_inputs = got[:, :feature_width]
+    extra = got[:, feature_width:].reshape(exp_count, capacity, row_count)
+    flat_prob = extra[:, 4, :capacity].reshape(-1).astype(jnp.float32)
+    stats = extra[:, :4].astype(jnp.float32)
+    all_max = stats[:, 0]
     row_max = jnp.max(all_max, axis=0)
-    row_total = jnp.sum(packed[:, row_count : 2 * row_count] * jnp.exp(all_max - row_max), axis=0)
-    flat_prob = packed[:, 2 * row_count : 2 * row_count + capacity].reshape(-1)
+    row_total = jnp.sum(
+        (stats[:, 1] + stats[:, 2] + stats[:, 3]) * jnp.exp(all_max - row_max), axis=0
+    )
     rows = jnp.concatenate([row_max, row_total, token_weights, token_ids.astype(jnp.float32)])
     rows = exchange(jnp.broadcast_to(rows[None], (ctx_count, 4 * row_count)), "ctx")
     rows = rows.reshape(ctx_count, 4, row_count).transpose(1, 0, 2).reshape(4, seq_length)
@@ -173,6 +182,9 @@
     down_w = w_down[0]
     row_max, row_total, weights = rows[0], rows[1], rows[2]
     all_ids = rows[3].astype(jnp.int32)
+
+    one = 1 - jnp.minimum(lax.axis_index("ctx"), 0)
+    head_weight = lax.optimization_barrier(head_weight * one.astype(jnp.bfloat16))
 
     slab_count = slab_order.shape[0]
     next_ids = jnp.concatenate([all_ids[1:], all_ids[-1:]]).reshape(slab_count, SLAB)
@@ -201,10 +213,8 @@
         return (partial * 4096.0).astype(jnp.float16)
 
     far = upstream_block((lax.axis_index("exp") // NZ + 2) % NY, per_row)
-    far, send_input = lax.optimization_barrier((far, send_input))
-    flat_inputs = exchange(send_input, "exp")
+    far, flat_inputs = lax.optimization_barrier((far, flat_inputs))
     over_y = ring_sum_over_y(upstream_block, far, per_row)
-    flat_inputs, over_y = lax.optimization_barrier((flat_inputs, over_y))
     part_both = jnp.concatenate(
         [
             jnp.dot(flat_inputs, weight, preferred_element_type=jnp.float32).astype(jnp.float16)
@@ -212,15 +222,14 @@
         ],
         axis=1,
     )
+    both_sum = ctx_scatter(part_both)
     upstream = exchange_sum(over_y, "exp", Z_GROUPS, NZ) * (1.0 / 4096.0)
     upstream_sent = upstream.astype(jnp.bfloat16)
 
     send_upstream = jnp.dot(slot_owner, upstream_sent, preferred_element_type=jnp.float32).astype(
         jnp.bfloat16
     )
-    send_upstream, part_both = lax.optimization_barrier((send_upstream, part_both))
     flat_upstream = exchange(send_upstream, "exp")
-    both_sum = ctx_scatter(part_both)
     flat_upstream, both_sum = lax.optimization_barrier((flat_upstream, both_sum))
     part_back = lax.dot_general(
         flat_upstream, down_w, CONTRACT_LAST, preferred_element_type=jnp.float32

time: 241 us -> 227 us (0.942)
  starting transfers between devices: 59.7 us -> 43.2 us
  waiting for transfers between devices: 72.6 us -> 81.3 us
  matrix products: 30.7 us -> 22.6 us
  other arithmetic: 15.4 us -> 20.6 us
  local copies, waits for them, and re-layouts: 12.8 us -> 9.89 us
    all_to_all x5 -> x4, waiting for transfers between devices: 27.2 us -> 42.9 us  [exchange(): return lax.all_to_all(x, axis, 0, 0, tiled=True, axis_index_groups=groups)]
    all_to_all x5 -> x4, starting transfers between devices: 37.5 us -> 25.3 us  [exchange(): return lax.all_to_all(x, axis, 0, 0, tiled=True, axis_index_groups=groups)]
    dot_general x4, matrix products: 16.7 us -> 10.1 us  [upstream_block(): jnp.dot(logit_grads, head_weight, preferred_element_type=jnp.float32)]
    all_gather x1, waiting for transfers between devices: 5.7 us -> 0.01 us  [local(): all_logits = lax.all_gather(logits, 'ctx', axis=0, tiled=True)]
    mul x0 -> x1, other arithmetic: none -> 4.86 us  [local(): head_weight * one.astype(jnp.bfloat16)]
    dynamic_slice x5 -> x4, local copies, waits for them, and re-layouts: 3.96 us -> 1.14 us  [rows_at(): return lax.dynamic_slice_in_dim(x, index * count, count, axis=0)]
    unnamed x30 -> x31, local copies, waits for them, and re-layouts: 3.06 us -> 4.99 us
  transfers between devices with their start and end apart: 24 -> 23, of which waited for: 15 -> 17; matrix products, arithmetic and copies ran while one was open for 16% -> 14% of each run, Pallas kernels for 0% -> 0%
where the time goes in v5:
time: 227 us; the launch traced here: 226 us
  waiting for transfers between devices  81.3 us (36%)
  starting transfers between devices  43.2 us (19%)
  blocking collectives  33.6 us (15%)
  matrix products  22.6 us (10%)
  other arithmetic  20.6 us (9%)
  between operations  14.7 us (6%)
  local copies, waits for them, and re-layouts  9.89 us (4%)
    all_to_all x4, waiting for transfers between devices, exchange(): return lax.all_to_all(x, axis, 0, 0, tiled=True, axis_index_groups=groups)  42.9 us
    all_to_all x1, blocking collectives, exchange(): return lax.all_to_all(x, axis, 0, 0, tiled=True, axis_index_groups=groups)  33.6 us
    ppermute x9, waiting for transfers between devices, ctx_shift(): return lax.ppermute(x, 'ctx', [(i, (i + 2 * shift) % 8) for i in range(8)])  26.6 us
    all_to_all x4, starting transfers between devices, exchange(): return lax.all_to_all(x, axis, 0, 0, tiled=True, axis_index_groups=groups)  25.3 us
    dot_general x4, matrix products, upstream_block(): jnp.dot(logit_grads, head_weight, preferred_element_type=jnp.float32)  10.1 us
    ppermute x9, starting transfers between devices, ctx_shift(): return lax.ppermute(x, 'ctx', [(i, (i + 2 * shift) % 8) for i in range(8)])  9.87 us
    ppermute x6, starting transfers between devices, y_shift(): lax.ppermute(x, 'exp', [(i, (i + NZ * shift) % (NY * NZ)) for i in range(...  7.81 us
    ppermute x6, waiting for transfers between devices, y_shift(): lax.ppermute(x, 'exp', [(i, (i + NZ * shift) % (NY * NZ)) for i in range(...  6.4 us
  transfers between devices with their start and end apart: 23, of which 17 were waited for; matrix products, arithmetic and copies ran while one was open for 14% of the time, Pallas kernels for 0%

profile of v5, /device:TPU:32, one launch (start us, length us, event | category | flops | bytes accessed | tf_op | source)
XLA Modules:
  0.0 226.0 jit_solution(14587343576911813479)
XLA Ops:
  11.1 1.3 reduce_max.25
  12.4 1.5 exponential_reduce_fusion
  14.6 1.1 pad_maximum_fusion
  15.8 11.4 %all-to-all-start = ((bf16[32,16,1024]{2,1,0:T(8,128)(2,1)}), bf16[32,16,1024]{2,1,0:T(8,128)(2,1)S(1)}, u32[]{:S(2)}, u32[]{:S(2)}) async-start(bf16[32,16,1024]{2,1,0:T(8,128)(2,1)} %pad_maximum_fusion), calls=%async_computation | async-start | bytes 2097152 | tf_op jit(solution)/shard_map/all_to_all | solution.py:13
  27.3 4.9 %broadcast_multiply_fusion = bf16[2560,896]{1,0:T(8,128)(2,1)} fusion(bf16[2560,896]{1,0:T(8,128)(2,1)} %param.12, bf16[]{:T(256)S(6)} %convert_element_type.284), kind=kLoop, calls=%fused_computation.16 | loop fusion | flops 2293760 | bytes 9175042 | tf_op jit(solution)/shard_map/mul | solution.py:187
  32.1 23.5 %all-to-all-done = bf16[32,16,1024]{2,1,0:T(8,128)(2,1)S(1)} async-done(((bf16[32,16,1024]{2,1,0:T(8,128)(2,1)}), bf16[32,16,1024]{2,1,0:T(8,128)(2,1)S(1)}, u32[]{:S(2)}, u32[]{:S(2)}) %all-to-all-start) | async-done | bytes 1048608 | tf_op jit(solution)/shard_map/all_to_all | solution.py:13
  57.1 4.3 %all-to-all-start.1 = ((f32[8,1,512]{2,1,0:T(1,128)}), f32[8,1,512]{2,1,0:T(1,128)S(1)}, u32[]{:S(2)}, u32[]{:S(2)}) async-start(f32[8,1,512]{2,1,0:T(1,128)} %broadcast_in_dim.63), calls=%async_computation.1 | async-start | bytes 32768 | tf_op jit(solution)/shard_map/all_to_all | solution.py:13
  61.5 1.0 slice.141
  62.6 4.2 %all-to-all-done.1 = f32[8,1,512]{2,1,0:T(1,128)S(1)} async-done(((f32[8,1,512]{2,1,0:T(1,128)}), f32[8,1,512]{2,1,0:T(1,128)S(1)}, u32[]{:S(2)}, u32[]{:S(2)}) %all-to-all-start.1) | async-done | bytes 16416 | tf_op jit(solution)/shard_map/all_to_all | solution.py:13
  68.6 4.7 %fusion.47 = f16[256,896]{1,0:T(8,128)(2,1)S(1)} fusion(bf16[2560,896]{1,0:T(8,128)(2,1)} %broadcast_multiply_fusion, s32[256]{0:T(256)S(1)} %bitcast.126, f32[256]{0:T(256)S(1)} %bitcast.123, f32[256]{0:T(256)S(1)} %bitcast.124, bf16[1024,2560]{1,0:T(8,128)(2,1)} %all-gather.2.cloned.1.call-done, s32[]{:T(128)S(6)} %select_n.151, f32[256]{0:T(256)S(1)} %bitcast.125), kind=kOutput, calls=%fused_computation.66 | convolution fusion | flops 1180106752 | bytes 6361092 | tf_op jit(solution)/shard_map/dot_general | solution.py:212
  73.3 1.2 collective-permute-start.2
  74.5 1.8 fusion.46
  77.4 2.4 %collective-permute-start.4 = (f16[128,896]{1,0:T(8,128)(2,1)S(1)}, f16[128,896]{1,0:T(8,128)(2,1)S(1)}, u32[]{:S(2)}, u32[]{:S(2)}) collective-permute-start(f16[128,896]{1,0:T(8,128)(2,1)S(1)} %get-tuple-element.35), channel_id=1, source_target_pairs={{0,24},{1,25},{2,26},{3,27},{4,28},{5,29},{6,30},{7,31},{8,0},{9,1... | collective-permute-start | bytes 688136 | tf_op jit(solution)/shard_map/ppermute | solution.py:71
  79.8 1.8 fusion.45
  81.9 1.8 fusion.44
  83.8 1.0 collective-permute-done
  85.6 2.7 %collective-permute-start.5 = (f16[128,896]{1,0:T(8,128)(2,1)S(1)}, f16[128,896]{1,0:T(8,128)(2,1)S(1)}, u32[]{:S(2)}, u32[]{:S(2)}) collective-permute-start(f16[128,896]{1,0:T(8,128)(2,1)S(1)} %add_convert_fusion.3), channel_id=1, source_target_pairs={{0,24},{1,25},{2,26},{3,27},{4,28},{5,29},{6,30},{7,31},{8,0},{9,1... | collective-permute-start | bytes 688136 | tf_op jit(solution)/shard_map/ppermute | solution.py:71
  88.3 1.3 fusion.12
  89.6 2.0 collective-permute-done.3
  91.6 2.9 %collective-permute-done.1 = f16[128,896]{1,0:T(8,128)(2,1)S(1)} collective-permute-done((f16[128,896]{1,0:T(8,128)(2,1)S(1)}, f16[128,896]{1,0:T(8,128)(2,1)S(1)}, u32[]{:S(2)}, u32[]{:S(2)}) %collective-permute-start.1) | collective-permute-done | bytes 229408 | tf_op jit(solution)/shard_map/ppermute | solution.py:71
  95.7 4.0 %all-to-all-start.2 = ((f16[8,32,896]{2,1,0:T(8,128)(2,1)}), f16[8,32,896]{2,1,0:T(8,128)(2,1)S(1)}, u32[]{:S(2)}, u32[]{:S(2)}) async-start(f16[8,32,896]{2,1,0:T(8,128)(2,1)} %bitcast.30), calls=%async_computation.2 | async-start | bytes 917504 | tf_op jit(solution)/shard_map/all_to_all | solution.py:13
  99.7 2.4 %fusion.15 = f16[512,1024]{1,0:T(8,128)(2,1)S(1)} fusion(bf16[512,896]{1,0:T(8,128)(2,1)} %slice.141, bf16[1,896,1024]{2,1,0:T(8,128)(2,1)S(1)} %copy-done), kind=kOutput, calls=%fused_computation.33 | convolution fusion | flops 940048384 | bytes 3801088 | tf_op jit(solution)/shard_map/dot_general | solution.py:220
  103.1 1.2 fusion.50
  104.3 8.3 %all-to-all-done.2 = f16[8,32,896]{2,1,0:T(8,128)(2,1)S(1)} async-done(((f16[8,32,896]{2,1,0:T(8,128)(2,1)}), f16[8,32,896]{2,1,0:T(8,128)(2,1)S(1)}, u32[]{:S(2)}, u32[]{:S(2)}) %all-to-all-start.2) | async-done | bytes 458784 | tf_op jit(solution)/shard_map/all_to_all | solution.py:13
  112.7 1.3 convolution_convert_fusion
  114.0 5.7 %all-to-all-start.3 = ((bf16[32,16,896]{2,1,0:T(8,128)(2,1)}), bf16[32,16,896]{2,1,0:T(8,128)(2,1)}, u32[]{:S(2)}, u32[]{:S(2)}) async-start(bf16[32,16,896]{2,1,0:T(8,128)(2,1)} %bitcast.99), calls=%async_computation.3 | async-start | bytes 1835008 | tf_op jit(solution)/shard_map/all_to_all | solution.py:13
  119.8 1.8 add_convert_fusion
  122.8 1.2 collective-permute-start.9
  124.0 2.1 collective-permute-start.8
  126.1 6.0 %collective-permute-done.9 = f16[64,2048]{1,0:T(8,128)(2,1)S(1)} collective-permute-done((f16[64,2048]{1,0:T(8,128)(2,1)S(1)}, f16[64,2048]{1,0:T(8,128)(2,1)S(1)}, u32[]{:S(2)}, u32[]{:S(2)}) %collective-permute-start.9) | collective-permute-done | bytes 262176 | tf_op jit(solution)/shard_map/ppermute | solution.py:28
  132.2 1.3 collective-permute-done.8
  133.4 1.6 collective-permute-done.7
  135.0 1.2 convert_add_fusion
  136.1 6.9 %all-to-all-done.3 = bf16[32,16,896]{2,1,0:T(8,128)(2,1)} async-done(((bf16[32,16,896]{2,1,0:T(8,128)(2,1)}), bf16[32,16,896]{2,1,0:T(8,128)(2,1)}, u32[]{:S(2)}, u32[]{:S(2)}) %all-to-all-start.3) | async-done | bytes 917536 | tf_op jit(solution)/shard_map/all_to_all | solution.py:13
  143.0 3.1 %fusion.18 = f16[512,1024]{1,0:T(8,128)(2,1)S(1)} fusion(bf16[512,896]{1,0:T(8,128)(2,1)} %bitcast.32, bf16[1,1024,896]{2,1,0:T(8,128)(2,1)} %param.21), kind=kOutput, calls=%fused_computation.34 | convolution fusion | flops 940048384 | bytes 3801088 | tf_op jit(solution)/shard_map/dot_general | solution.py:234
  146.3 1.9 collective-permute-done.10
  149.2 1.1 collective-permute-start.13
  150.3 2.1 collective-permute-start.12
  153.5 3.8 %collective-permute-done.13 = f16[64,1024]{1,0:T(8,128)(2,1)S(1)} collective-permute-done((f16[64,1024]{1,0:T(8,128)(2,1)}, f16[64,1024]{1,0:T(8,128)(2,1)S(1)}, u32[]{:S(2)}, u32[]{:S(2)}) %collective-permute-start.13) | collective-permute-done | bytes 131104 | tf_op jit(solution)/shard_map/ppermute | solution.py:28
  157.7 1.7 collective-permute-done.11
  159.4 1.1 multiply_convert_fusion.19
  161.1 3.2 %collective-permute-start.15 = (bf16[64,2176]{1,0:T(8,128)(2,1)S(1)}, bf16[64,2176]{1,0:T(8,128)(2,1)S(1)}, u32[]{:S(2)}, u32[]{:S(2)}) collective-permute-start(bf16[64,2176]{1,0:T(8,128)(2,1)S(1)} %get-tuple-element.36), channel_id=1, source_target_pairs={{0,192},{32,224},{64,0},{96,32},{128,64},{160,96},{192,128},{224,1... | collective-permute-start | bytes 835592 | tf_op jit(solution)/shard_map/ppermute | solution.py:28
  164.3 11.9 %collective-permute-done.14 = bf16[64,2176]{1,0:T(8,128)(2,1)S(1)} collective-permute-done((bf16[64,2176]{1,0:T(8,128)(2,1)S(1)}, bf16[64,2176]{1,0:T(8,128)(2,1)S(1)}, u32[]{:S(2)}, u32[]{:S(2)}) %collective-permute-start.14) | collective-permute-done | bytes 278560 | tf_op jit(solution)/shard_map/ppermute | solution.py:28
  176.3 2.9 %collective-permute-done.17 = bf16[256,2176]{1,0:T(8,128)(2,1)} collective-permute-done((bf16[256,2176]{1,0:T(8,128)(2,1)S(1)}, bf16[256,2176]{1,0:T(8,128)(2,1)}, u32[]{:S(2)}, u32[]{:S(2)}) %collective-permute-start.17) | collective-permute-done | bytes 1114144 | tf_op jit(solution)/shard_map/ppermute | solution.py:32
  179.2 1.4 broadcast_select_fusion.1
  180.7 1.3 fusion.4
  182.2 1.3 add_convert_fusion.1
  183.6 33.6 %all_to_all.45 = bf16[32,16,1024]{2,1,0:T(8,128)(2,1)S(1)} all-to-all(bf16[32,16,1024]{2,1,0:T(8,128)(2,1)S(1)} %bitcast.96), channel_id=1, replica_groups=mesh['ctx'=8,'exp'=32] {'exp'}, dimensions={0} | all-to-all | bytes 2097152 | tf_op jit(solution)/shard_map/all_to_all | solution.py:13
  (126 shorter events, 19.3 us)
Async XLA Ops:
  7.2 92.5 %copy-start = (bf16[1,896,1024]{2,1,0:T(8,128)(2,1)S(1)}, bf16[1,896,1024]{2,1,0:T(8,128)(2,1)}, u32[]{:S(2)}) copy-start(bf16[1,896,1024]{2,1,0:T(8,128)(2,1)} %param.20) | copy-start | bytes 5505028
  7.2 7.0 %copy-start.5 = (bf16[32,896]{1,0:T(8,128)(2,1)S(1)}, bf16[32,896]{1,0:T(8,128)(2,1)}, u32[]{:S(2)}) copy-start(bf16[32,896]{1,0:T(8,128)(2,1)} %param.16) | copy-start | bytes 172036
  7.2 59.5 %all-gather.2.cloned.1.call-start = ((), (), s32[]{:S(2)}) async-start(), calls=%async_computation.5 | async-start | bytes 5898240 | tf_op jit(solution)/shard_map/all_gather | solution.py:124
  14.6 12.5 %copy-start.11 = (s32[128]{0:T(128)S(1)}, s32[128]{0:T(128)}, u32[]{:S(2)}) copy-start(s32[128]{0:T(128)} %param.13) | copy-start | bytes 1540
  14.6 12.5 %copy-start.6 = (s32[16]{0:T(128)S(1)}, s32[16]{0:T(128)}, u32[]{:S(2)}) copy-start(s32[16]{0:T(128)} %param.14) | copy-start | bytes 196
  15.8 39.9 %all-to-all-start = ((bf16[32,16,1024]{2,1,0:T(8,128)(2,1)}), bf16[32,16,1024]{2,1,0:T(8,128)(2,1)S(1)}, u32[]{:S(2)}, u32[]{:S(2)}) async-start(bf16[32,16,1024]{2,1,0:T(8,128)(2,1)} %pad_maximum_fusion), calls=%async_computation | async-start | bytes 2097152 | tf_op jit(solution)/shard_map/all_to_all | solution.py:13
  27.3 29.2 %copy-start.7 = (f32[128]{0:T(128)S(1)}, f32[128]{0:T(128)}, u32[]{:S(2)}) copy-start(f32[128]{0:T(128)} %param.15) | copy-start | bytes 1540
  55.7 0.7 copy-start.4
  57.1 9.7 %all-to-all-start.1 = ((f32[8,1,512]{2,1,0:T(1,128)}), f32[8,1,512]{2,1,0:T(1,128)S(1)}, u32[]{:S(2)}, u32[]{:S(2)}) async-start(f32[8,1,512]{2,1,0:T(1,128)} %broadcast_in_dim.63), calls=%async_computation.1 | async-start | bytes 32768 | tf_op jit(solution)/shard_map/all_to_all | solution.py:13
  61.5 13.0 %slice-start = ((s8[4587520]{0:T(1024)(128)(4,1)}), s8[393216]{0:T(1024)(128)(4,1)S(1)}, s32[]{:S(2)}) async-start(s8[4587520]{0:T(1024)(128)(4,1)} %bitcast.92), calls=%async_computation.6 | async-start | bytes 786432
  68.5 6.0 %slice-start.1 = ((s8[4587520]{0:T(1024)(128)(4,1)}), s8[4194304]{0:T(1024)(128)(4,1)S(1)}, s32[]{:S(2)}) async-start(s8[4587520]{0:T(1024)(128)(4,1)} %bitcast.92), calls=%async_computation.7 | async-start | bytes 8388608
  68.6 6.0 %copy-start.8 = (bf16[1024,2560]{1,0:T(8,128)(2,1)S(1)}, bf16[1024,2560]{1,0:T(8,128)(2,1)}, u32[]{:S(2)}) copy-start(bf16[1024,2560]{1,0:T(8,128)(2,1)} %all-gather.2.cloned.1.call-done) | copy-start | bytes 15728644
  73.3 16.3 %collective-permute-start.2 = (f16[128,896]{1,0:T(8,128)(2,1)S(1)}, f16[128,896]{1,0:T(8,128)(2,1)S(1)}, u32[]{:S(2)}, u32[]{:S(2)}) collective-permute-start(f16[128,896]{1,0:T(8,128)(2,1)S(1)} %slice.142), channel_id=1, source_target_pairs={{0,24},{1,25},{2,26},{3,27},{4,28},{5,29},{6,30},{7,31},{8,0},{9,1... | collective-permute-start | bytes 688136 | tf_op jit(solution)/shard_map/ppermute | solution.py:71
  76.4 8.3 %collective-permute-start = (f16[128,896]{1,0:T(8,128)(2,1)S(1)}, f16[128,896]{1,0:T(8,128)(2,1)S(1)}, u32[]{:S(2)}, u32[]{:S(2)}) collective-permute-start(f16[128,896]{1,0:T(8,128)(2,1)S(1)} %get-tuple-element.34), channel_id=1, source_target_pairs={{0,8},{1,9},{2,10},{3,11},{4,12},{5,13},{6,14},{7,15},{8,16},{9,17... | collective-permute-start | bytes 688136 | tf_op jit(solution)/shard_map/ppermute | solution.py:71
  77.4 8.2 %collective-permute-start.4 = (f16[128,896]{1,0:T(8,128)(2,1)S(1)}, f16[128,896]{1,0:T(8,128)(2,1)S(1)}, u32[]{:S(2)}, u32[]{:S(2)}) collective-permute-start(f16[128,896]{1,0:T(8,128)(2,1)S(1)} %get-tuple-element.35), channel_id=1, source_target_pairs={{0,24},{1,25},{2,26},{3,27},{4,28},{5,29},{6,30},{7,31},{8,0},{9,1... | collective-permute-start | bytes 688136 | tf_op jit(solution)/shard_map/ppermute | solution.py:71
  81.6 10.0 %collective-permute-start.3 = (f16[128,896]{1,0:T(8,128)(2,1)S(1)}, f16[128,896]{1,0:T(8,128)(2,1)S(1)}, u32[]{:S(2)}, u32[]{:S(2)}) collective-permute-start(f16[128,896]{1,0:T(8,128)(2,1)S(1)} %slice.144), channel_id=1, source_target_pairs={{0,8},{1,9},{2,10},{3,11},{4,12},{5,13},{6,14},{7,15},{8,16},{9,17... | collective-permute-start | bytes 688136 | tf_op jit(solution)/shard_map/ppermute | solution.py:71
  81.9 6.4 %copy-start.3 = (bf16[512,896]{1,0:T(8,128)(2,1)S(1)}, bf16[512,896]{1,0:T(8,128)(2,1)}, u32[]{:S(2)}) copy-start(bf16[512,896]{1,0:T(8,128)(2,1)} %slice.141) | copy-start | bytes 2752516
  81.9 6.4 %copy-start.9 = (bf16[1,896,1024]{2,1,0:T(8,128)(2,1)S(1)}, bf16[1,896,1024]{2,1,0:T(8,128)(2,1)}, u32[]{:S(2)}) copy-start(bf16[1,896,1024]{2,1,0:T(8,128)(2,1)} %param.19) | copy-start | bytes 5505028
  84.9 9.7 %collective-permute-start.1 = (f16[128,896]{1,0:T(8,128)(2,1)S(1)}, f16[128,896]{1,0:T(8,128)(2,1)S(1)}, u32[]{:S(2)}, u32[]{:S(2)}) collective-permute-start(f16[128,896]{1,0:T(8,128)(2,1)S(1)} %add_convert_fusion.4), channel_id=1, source_target_pairs={{0,8},{1,9},{2,10},{3,11},{4,12},{5,13},{6,14},{7,15},{8,16},{9,17... | collective-permute-start | bytes 688136 | tf_op jit(solution)/shard_map/ppermute | solution.py:71
  85.6 9.0 %collective-permute-start.5 = (f16[128,896]{1,0:T(8,128)(2,1)S(1)}, f16[128,896]{1,0:T(8,128)(2,1)S(1)}, u32[]{:S(2)}, u32[]{:S(2)}) collective-permute-start(f16[128,896]{1,0:T(8,128)(2,1)S(1)} %add_convert_fusion.3), channel_id=1, source_target_pairs={{0,24},{1,25},{2,26},{3,27},{4,28},{5,29},{6,30},{7,31},{8,0},{9,1... | collective-permute-start | bytes 688136 | tf_op jit(solution)/shard_map/ppermute | solution.py:71
  95.7 16.9 %all-to-all-start.2 = ((f16[8,32,896]{2,1,0:T(8,128)(2,1)}), f16[8,32,896]{2,1,0:T(8,128)(2,1)S(1)}, u32[]{:S(2)}, u32[]{:S(2)}) async-start(f16[8,32,896]{2,1,0:T(8,128)(2,1)} %bitcast.30), calls=%async_computation.2 | async-start | bytes 917504 | tf_op jit(solution)/shard_map/all_to_all | solution.py:13
  102.1 1.0 copy-start.1
  104.3 15.5 %collective-permute-start.6 = (f16[256,2048]{1,0:T(8,128)(2,1)}, f16[256,2048]{1,0:T(8,128)(2,1)}, u32[]{:S(2)}, u32[]{:S(2)}) collective-permute-start(f16[256,2048]{1,0:T(8,128)(2,1)} %fusion.50), channel_id=1, source_target_pairs={{0,32},{32,0},{64,96},{96,64},{128,160},{160,128},{192,224},{224,1... | collective-permute-start | bytes 3145736 | tf_op jit(solution)/shard_map/ppermute | solution.py:32
  114.0 29.0 %all-to-all-start.3 = ((bf16[32,16,896]{2,1,0:T(8,128)(2,1)}), bf16[32,16,896]{2,1,0:T(8,128)(2,1)}, u32[]{:S(2)}, u32[]{:S(2)}) async-start(bf16[32,16,896]{2,1,0:T(8,128)(2,1)} %bitcast.99), calls=%async_computation.3 | async-start | bytes 1835008 | tf_op jit(solution)/shard_map/all_to_all | solution.py:13
  121.6 1.0 copy-start.2
  122.8 9.3 %collective-permute-start.9 = (f16[64,2048]{1,0:T(8,128)(2,1)S(1)}, f16[64,2048]{1,0:T(8,128)(2,1)S(1)}, u32[]{:S(2)}, u32[]{:S(2)}) collective-permute-start(f16[64,2048]{1,0:T(8,128)(2,1)S(1)} %get-tuple-element.25), channel_id=1, source_target_pairs={{0,128},{32,160},{64,192},{96,224},{128,0},{160,32},{192,64},{224,... | collective-permute-start | bytes 786440 | tf_op jit(solution)/shard_map/ppermute | solution.py:28
  124.0 9.4 %collective-permute-start.8 = (f16[64,2048]{1,0:T(8,128)(2,1)S(1)}, f16[64,2048]{1,0:T(8,128)(2,1)S(1)}, u32[]{:S(2)}, u32[]{:S(2)}) collective-permute-start(f16[64,2048]{1,0:T(8,128)(2,1)S(1)} %get-tuple-element.26), channel_id=1, source_target_pairs={{0,192},{32,224},{64,0},{96,32},{128,64},{160,96},{192,128},{224,1... | collective-permute-start | bytes 786440 | tf_op jit(solution)/shard_map/ppermute | solution.py:28
  126.1 8.8 %collective-permute-start.7 = (f16[64,2048]{1,0:T(8,128)(2,1)S(1)}, f16[64,2048]{1,0:T(8,128)(2,1)}, u32[]{:S(2)}, u32[]{:S(2)}) collective-permute-start(f16[64,2048]{1,0:T(8,128)(2,1)S(1)} %get-tuple-element.24), channel_id=1, source_target_pairs={{0,64},{32,96},{64,128},{96,160},{128,192},{160,224},{192,0},{224,... | collective-permute-start | bytes 786440 | tf_op jit(solution)/shard_map/ppermute | solution.py:28
  146.2 2.0 collective-permute-start.10
  149.2 8.1 %collective-permute-start.13 = (f16[64,1024]{1,0:T(8,128)(2,1)}, f16[64,1024]{1,0:T(8,128)(2,1)S(1)}, u32[]{:S(2)}, u32[]{:S(2)}) collective-permute-start(f16[64,1024]{1,0:T(8,128)(2,1)} %get-tuple-element.32), channel_id=1, source_target_pairs={{0,128},{32,160},{64,192},{96,224},{128,0},{160,32},{192,64},{224,... | collective-permute-start | bytes 393224 | tf_op jit(solution)/shard_map/ppermute | solution.py:28
  150.3 7.4 %collective-permute-start.12 = (f16[64,1024]{1,0:T(8,128)(2,1)}, f16[64,1024]{1,0:T(8,128)(2,1)S(1)}, u32[]{:S(2)}, u32[]{:S(2)}) collective-permute-start(f16[64,1024]{1,0:T(8,128)(2,1)} %get-tuple-element.33), channel_id=1, source_target_pairs={{0,192},{32,224},{64,0},{96,32},{128,64},{160,96},{192,128},{224,1... | collective-permute-start | bytes 393224 | tf_op jit(solution)/shard_map/ppermute | solution.py:28
  152.4 7.0 %collective-permute-start.11 = (f16[64,1024]{1,0:T(8,128)(2,1)S(1)}, f16[64,1024]{1,0:T(8,128)(2,1)}, u32[]{:S(2)}, u32[]{:S(2)}) collective-permute-start(f16[64,1024]{1,0:T(8,128)(2,1)S(1)} %get-tuple-element.31), channel_id=1, source_target_pairs={{0,64},{32,96},{64,128},{96,160},{128,192},{160,224},{192,0},{224,... | collective-permute-start | bytes 393224 | tf_op jit(solution)/shard_map/ppermute | solution.py:28
  160.9 15.2 %collective-permute-start.14 = (bf16[64,2176]{1,0:T(8,128)(2,1)S(1)}, bf16[64,2176]{1,0:T(8,128)(2,1)S(1)}, u32[]{:S(2)}, u32[]{:S(2)}) collective-permute-start(bf16[64,2176]{1,0:T(8,128)(2,1)S(1)} %get-tuple-element.36), channel_id=1, source_target_pairs={{0,64},{32,96},{64,128},{96,160},{128,192},{160,224},{192,0},{224,... | collective-permute-start | bytes 835592 | tf_op jit(solution)/shard_map/ppermute | solution.py:28
  161.1 15.1 %collective-permute-start.15 = (bf16[64,2176]{1,0:T(8,128)(2,1)S(1)}, bf16[64,2176]{1,0:T(8,128)(2,1)S(1)}, u32[]{:S(2)}, u32[]{:S(2)}) collective-permute-start(bf16[64,2176]{1,0:T(8,128)(2,1)S(1)} %get-tuple-element.36), channel_id=1, source_target_pairs={{0,192},{32,224},{64,0},{96,32},{128,64},{160,96},{192,128},{224,1... | collective-permute-start | bytes 835592 | tf_op jit(solution)/shard_map/ppermute | solution.py:28
  164.3 11.9 %collective-permute-start.16 = (bf16[64,2176]{1,0:T(8,128)(2,1)S(1)}, bf16[64,2176]{1,0:T(8,128)(2,1)S(1)}, u32[]{:S(2)}, u32[]{:S(2)}) collective-permute-start(bf16[64,2176]{1,0:T(8,128)(2,1)S(1)} %get-tuple-element.36), channel_id=1, source_target_pairs={{0,128},{32,160},{64,192},{96,224},{128,0},{160,32},{192,64},{224,... | collective-permute-start | bytes 835592 | tf_op jit(solution)/shard_map/ppermute | solution.py:28
  176.2 3.0 %collective-permute-start.17 = (bf16[256,2176]{1,0:T(8,128)(2,1)S(1)}, bf16[256,2176]{1,0:T(8,128)(2,1)}, u32[]{:S(2)}, u32[]{:S(2)}) collective-permute-start(bf16[256,2176]{1,0:T(8,128)(2,1)S(1)} %constant_dynamic-update-slice_fusion), channel_id=1, source_target_pairs={{0,32},{32,0},{64,96},{96,64},{128,160},{160,128},{192,224},{224,1... | collective-permute-start | bytes 3342344 | tf_op jit(solution)/shard_map/ppermute | solution.py:32
  180.7 1.5 copy-start.10
Sparse Core Ops, SparseCore 0:
  9.9 41.6 all-gather.1

commit v6 on v4

--- a/solution.py
+++ b/solution.py
@@ -36,7 +36,7 @@
     return lax.dynamic_slice_in_dim(x, index * count, count, axis=0)
 
 
-def ctx_scatter(x):
+def ctx_scatter(x, after=None):
     core = lax.axis_index("ctx") % 2
     chip = lax.axis_index("ctx") // 2
     half_rows = x.shape[0] // 2
@@ -46,11 +46,13 @@
     pair = (
         rows_at(x, core, half_rows).astype(jnp.float32) + other.astype(jnp.float32)
     ).astype(jnp.float16)
+    if after is not None:
+        pair, after = lax.optimization_barrier((pair, after))
     got = [ctx_shift(rows_at(pair, (chip + shift) % 4, own_rows), shift) for shift in (1, 3, 2)]
     own = rows_at(pair, chip, own_rows).astype(jnp.float32)
     for piece in got:
         own = own + piece.astype(jnp.float32)
-    return own
+    return own, after
 
 
 def ctx_gather(own):
@@ -78,7 +80,6 @@
     split = far.shape[0] // 2
     from_down = y_shift(far[:split], 1)
     from_up = y_shift(far[split:], 3)
-    from_down, from_up, per_row = lax.optimization_barrier((from_down, from_up, per_row))
     up = block((y + 1) % NY, per_row)
     up_late = y_shift(up[split:], 1)
     down = block((y + 3) % NY, per_row)
@@ -141,38 +142,41 @@
         jnp.bfloat16
     )
 
+    send_input = jnp.dot(slot_owner, moe_input, preferred_element_type=jnp.float32).astype(
+        jnp.bfloat16
+    )
+    flat_inputs = exchange(send_input, "exp")
+
     scores = logits.astype(jnp.float32)
     local_max = jnp.max(scores, axis=1)
     local_sum = jnp.sum(jnp.exp(scores - local_max[:, None]), axis=1)
+    own_rows = jnp.stack([local_max, local_sum, token_weights, token_ids.astype(jnp.float32)])
+    rows = ctx_gather(jnp.pad(own_rows, ((0, 4), (0, 0))))
+    rows = rows.reshape(2, 4, 8, row_count).transpose(2, 1, 0, 3).reshape(8, seq_length)
+    weights = rows[2]
+    all_ids = rows[3].astype(jnp.int32)
     send_prob = jnp.dot(
-        chosen, probs.reshape(-1).astype(jnp.float32), precision=lax.Precision.HIGHEST
+        chosen.astype(jnp.bfloat16), probs.reshape(-1), preferred_element_type=jnp.float32
     ).reshape(exp_count, capacity)
-    send_input = jnp.dot(slot_owner, moe_input, preferred_element_type=jnp.float32).astype(
-        jnp.bfloat16
-    )
     packed = jnp.concatenate(
         [
-            jnp.broadcast_to(local_max[None], (exp_count, row_count)),
-            jnp.broadcast_to(local_sum[None], (exp_count, row_count)),
+            jnp.broadcast_to(rows[:2].reshape(1, -1), (exp_count, 2 * seq_length)),
             jnp.pad(send_prob, ((0, 0), (0, 128 - capacity))),
         ],
         axis=1,
     )
+    packed, flat_inputs = lax.optimization_barrier((packed, flat_inputs))
     packed = exchange(packed, "exp")
-    all_max = packed[:, :row_count]
+    all_max = packed[:, :seq_length]
     row_max = jnp.max(all_max, axis=0)
-    row_total = jnp.sum(packed[:, row_count : 2 * row_count] * jnp.exp(all_max - row_max), axis=0)
-    flat_prob = packed[:, 2 * row_count : 2 * row_count + capacity].reshape(-1)
-    rows = jnp.concatenate([row_max, row_total, token_weights, token_ids.astype(jnp.float32)])
-    rows = exchange(jnp.broadcast_to(rows[None], (ctx_count, 4 * row_count)), "ctx")
-    rows = rows.reshape(ctx_count, 4, row_count).transpose(1, 0, 2).reshape(4, seq_length)
-    rows, all_logits = lax.optimization_barrier((rows, all_logits))
+    row_total = jnp.sum(packed[:, seq_length : 2 * seq_length] * jnp.exp(all_max - row_max), axis=0)
+    flat_prob = packed[:, 2 * seq_length : 2 * seq_length + capacity].reshape(-1)
 
     gate_w = w_gate[0]
     up_w = w_up[0]
     down_w = w_down[0]
-    row_max, row_total, weights = rows[0], rows[1], rows[2]
-    all_ids = rows[3].astype(jnp.int32)
+    one = 1 - jnp.minimum(lax.axis_index("ctx"), 0)
+    head_weight = lax.optimization_barrier(head_weight * one.astype(jnp.bfloat16))
 
     slab_count = slab_order.shape[0]
     next_ids = jnp.concatenate([all_ids[1:], all_ids[-1:]]).reshape(slab_count, SLAB)
@@ -185,14 +189,16 @@
     columns = jnp.arange(vocab_width, dtype=jnp.int32)[None, :]
     per_row = jnp.stack([row_max, row_total, weighting, local_target.astype(jnp.float32)])
 
-    def upstream_block(q, per_row):
+    def upstream_block(q, per_row, block_logits=None):
         count = seq_length // NY
+        if block_logits is None:
+            block_logits = rows_at(all_logits, q, count)
         top, total, weight, aim = lax.dynamic_slice_in_dim(per_row, q * count, count, axis=1)
         is_target = columns == aim.astype(jnp.int32)[:, None]
         logit_grads = (
             weight[:, None]
             * (
-                jnp.exp(rows_at(all_logits, q, count).astype(jnp.float32) - top[:, None])
+                jnp.exp(block_logits.astype(jnp.float32) - top[:, None])
                 / total[:, None]
                 - is_target.astype(jnp.float32)
             )
@@ -200,11 +206,10 @@
         partial = jnp.dot(logit_grads, head_weight, preferred_element_type=jnp.float32)
         return (partial * 4096.0).astype(jnp.float16)
 
-    far = upstream_block((lax.axis_index("exp") // NZ + 2) % NY, per_row)
-    far, send_input = lax.optimization_barrier((far, send_input))
-    flat_inputs = exchange(send_input, "exp")
-    over_y = ring_sum_over_y(upstream_block, far, per_row)
-    flat_inputs, over_y = lax.optimization_barrier((flat_inputs, over_y))
+    far_index = (lax.axis_index("exp") // NZ + 2) % NY
+    far_logits = lax.optimization_barrier(rows_at(all_logits, far_index, seq_length // NY))
+    far_logits, per_row = lax.optimization_barrier((far_logits, per_row))
+    far = upstream_block(far_index, per_row, far_logits)
     part_both = jnp.concatenate(
         [
             jnp.dot(flat_inputs, weight, preferred_element_type=jnp.float32).astype(jnp.float16)
@@ -212,20 +217,20 @@
         ],
         axis=1,
     )
+    both_sum, far = ctx_scatter(part_both, far)
+    over_y = ring_sum_over_y(upstream_block, far, per_row)
     upstream = exchange_sum(over_y, "exp", Z_GROUPS, NZ) * (1.0 / 4096.0)
     upstream_sent = upstream.astype(jnp.bfloat16)
 
     send_upstream = jnp.dot(slot_owner, upstream_sent, preferred_element_type=jnp.float32).astype(
         jnp.bfloat16
     )
-    send_upstream, part_both = lax.optimization_barrier((send_upstream, part_both))
     flat_upstream = exchange(send_upstream, "exp")
-    both_sum = ctx_scatter(part_both)
     flat_upstream, both_sum = lax.optimization_barrier((flat_upstream, both_sum))
     part_back = lax.dot_general(
         flat_upstream, down_w, CONTRACT_LAST, preferred_element_type=jnp.float32
     )
-    back_sum = ctx_scatter(part_back)
+    back_sum, _ = ctx_scatter(part_back)
 
     hidden = w_gate.shape[2]
     own_count = slot_count // ctx_count

time: 241 us -> 243 us (level)
  blocking collectives: 34 us -> 48.5 us
  starting transfers between devices: 59.7 us -> 49.9 us
  matrix products: 30.7 us -> 23 us
  other arithmetic: 15.4 us -> 17.9 us
    all_to_all x5 -> x3, starting transfers between devices: 37.5 us -> 22.3 us  [exchange(): return lax.all_to_all(x, axis, 0, 0, tiled=True, axis_index_groups=groups)]
    all_to_all x1 -> x2, blocking collectives: 34 us -> 48.5 us  [exchange(): return lax.all_to_all(x, axis, 0, 0, tiled=True, axis_index_groups=groups)]
    all_to_all x5 -> x3, waiting for transfers between devices: 27.2 us -> 39.6 us  [exchange(): return lax.all_to_all(x, axis, 0, 0, tiled=True, axis_index_groups=groups)]
    dot_general x4, matrix products: 16.7 us -> 10.5 us  [upstream_block(): jnp.dot(logit_grads, head_weight, preferred_element_type=jnp.float32)]
    ppermute x9 -> x12, starting transfers between devices: 12.1 us -> 17.8 us  [ctx_shift(): return lax.ppermute(x, 'ctx', [(i, (i + 2 * shift) % 8) for i in range(8)])]
    all_gather x1, waiting for transfers between devices: 5.7 us -> 0.02 us  [local(): all_logits = lax.all_gather(logits, 'ctx', axis=0, tiled=True)]
    mul x0 -> x1, other arithmetic: none -> 4.99 us  [local(): head_weight * one.astype(jnp.bfloat16)]
    ppermute x6, waiting for transfers between devices: 8.66 us -> 5.35 us  [y_shift(): lax.ppermute(x, 'exp', [(i, (i + NZ * shift) % (NY * NZ)) for i in range(...]
  transfers between devices with their start and end apart: 24 -> 26, of which waited for: 15 -> 15; matrix products, arithmetic and copies ran while one was open for 16% -> 13% of each run, Pallas kernels for 0% -> 0%
where the time goes in v6:
time: 243 us; the launch traced here: 242 us
  waiting for transfers between devices  74.3 us (31%)
  starting transfers between devices  49.9 us (21%)
  blocking collectives  48.5 us (20%)
  matrix products  23 us (9%)
  other arithmetic  17.9 us (7%)
  between operations  14.7 us (6%)
  local copies, waits for them, and re-layouts  13.5 us (6%)
    all_to_all x2, blocking collectives, exchange(): return lax.all_to_all(x, axis, 0, 0, tiled=True, axis_index_groups=groups)  48.5 us
    all_to_all x3, waiting for transfers between devices, exchange(): return lax.all_to_all(x, axis, 0, 0, tiled=True, axis_index_groups=groups)  39.6 us
    ppermute x12, waiting for transfers between devices, ctx_shift(): return lax.ppermute(x, 'ctx', [(i, (i + 2 * shift) % 8) for i in range(8)])  23 us
    all_to_all x3, starting transfers between devices, exchange(): return lax.all_to_all(x, axis, 0, 0, tiled=True, axis_index_groups=groups)  22.3 us
    ppermute x12, starting transfers between devices, ctx_shift(): return lax.ppermute(x, 'ctx', [(i, (i + 2 * shift) % 8) for i in range(8)])  17.8 us
    dot_general x4, matrix products, upstream_block(): jnp.dot(logit_grads, head_weight, preferred_element_type=jnp.float32)  10.5 us
    ppermute x6, starting transfers between devices, y_shift(): lax.ppermute(x, 'exp', [(i, (i + NZ * shift) % (NY * NZ)) for i in range(...  9.53 us
    ppermute x4, waiting for transfers between devices, ctx_swap(): return lax.ppermute(x, 'ctx', [(i, i ^ 1) for i in range(8)])  5.61 us
  transfers between devices with their start and end apart: 26, of which 15 were waited for; matrix products, arithmetic and copies ran while one was open for 13% of the time, Pallas kernels for 0%

profile of v6, /device:TPU:32, one launch (start us, length us, event | category | flops | bytes accessed | tf_op | source)
XLA Modules:
  0.0 241.7 jit_solution(15486580974772442333)
XLA Ops:
  8.0 1.3 reduce_max.27
  9.3 1.5 exponential_reduce_fusion
  12.0 1.5 collective-permute-start
  13.5 1.7 collective-permute-start.1
  15.3 1.8 collective-permute-start.2
  19.3 1.4 convolution_convert_fusion.1
  20.7 11.4 %all-to-all-start = ((bf16[32,16,896]{2,1,0:T(8,128)(2,1)}), bf16[32,16,896]{2,1,0:T(8,128)(2,1)S(1)}, u32[]{:S(2)}, u32[]{:S(2)}) async-start(bf16[32,16,896]{2,1,0:T(8,128)(2,1)} %bitcast.10), calls=%async_computation | async-start | bytes 1835008 | tf_op jit(solution)/shard_map/all_to_all | solution.py:13
  32.8 5.0 %broadcast_multiply_fusion = bf16[2560,896]{1,0:T(8,128)(2,1)} fusion(bf16[2560,896]{1,0:T(8,128)(2,1)} %param.12, bf16[]{:T(256)S(6)} %convert_element_type.284), kind=kLoop, calls=%fused_computation.16 | loop fusion | flops 2293760 | bytes 9175042 | tf_op jit(solution)/shard_map/mul | solution.py:179
  39.3 17.8 %all-to-all-done = bf16[32,16,896]{2,1,0:T(8,128)(2,1)S(1)} async-done(((bf16[32,16,896]{2,1,0:T(8,128)(2,1)}), bf16[32,16,896]{2,1,0:T(8,128)(2,1)S(1)}, u32[]{:S(2)}, u32[]{:S(2)}) %all-to-all-start) | async-done | bytes 917536 | tf_op jit(solution)/shard_map/all_to_all | solution.py:13
  57.1 1.3 fusion.15
  58.6 1.3 fusion.12
  63.2 5.1 %all-to-all-start.1 = ((f32[32,1,2176]{2,1,0:T(1,128)}), f32[32,1,2176]{2,1,0:T(1,128)S(1)}, u32[]{:S(2)}, u32[]{:S(2)}) async-start(f32[32,1,2176]{2,1,0:T(1,128)} %all_to_all.39), calls=%async_computation.1 | async-start | bytes 557056 | tf_op jit(solution)/shard_map/all_to_all | solution.py:13
  68.5 13.1 %all-to-all-done.1 = f32[32,1,2176]{2,1,0:T(1,128)S(1)} async-done(((f32[32,1,2176]{2,1,0:T(1,128)}), f32[32,1,2176]{2,1,0:T(1,128)S(1)}, u32[]{:S(2)}, u32[]{:S(2)}) %all-to-all-start.1) | async-done | bytes 278560 | tf_op jit(solution)/shard_map/all_to_all | solution.py:13
  82.3 2.0 add_convert_fusion
  84.3 1.6 constant_dynamic-slice_fusion.11
  86.0 4.9 %fusion.46 = f16[256,896]{1,0:T(8,128)(2,1)S(1)} fusion(bf16[2560,896]{1,0:T(8,128)(2,1)} %broadcast_multiply_fusion, bf16[256,2560]{1,0:T(8,128)(2,1)S(1)} %constant_dynamic-slice_fusion.11, s32[256]{0:T(256)S(1)} %bitcast.131, f32[256]{0:T(256)S(1)} %bitcast.128, f32[256]{0:T(256)S(1)} %bitcast.129, f32[256]{0:T(256)S(1)} %bitcast.130), kind=kOutput, calls=%fused_computation.65 | convolution fusion | flops 1180106752 | bytes 6361088 | tf_op jit(solution)/shard_map/dot_general | solution.py:206
  91.9 2.6 %collective-permute-start.9 = (f16[128,896]{1,0:T(8,128)(2,1)S(1)}, f16[128,896]{1,0:T(8,128)(2,1)S(1)}, u32[]{:S(2)}, u32[]{:S(2)}) collective-permute-start(f16[128,896]{1,0:T(8,128)(2,1)S(1)} %get-tuple-element.43), channel_id=1, source_target_pairs={{0,24},{1,25},{2,26},{3,27},{4,28},{5,29},{6,30},{7,31},{8,0},{9,1... | collective-permute-start | bytes 688136 | tf_op jit(solution)/shard_map/ppermute | solution.py:73
  94.5 1.9 fusion.45
  96.5 1.9 fusion.44
  98.4 2.1 collective-permute-start.8
  100.6 3.8 %collective-permute-start.10 = (f16[128,896]{1,0:T(8,128)(2,1)S(1)}, f16[128,896]{1,0:T(8,128)(2,1)S(1)}, u32[]{:S(2)}, u32[]{:S(2)}) collective-permute-start(f16[128,896]{1,0:T(8,128)(2,1)S(1)} %add_convert_fusion.3), channel_id=1, source_target_pairs={{0,24},{1,25},{2,26},{3,27},{4,28},{5,29},{6,30},{7,31},{8,0},{9,1... | collective-permute-start | bytes 688136 | tf_op jit(solution)/shard_map/ppermute | solution.py:73
  104.5 1.9 fusion.43
  106.4 1.4 collective-permute-done.8
  108.0 3.7 %collective-permute-done.6 = f16[128,896]{1,0:T(8,128)(2,1)S(1)} collective-permute-done((f16[128,896]{1,0:T(8,128)(2,1)S(1)}, f16[128,896]{1,0:T(8,128)(2,1)S(1)}, u32[]{:S(2)}, u32[]{:S(2)}) %collective-permute-start.6) | collective-permute-done | bytes 229408 | tf_op jit(solution)/shard_map/ppermute | solution.py:73
  112.1 14.8 %all_to_all.54 = f16[8,32,896]{2,1,0:T(8,128)(2,1)S(1)} all-to-all(f16[8,32,896]{2,1,0:T(8,128)(2,1)S(1)} %bitcast.97), channel_id=1, replica_groups={{0,1,2,3,4,5,6,7},{8,9,10,11,12,13,14,15},{16,17,18,19,20,21,22,23},{24..., dimensions={0} | all-to-all | bytes 917504 | tf_op jit(solution)/shard_map/all_to_all | solution.py:13
  127.0 1.3 convolution_convert_fusion
  128.3 5.9 %all-to-all-start.3 = ((bf16[32,16,896]{2,1,0:T(8,128)(2,1)}), bf16[32,16,896]{2,1,0:T(8,128)(2,1)}, u32[]{:S(2)}, u32[]{:S(2)}) async-start(bf16[32,16,896]{2,1,0:T(8,128)(2,1)} %bitcast.96), calls=%async_computation.3 | async-start | bytes 1835008 | tf_op jit(solution)/shard_map/all_to_all | solution.py:13
  135.7 2.0 collective-permute-start.13
  137.7 1.7 collective-permute-start.12
  139.4 8.7 %collective-permute-done.11 = f16[64,2048]{1,0:T(8,128)(2,1)} collective-permute-done((f16[64,2048]{1,0:T(8,128)(2,1)}, f16[64,2048]{1,0:T(8,128)(2,1)}, u32[]{:S(2)}, u32[]{:S(2)}) %collective-permute-start.11) | collective-permute-done | bytes 262176 | tf_op jit(solution)/shard_map/ppermute | solution.py:28
  148.6 1.2 convert_add_fusion
  149.8 8.7 %all-to-all-done.3 = bf16[32,16,896]{2,1,0:T(8,128)(2,1)} async-done(((bf16[32,16,896]{2,1,0:T(8,128)(2,1)}), bf16[32,16,896]{2,1,0:T(8,128)(2,1)}, u32[]{:S(2)}, u32[]{:S(2)}) %all-to-all-start.3) | async-done | bytes 917536 | tf_op jit(solution)/shard_map/all_to_all | solution.py:13
  158.6 3.1 %fusion.18 = f16[512,1024]{1,0:T(8,128)(2,1)S(1)} fusion(bf16[512,896]{1,0:T(8,128)(2,1)} %bitcast.36, bf16[1,1024,896]{2,1,0:T(8,128)(2,1)} %param.21), kind=kOutput, calls=%fused_computation.34 | convolution fusion | flops 940048384 | bytes 3801088 | tf_op jit(solution)/shard_map/dot_general | solution.py:230
  161.8 1.9 collective-permute-done.14
  165.3 2.0 collective-permute-start.17
  167.3 1.7 collective-permute-start.16
  169.6 1.3 slice.115
  170.9 1.4 reshape.248
  173.1 1.4 collective-permute-done.15
  175.1 1.1 multiply_convert_fusion.19
  177.7 2.3 collective-permute-start.19
  180.7 5.3 %collective-permute-done.18 = bf16[64,2176]{1,0:T(8,128)(2,1)S(1)} collective-permute-done((bf16[64,2176]{1,0:T(8,128)(2,1)S(1)}, bf16[64,2176]{1,0:T(8,128)(2,1)S(1)}, u32[]{:S(2)}, u32[]{:S(2)}) %collective-permute-start.18) | collective-permute-done | bytes 278560 | tf_op jit(solution)/shard_map/ppermute | solution.py:28
  186.1 5.3 %collective-permute-done.19 = bf16[64,2176]{1,0:T(8,128)(2,1)S(1)} collective-permute-done((bf16[64,2176]{1,0:T(8,128)(2,1)S(1)}, bf16[64,2176]{1,0:T(8,128)(2,1)S(1)}, u32[]{:S(2)}, u32[]{:S(2)}) %collective-permute-start.19) | collective-permute-done | bytes 278560 | tf_op jit(solution)/shard_map/ppermute | solution.py:28
  191.5 1.8 collective-permute-done.20
  193.4 2.7 %collective-permute-done.21 = bf16[256,2176]{1,0:T(8,128)(2,1)S(1)} collective-permute-done((bf16[256,2176]{1,0:T(8,128)(2,1)S(1)}, bf16[256,2176]{1,0:T(8,128)(2,1)S(1)}, u32[]{:S(2)}, u32[]{:S(2)}) %collective-permute-start.21) | collective-permute-done | bytes 1114144 | tf_op jit(solution)/shard_map/ppermute | solution.py:32
  196.3 1.3 fusion.4
  197.8 1.3 add_convert_fusion.1
  199.3 33.6 %all_to_all.55 = bf16[32,16,1024]{2,1,0:T(8,128)(2,1)S(1)} all-to-all(bf16[32,16,1024]{2,1,0:T(8,128)(2,1)S(1)} %bitcast.93), channel_id=1, replica_groups=mesh['ctx'=8,'exp'=32] {'exp'}, dimensions={0} | all-to-all | bytes 2097152 | tf_op jit(solution)/shard_map/all_to_all | solution.py:13
  (146 shorter events, 23.2 us)
Async XLA Ops:
  7.2 49.9 %copy-start = (bf16[1,896,1024]{2,1,0:T(8,128)(2,1)S(1)}, bf16[1,896,1024]{2,1,0:T(8,128)(2,1)}, u32[]{:S(2)}) copy-start(bf16[1,896,1024]{2,1,0:T(8,128)(2,1)} %param.20) | copy-start | bytes 5505028
  7.2 12.1 %copy-start.5 = (bf16[32,896]{1,0:T(8,128)(2,1)S(1)}, bf16[32,896]{1,0:T(8,128)(2,1)}, u32[]{:S(2)}) copy-start(bf16[32,896]{1,0:T(8,128)(2,1)} %param.16) | copy-start | bytes 172036
  7.2 77.1 %all-gather.2.cloned.1.call-start = ((), (), s32[]{:S(2)}) async-start(), calls=%async_computation.5 | async-start | bytes 5898240 | tf_op jit(solution)/shard_map/all_gather | solution.py:126
  9.2 22.8 %copy-start.6 = (bf16[32,8]{0,1:T(8,128)(2,1)S(1)}, bf16[32,8]{0,1:T(8,128)(2,1)}, u32[]{:S(2)}) copy-start(bf16[32,8]{0,1:T(8,128)(2,1)} %param.18) | copy-start | bytes 1540
  9.2 23.0 %copy-start.9 = (s32[16]{0:T(128)S(1)}, s32[16]{0:T(128)}, u32[]{:S(2)}) copy-start(s32[16]{0:T(128)} %param.14) | copy-start | bytes 196
  12.0 25.8 %collective-permute-start = (f32[8,128]{1,0:T(8,128)S(1)}, f32[8,128]{1,0:T(8,128)S(1)}, u32[]{:S(2)}, u32[]{:S(2)}) collective-permute-start(f32[8,128]{1,0:T(8,128)S(1)} %get-tuple-element.66), channel_id=1, source_target_pairs={{0,64},{32,96},{64,128},{96,160},{128,192},{160,224},{192,0},{224,... | collective-permute-start | bytes 12296 | tf_op jit(solution)/shard_map/ppermute | solution.py:28
  13.5 24.3 %collective-permute-start.1 = (f32[8,128]{1,0:T(8,128)S(1)}, f32[8,128]{1,0:T(8,128)S(1)}, u32[]{:S(2)}, u32[]{:S(2)}) collective-permute-start(f32[8,128]{1,0:T(8,128)S(1)} %get-tuple-element.66), channel_id=1, source_target_pairs={{0,192},{32,224},{64,0},{96,32},{128,64},{160,96},{192,128},{224,1... | collective-permute-start | bytes 12296 | tf_op jit(solution)/shard_map/ppermute | solution.py:28
  15.3 22.6 %collective-permute-start.2 = (f32[8,128]{1,0:T(8,128)S(1)}, f32[8,128]{1,0:T(8,128)S(1)}, u32[]{:S(2)}, u32[]{:S(2)}) collective-permute-start(f32[8,128]{1,0:T(8,128)S(1)} %get-tuple-element.66), channel_id=1, source_target_pairs={{0,128},{32,160},{64,192},{96,224},{128,0},{160,32},{192,64},{224,... | collective-permute-start | bytes 12296 | tf_op jit(solution)/shard_map/ppermute | solution.py:28
  20.7 36.4 %all-to-all-start = ((bf16[32,16,896]{2,1,0:T(8,128)(2,1)}), bf16[32,16,896]{2,1,0:T(8,128)(2,1)S(1)}, u32[]{:S(2)}, u32[]{:S(2)}) async-start(bf16[32,16,896]{2,1,0:T(8,128)(2,1)} %bitcast.10), calls=%async_computation | async-start | bytes 1835008 | tf_op jit(solution)/shard_map/all_to_all | solution.py:13
  32.3 5.5 %copy-start.7 = (s32[256]{0:T(256)}, s32[256]{0:T(256)S(1)}, u32[]{:S(2)}) copy-start(s32[256]{0:T(256)S(1)} %multiply_add_fusion.2) | copy-start | bytes 3076
  37.9 1.3 collective-permute-start.3
  57.1 1.5 copy-start.12
  58.6 1.3 copy-start.1
  59.9 1.0 copy-start.2
  60.8 21.5 %collective-permute-start.4 = (f16[256,2048]{1,0:T(8,128)(2,1)S(1)}, f16[256,2048]{1,0:T(8,128)(2,1)}, u32[]{:S(2)}, u32[]{:S(2)}) collective-permute-start(f16[256,2048]{1,0:T(8,128)(2,1)S(1)} %fusion.49), channel_id=1, source_target_pairs={{0,32},{32,0},{64,96},{96,64},{128,160},{160,128},{192,224},{224,1... | collective-permute-start | bytes 3145736 | tf_op jit(solution)/shard_map/ppermute | solution.py:32
  63.2 18.3 %all-to-all-start.1 = ((f32[32,1,2176]{2,1,0:T(1,128)}), f32[32,1,2176]{2,1,0:T(1,128)S(1)}, u32[]{:S(2)}, u32[]{:S(2)}) async-start(f32[32,1,2176]{2,1,0:T(1,128)} %all_to_all.39), calls=%async_computation.1 | async-start | bytes 557056 | tf_op jit(solution)/shard_map/all_to_all | solution.py:13
  81.6 0.7 copy-start.3
  84.3 10.2 %slice-start = ((s8[4587520]{0:T(1024)(128)(4,1)}), s8[4194304]{0:T(1024)(128)(4,1)S(1)}, s32[]{:S(2)}) async-start(s8[4587520]{0:T(1024)(128)(4,1)} %bitcast.91), calls=%async_computation.6 | async-start | bytes 8388608
  84.3 10.2 %slice-start.2 = ((s8[5242880]{0:T(1024)(128)(4,1)}), s8[4194304]{0:T(1024)(128)(4,1)S(1)}, s32[]{:S(2)}) async-start(s8[5242880]{0:T(1024)(128)(4,1)} %bitcast.103), calls=%async_computation.8 | async-start | bytes 8388608
  86.0 8.5 %slice-start.1 = ((s8[4587520]{0:T(1024)(128)(4,1)}), s8[393216]{0:T(1024)(128)(4,1)S(1)}, s32[]{:S(2)}) async-start(s8[4587520]{0:T(1024)(128)(4,1)} %bitcast.91), calls=%async_computation.7 | async-start | bytes 786432
  86.0 8.5 %slice-start.3 = ((s8[5242880]{0:T(1024)(128)(4,1)}), s8[1048576]{0:T(1024)(128)(4,1)S(1)}, s32[]{:S(2)}) async-start(s8[5242880]{0:T(1024)(128)(4,1)} %bitcast.103), calls=%async_computation.9 | async-start | bytes 2097152
  91.0 13.4 %collective-permute-start.5 = (f16[128,896]{1,0:T(8,128)(2,1)S(1)}, f16[128,896]{1,0:T(8,128)(2,1)S(1)}, u32[]{:S(2)}, u32[]{:S(2)}) collective-permute-start(f16[128,896]{1,0:T(8,128)(2,1)S(1)} %get-tuple-element.42), channel_id=1, source_target_pairs={{0,8},{1,9},{2,10},{3,11},{4,12},{5,13},{6,14},{7,15},{8,16},{9,17... | collective-permute-start | bytes 688136 | tf_op jit(solution)/shard_map/ppermute | solution.py:73
  91.9 8.7 %collective-permute-start.9 = (f16[128,896]{1,0:T(8,128)(2,1)S(1)}, f16[128,896]{1,0:T(8,128)(2,1)S(1)}, u32[]{:S(2)}, u32[]{:S(2)}) collective-permute-start(f16[128,896]{1,0:T(8,128)(2,1)S(1)} %get-tuple-element.43), channel_id=1, source_target_pairs={{0,24},{1,25},{2,26},{3,27},{4,28},{5,29},{6,30},{7,31},{8,0},{9,1... | collective-permute-start | bytes 688136 | tf_op jit(solution)/shard_map/ppermute | solution.py:73
  96.4 10.0 %collective-permute-start.7 = (f16[128,896]{1,0:T(8,128)(2,1)S(1)}, f16[128,896]{1,0:T(8,128)(2,1)S(1)}, u32[]{:S(2)}, u32[]{:S(2)}) collective-permute-start(f16[128,896]{1,0:T(8,128)(2,1)S(1)} %slice.111), channel_id=1, source_target_pairs={{0,24},{1,25},{2,26},{3,27},{4,28},{5,29},{6,30},{7,31},{8,0},{9,1... | collective-permute-start | bytes 688136 | tf_op jit(solution)/shard_map/ppermute | solution.py:73
  98.4 9.4 %collective-permute-start.8 = (f16[128,896]{1,0:T(8,128)(2,1)S(1)}, f16[128,896]{1,0:T(8,128)(2,1)S(1)}, u32[]{:S(2)}, u32[]{:S(2)}) collective-permute-start(f16[128,896]{1,0:T(8,128)(2,1)S(1)} %slice.113), channel_id=1, source_target_pairs={{0,8},{1,9},{2,10},{3,11},{4,12},{5,13},{6,14},{7,15},{8,16},{9,17... | collective-permute-start | bytes 688136 | tf_op jit(solution)/shard_map/ppermute | solution.py:73
  100.6 7.4 %collective-permute-start.10 = (f16[128,896]{1,0:T(8,128)(2,1)S(1)}, f16[128,896]{1,0:T(8,128)(2,1)S(1)}, u32[]{:S(2)}, u32[]{:S(2)}) collective-permute-start(f16[128,896]{1,0:T(8,128)(2,1)S(1)} %add_convert_fusion.3), channel_id=1, source_target_pairs={{0,24},{1,25},{2,26},{3,27},{4,28},{5,29},{6,30},{7,31},{8,0},{9,1... | collective-permute-start | bytes 688136 | tf_op jit(solution)/shard_map/ppermute | solution.py:73
  104.5 7.3 %collective-permute-start.6 = (f16[128,896]{1,0:T(8,128)(2,1)S(1)}, f16[128,896]{1,0:T(8,128)(2,1)S(1)}, u32[]{:S(2)}, u32[]{:S(2)}) collective-permute-start(f16[128,896]{1,0:T(8,128)(2,1)S(1)} %add_convert_fusion.4), channel_id=1, source_target_pairs={{0,8},{1,9},{2,10},{3,11},{4,12},{5,13},{6,14},{7,15},{8,16},{9,17... | collective-permute-start | bytes 688136 | tf_op jit(solution)/shard_map/ppermute | solution.py:73
  128.3 30.2 %all-to-all-start.3 = ((bf16[32,16,896]{2,1,0:T(8,128)(2,1)}), bf16[32,16,896]{2,1,0:T(8,128)(2,1)}, u32[]{:S(2)}, u32[]{:S(2)}) async-start(bf16[32,16,896]{2,1,0:T(8,128)(2,1)} %bitcast.96), calls=%async_computation.3 | async-start | bytes 1835008 | tf_op jit(solution)/shard_map/all_to_all | solution.py:13
  135.1 13.1 %collective-permute-start.11 = (f16[64,2048]{1,0:T(8,128)(2,1)}, f16[64,2048]{1,0:T(8,128)(2,1)}, u32[]{:S(2)}, u32[]{:S(2)}) collective-permute-start(f16[64,2048]{1,0:T(8,128)(2,1)} %get-tuple-element.32), channel_id=1, source_target_pairs={{0,64},{32,96},{64,128},{96,160},{128,192},{160,224},{192,0},{224,... | collective-permute-start | bytes 786440 | tf_op jit(solution)/shard_map/ppermute | solution.py:28
  135.7 12.5 %collective-permute-start.13 = (f16[64,2048]{1,0:T(8,128)(2,1)S(1)}, f16[64,2048]{1,0:T(8,128)(2,1)}, u32[]{:S(2)}, u32[]{:S(2)}) collective-permute-start(f16[64,2048]{1,0:T(8,128)(2,1)S(1)} %get-tuple-element.33), channel_id=1, source_target_pairs={{0,128},{32,160},{64,192},{96,224},{128,0},{160,32},{192,64},{224,... | collective-permute-start | bytes 786440 | tf_op jit(solution)/shard_map/ppermute | solution.py:28
  137.7 10.9 %collective-permute-start.12 = (f16[64,2048]{1,0:T(8,128)(2,1)S(1)}, f16[64,2048]{1,0:T(8,128)(2,1)}, u32[]{:S(2)}, u32[]{:S(2)}) collective-permute-start(f16[64,2048]{1,0:T(8,128)(2,1)S(1)} %get-tuple-element.34), channel_id=1, source_target_pairs={{0,192},{32,224},{64,0},{96,32},{128,64},{160,96},{192,128},{224,1... | collective-permute-start | bytes 786440 | tf_op jit(solution)/shard_map/ppermute | solution.py:28
  161.7 2.0 collective-permute-start.14
  164.7 9.8 %collective-permute-start.15 = (f16[64,1024]{1,0:T(8,128)(2,1)}, f16[64,1024]{1,0:T(8,128)(2,1)S(1)}, u32[]{:S(2)}, u32[]{:S(2)}) collective-permute-start(f16[64,1024]{1,0:T(8,128)(2,1)} %get-tuple-element.39), channel_id=1, source_target_pairs={{0,64},{32,96},{64,128},{96,160},{128,192},{160,224},{192,0},{224,... | collective-permute-start | bytes 393224 | tf_op jit(solution)/shard_map/ppermute | solution.py:28
  165.3 9.2 %collective-permute-start.17 = (f16[64,1024]{1,0:T(8,128)(2,1)S(1)}, f16[64,1024]{1,0:T(8,128)(2,1)S(1)}, u32[]{:S(2)}, u32[]{:S(2)}) collective-permute-start(f16[64,1024]{1,0:T(8,128)(2,1)S(1)} %get-tuple-element.40), channel_id=1, source_target_pairs={{0,128},{32,160},{64,192},{96,224},{128,0},{160,32},{192,64},{224,... | collective-permute-start | bytes 393224 | tf_op jit(solution)/shard_map/ppermute | solution.py:28
  167.3 7.8 %collective-permute-start.16 = (f16[64,1024]{1,0:T(8,128)(2,1)S(1)}, f16[64,1024]{1,0:T(8,128)(2,1)}, u32[]{:S(2)}, u32[]{:S(2)}) collective-permute-start(f16[64,1024]{1,0:T(8,128)(2,1)S(1)} %get-tuple-element.41), channel_id=1, source_target_pairs={{0,192},{32,224},{64,0},{96,32},{128,64},{160,96},{192,128},{224,1... | collective-permute-start | bytes 393224 | tf_op jit(solution)/shard_map/ppermute | solution.py:28
  172.3 4.1 %copy-start.10 = (pred[128]{0:T(512)(128)(4,1)S(1)}, pred[128]{0:T(512)(128)(4,1)}, u32[]{:S(2)}) copy-start(pred[128]{0:T(512)(128)(4,1)} %get-tuple-element.72) | copy-start | bytes 388
  172.3 4.2 %copy-start.11 = (pred[128]{0:T(512)(128)(4,1)S(1)}, pred[128]{0:T(512)(128)(4,1)}, u32[]{:S(2)}) copy-start(pred[128]{0:T(512)(128)(4,1)} %get-tuple-element.73) | copy-start | bytes 388
  174.5 0.6 copy-start.4
  176.7 9.4 %collective-permute-start.18 = (bf16[64,2176]{1,0:T(8,128)(2,1)S(1)}, bf16[64,2176]{1,0:T(8,128)(2,1)S(1)}, u32[]{:S(2)}, u32[]{:S(2)}) collective-permute-start(bf16[64,2176]{1,0:T(8,128)(2,1)S(1)} %get-tuple-element.44), channel_id=1, source_target_pairs={{0,64},{32,96},{64,128},{96,160},{128,192},{160,224},{192,0},{224,... | collective-permute-start | bytes 835592 | tf_op jit(solution)/shard_map/ppermute | solution.py:28
  177.7 13.7 %collective-permute-start.19 = (bf16[64,2176]{1,0:T(8,128)(2,1)S(1)}, bf16[64,2176]{1,0:T(8,128)(2,1)S(1)}, u32[]{:S(2)}, u32[]{:S(2)}) collective-permute-start(bf16[64,2176]{1,0:T(8,128)(2,1)S(1)} %get-tuple-element.44), channel_id=1, source_target_pairs={{0,192},{32,224},{64,0},{96,32},{128,64},{160,96},{192,128},{224,1... | collective-permute-start | bytes 835592 | tf_op jit(solution)/shard_map/ppermute | solution.py:28
  180.0 13.2 %collective-permute-start.20 = (bf16[64,2176]{1,0:T(8,128)(2,1)S(1)}, bf16[64,2176]{1,0:T(8,128)(2,1)S(1)}, u32[]{:S(2)}, u32[]{:S(2)}) collective-permute-start(bf16[64,2176]{1,0:T(8,128)(2,1)S(1)} %get-tuple-element.44), channel_id=1, source_target_pairs={{0,128},{32,160},{64,192},{96,224},{128,0},{160,32},{192,64},{224,... | collective-permute-start | bytes 835592 | tf_op jit(solution)/shard_map/ppermute | solution.py:28
  193.3 2.8 %collective-permute-start.21 = (bf16[256,2176]{1,0:T(8,128)(2,1)S(1)}, bf16[256,2176]{1,0:T(8,128)(2,1)S(1)}, u32[]{:S(2)}, u32[]{:S(2)}) collective-permute-start(bf16[256,2176]{1,0:T(8,128)(2,1)S(1)} %constant_dynamic-update-slice_fusion), channel_id=1, source_target_pairs={{0,32},{32,0},{64,96},{96,64},{128,160},{160,128},{192,224},{224,1... | collective-permute-start | bytes 3342344 | tf_op jit(solution)/shard_map/ppermute | solution.py:32
  196.3 1.5 copy-start.13
  199.3 34.6 %copy-start.8 = (s32[256]{0:T(256)S(1)}, s32[256]{0:T(256)}, u32[]{:S(2)}) copy-start(s32[256]{0:T(256)} %copy-done.7) | copy-start | bytes 3076
Sparse Core Ops, SparseCore 0:
  9.9 41.6 all-gather.1

commit v7 on v5

--- a/solution.py
+++ b/solution.py
@@ -127,25 +127,21 @@
     feature_width = moe_input.shape[1]
     capacity = min(token_count, 2 * token_count * route_count // exp_count)
     slot_count = exp_count * capacity
-    route_list = routes.reshape(-1)
-    expert_match = (route_list[:, None] == jnp.arange(exp_count, dtype=jnp.int32)[None, :]).astype(
-        jnp.int32
-    )
-    route_rank = jnp.sum((jnp.cumsum(expert_match, axis=0) - 1) * expert_match, axis=1)
-    slot_of_route = route_list * capacity + route_rank
-    chosen = (jnp.arange(slot_count, dtype=jnp.int32)[:, None] == slot_of_route[None, :]).astype(
-        jnp.float32
-    )
-    slot_owner = jnp.sum(chosen.reshape(slot_count, token_count, route_count), axis=2).astype(
-        jnp.bfloat16
-    )
+    tokens = jnp.arange(token_count, dtype=jnp.int32)
+    experts = jnp.arange(exp_count, dtype=jnp.int32)
+    named = routes.T[None] == experts[:, None, None]
+    named_once = jnp.sum(named.astype(jnp.float32), axis=1)
+    earlier = (tokens[:, None] < tokens[None, :]).astype(jnp.bfloat16)
+    place = jnp.dot(named_once.astype(jnp.bfloat16), earlier, preferred_element_type=jnp.float32)
+    place = jnp.where(named_once > 0, place, -1.0)
+    held = place[:, None, :] == jnp.arange(capacity, dtype=jnp.float32)[None, :, None]
+    slot_owner = held.astype(jnp.bfloat16).reshape(slot_count, token_count)
 
     scores = logits.astype(jnp.float32)
     local_max = jnp.max(scores, axis=1)
     local_sum = jnp.sum(jnp.exp(scores - local_max[:, None]), axis=1)
-    send_prob = jnp.dot(
-        chosen.astype(jnp.bfloat16), probs.reshape(-1), preferred_element_type=jnp.float32
-    ).astype(jnp.bfloat16)
+    expert_prob = jnp.sum(jnp.where(named, probs.astype(jnp.float32).T[None], 0.0), axis=1)
+    send_prob = jnp.sum(jnp.where(held, expert_prob[:, None, :], 0.0), axis=2).astype(jnp.bfloat16)
     send_input = jnp.dot(slot_owner, moe_input, preferred_element_type=jnp.float32).astype(
         jnp.bfloat16
     )
@@ -173,6 +169,7 @@
         (stats[:, 1] + stats[:, 2] + stats[:, 3]) * jnp.exp(all_max - row_max), axis=0
     )
     rows = jnp.concatenate([row_max, row_total, token_weights, token_ids.astype(jnp.float32)])
+    rows, head_weight = lax.optimization_barrier((rows, head_weight))
     rows = exchange(jnp.broadcast_to(rows[None], (ctx_count, 4 * row_count)), "ctx")
     rows = rows.reshape(ctx_count, 4, row_count).transpose(1, 0, 2).reshape(4, seq_length)
     rows, all_logits = lax.optimization_barrier((rows, all_logits))
@@ -263,15 +260,10 @@
         (((0,), (0,)), ((), ())),
         preferred_element_type=jnp.float32,
     )
-    d_prob = jnp.sum(
-        lax.dot_general(
-            back[:, feature_width : feature_width + 2],
-            chosen.astype(jnp.bfloat16),
-            (((0,), (0,)), ((), ())),
-            preferred_element_type=jnp.float32,
-        ),
-        axis=0,
-    ).reshape(token_count, route_count)
+    back_prob = back[:, feature_width : feature_width + 2].astype(jnp.float32)
+    back_prob = (back_prob[:, 0] + back_prob[:, 1]).reshape(exp_count, capacity)
+    token_prob = jnp.sum(jnp.where(held, back_prob[:, :, None], 0.0), axis=1)
+    d_prob = jnp.sum(jnp.where(named, token_prob[:, None, :], 0.0), axis=0).T
     return (d_x, d_prob)
 
 

time: 227 us -> 230 us (1.013)
  starting transfers between devices: 43.2 us -> 46.5 us
    ppermute x9, starting transfers between devices: 9.87 us -> 13.1 us  [ctx_shift(): return lax.ppermute(x, 'ctx', [(i, (i + 2 * shift) % 8) for i in range(8)])]
    unnamed x31 -> x35, local copies, waits for them, and re-layouts: 4.99 us -> 3.54 us
  transfers between devices with their start and end apart: 23 -> 23, of which waited for: 17 -> 18; matrix products, arithmetic and copies ran while one was open for 14% -> 13% of each run, Pallas kernels for 0% -> 0%
where the time goes in v7:
time: 230 us; the launch traced here: 229 us
  waiting for transfers between devices  81.2 us (35%)
  starting transfers between devices  46.5 us (20%)
  blocking collectives  33.6 us (15%)
  other arithmetic  22.6 us (10%)
  matrix products  22.2 us (10%)
  between operations  14.7 us (6%)
  local copies, waits for them, and re-layouts  7.91 us (3%)
    all_to_all x4, waiting for transfers between devices, exchange(): return lax.all_to_all(x, axis, 0, 0, tiled=True, axis_index_groups=groups)  44.1 us
    all_to_all x1, blocking collectives, exchange(): return lax.all_to_all(x, axis, 0, 0, tiled=True, axis_index_groups=groups)  33.6 us
    all_to_all x4, starting transfers between devices, exchange(): return lax.all_to_all(x, axis, 0, 0, tiled=True, axis_index_groups=groups)  25.3 us
    ppermute x9, waiting for transfers between devices, ctx_shift(): return lax.ppermute(x, 'ctx', [(i, (i + 2 * shift) % 8) for i in range(8)])  24.5 us
    ppermute x9, starting transfers between devices, ctx_shift(): return lax.ppermute(x, 'ctx', [(i, (i + 2 * shift) % 8) for i in range(8)])  13.1 us
    dot_general x4, matrix products, upstream_block(): jnp.dot(logit_grads, head_weight, preferred_element_type=jnp.float32)  10.1 us
    ppermute x6, starting transfers between devices, y_shift(): lax.ppermute(x, 'exp', [(i, (i + NZ * shift) % (NY * NZ)) for i in range(...  7.82 us
    ppermute x6, waiting for transfers between devices, y_shift(): lax.ppermute(x, 'exp', [(i, (i + NZ * shift) % (NY * NZ)) for i in range(...  7.11 us
  transfers between devices with their start and end apart: 23, of which 18 were waited for; matrix products, arithmetic and copies ran while one was open for 13% of the time, Pallas kernels for 0%

profile of v7, /device:TPU:32, one launch (start us, length us, event | category | flops | bytes accessed | tf_op | source)
XLA Modules:
  0.0 228.9 jit_solution(7562202717315444410)
XLA Ops:
  10.1 1.3 reduce_max.25
  11.4 1.5 exponential_reduce_fusion
  13.3 1.2 fusion.52
  14.5 11.4 %all-to-all-start = ((bf16[32,16,1024]{2,1,0:T(8,128)(2,1)}), bf16[32,16,1024]{2,1,0:T(8,128)(2,1)S(1)}, u32[]{:S(2)}, u32[]{:S(2)}) async-start(bf16[32,16,1024]{2,1,0:T(8,128)(2,1)} %fusion.52), calls=%async_computation | async-start | bytes 2097152 | tf_op jit(solution)/shard_map/all_to_all | solution.py:13
  26.3 28.2 %all-to-all-done = bf16[32,16,1024]{2,1,0:T(8,128)(2,1)S(1)} async-done(((bf16[32,16,1024]{2,1,0:T(8,128)(2,1)}), bf16[32,16,1024]{2,1,0:T(8,128)(2,1)S(1)}, u32[]{:S(2)}, u32[]{:S(2)}) %all-to-all-start) | async-done | bytes 1048608 | tf_op jit(solution)/shard_map/all_to_all | solution.py:13
  55.8 4.3 %all-to-all-start.1 = ((f32[8,1,512]{2,1,0:T(1,128)}), f32[8,1,512]{2,1,0:T(1,128)S(1)}, u32[]{:S(2)}, u32[]{:S(2)}) async-start(f32[8,1,512]{2,1,0:T(1,128)} %broadcast_in_dim.156), calls=%async_computation.1 | async-start | bytes 32768 | tf_op jit(solution)/shard_map/all_to_all | solution.py:13
  60.1 4.8 %broadcast_multiply_fusion = bf16[2560,896]{1,0:T(8,128)(2,1)} fusion(bf16[2560,896]{1,0:T(8,128)(2,1)} %param.12, bf16[]{:T(256)S(6)} %convert_element_type.286), kind=kLoop, calls=%fused_computation.16 | loop fusion | flops 2293760 | bytes 9175042 | tf_op jit(solution)/shard_map/mul | solution.py:184
  67.8 4.6 %fusion.50 = f16[256,896]{1,0:T(8,128)(2,1)S(1)} fusion(bf16[2560,896]{1,0:T(8,128)(2,1)} %broadcast_multiply_fusion, s32[256]{0:T(256)S(1)} %bitcast.121, f32[256]{0:T(256)S(1)} %bitcast.118, f32[256]{0:T(256)S(1)} %bitcast.119, bf16[1024,2560]{1,0:T(8,128)(2,1)} %all-gather.2.cloned.1.call-done, s32[]{:T(128)S(6)} %select_n.174, f32[256]{0:T(256)S(1)} %bitcast.120), kind=kOutput, calls=%fused_computation.71 | convolution fusion | flops 1180106752 | bytes 6361092 | tf_op jit(solution)/shard_map/dot_general | solution.py:209
  72.5 1.2 collective-permute-start.2
  73.8 1.8 fusion.49
  76.6 2.4 %collective-permute-start.4 = (f16[128,896]{1,0:T(8,128)(2,1)S(1)}, f16[128,896]{1,0:T(8,128)(2,1)S(1)}, u32[]{:S(2)}, u32[]{:S(2)}) collective-permute-start(f16[128,896]{1,0:T(8,128)(2,1)S(1)} %get-tuple-element.35), channel_id=1, source_target_pairs={{0,24},{1,25},{2,26},{3,27},{4,28},{5,29},{6,30},{7,31},{8,0},{9,1... | collective-permute-start | bytes 688136 | tf_op jit(solution)/shard_map/ppermute | solution.py:71
  79.0 1.8 fusion.48
  81.2 1.8 fusion.47
  83.0 1.7 collective-permute-done
  85.6 2.7 %collective-permute-start.5 = (f16[128,896]{1,0:T(8,128)(2,1)S(1)}, f16[128,896]{1,0:T(8,128)(2,1)S(1)}, u32[]{:S(2)}, u32[]{:S(2)}) collective-permute-start(f16[128,896]{1,0:T(8,128)(2,1)S(1)} %add_convert_fusion.3), channel_id=1, source_target_pairs={{0,24},{1,25},{2,26},{3,27},{4,28},{5,29},{6,30},{7,31},{8,0},{9,1... | collective-permute-start | bytes 688136 | tf_op jit(solution)/shard_map/ppermute | solution.py:71
  88.3 1.3 fusion.15
  89.6 1.3 collective-permute-done.3
  90.9 3.7 %collective-permute-done.1 = f16[128,896]{1,0:T(8,128)(2,1)S(1)} collective-permute-done((f16[128,896]{1,0:T(8,128)(2,1)S(1)}, f16[128,896]{1,0:T(8,128)(2,1)S(1)}, u32[]{:S(2)}, u32[]{:S(2)}) %collective-permute-start.1) | collective-permute-done | bytes 229408 | tf_op jit(solution)/shard_map/ppermute | solution.py:71
  95.6 4.0 %all-to-all-start.2 = ((f16[8,32,896]{2,1,0:T(8,128)(2,1)}), f16[8,32,896]{2,1,0:T(8,128)(2,1)S(1)}, u32[]{:S(2)}, u32[]{:S(2)}) async-start(f16[8,32,896]{2,1,0:T(8,128)(2,1)} %bitcast.32), calls=%async_computation.2 | async-start | bytes 917504 | tf_op jit(solution)/shard_map/all_to_all | solution.py:13
  99.6 2.4 %fusion.18 = f16[512,1024]{1,0:T(8,128)(2,1)S(1)} fusion(bf16[512,896]{1,0:T(8,128)(2,1)} %slice.140, bf16[1,896,1024]{2,1,0:T(8,128)(2,1)S(1)} %copy-done), kind=kOutput, calls=%fused_computation.38 | convolution fusion | flops 940048384 | bytes 3801088 | tf_op jit(solution)/shard_map/dot_general | solution.py:217
  103.1 1.2 fusion.55
  104.3 9.0 %all-to-all-done.2 = f16[8,32,896]{2,1,0:T(8,128)(2,1)S(1)} async-done(((f16[8,32,896]{2,1,0:T(8,128)(2,1)}), f16[8,32,896]{2,1,0:T(8,128)(2,1)S(1)}, u32[]{:S(2)}, u32[]{:S(2)}) %all-to-all-start.2) | async-done | bytes 458784 | tf_op jit(solution)/shard_map/all_to_all | solution.py:13
  113.4 1.3 convolution_convert_fusion
  114.7 5.7 %all-to-all-start.3 = ((bf16[32,16,896]{2,1,0:T(8,128)(2,1)}), bf16[32,16,896]{2,1,0:T(8,128)(2,1)}, u32[]{:S(2)}, u32[]{:S(2)}) async-start(bf16[32,16,896]{2,1,0:T(8,128)(2,1)} %bitcast.91), calls=%async_computation.3 | async-start | bytes 1835008 | tf_op jit(solution)/shard_map/all_to_all | solution.py:13
  120.5 1.8 add_convert_fusion
  123.5 2.9 %collective-permute-start.9 = (f16[64,2048]{1,0:T(8,128)(2,1)S(1)}, f16[64,2048]{1,0:T(8,128)(2,1)S(1)}, u32[]{:S(2)}, u32[]{:S(2)}) collective-permute-start(f16[64,2048]{1,0:T(8,128)(2,1)S(1)} %get-tuple-element.25), channel_id=1, source_target_pairs={{0,128},{32,160},{64,192},{96,224},{128,0},{160,32},{192,64},{224,... | collective-permute-start | bytes 786440 | tf_op jit(solution)/shard_map/ppermute | solution.py:28
  126.3 1.2 collective-permute-start.8
  128.4 5.1 %collective-permute-done.9 = f16[64,2048]{1,0:T(8,128)(2,1)S(1)} collective-permute-done((f16[64,2048]{1,0:T(8,128)(2,1)S(1)}, f16[64,2048]{1,0:T(8,128)(2,1)S(1)}, u32[]{:S(2)}, u32[]{:S(2)}) %collective-permute-start.9) | collective-permute-done | bytes 262176 | tf_op jit(solution)/shard_map/ppermute | solution.py:28
  133.5 1.9 collective-permute-done.8
  136.4 1.2 convert_add_fusion
  137.5 7.0 %all-to-all-done.3 = bf16[32,16,896]{2,1,0:T(8,128)(2,1)} async-done(((bf16[32,16,896]{2,1,0:T(8,128)(2,1)}), bf16[32,16,896]{2,1,0:T(8,128)(2,1)}, u32[]{:S(2)}, u32[]{:S(2)}) %all-to-all-start.3) | async-done | bytes 917536 | tf_op jit(solution)/shard_map/all_to_all | solution.py:13
  144.5 3.1 %fusion.21 = f16[512,1024]{1,0:T(8,128)(2,1)S(1)} fusion(bf16[512,896]{1,0:T(8,128)(2,1)} %bitcast.34, bf16[1,1024,896]{2,1,0:T(8,128)(2,1)} %param.21), kind=kOutput, calls=%fused_computation.39 | convolution fusion | flops 940048384 | bytes 3801088 | tf_op jit(solution)/shard_map/dot_general | solution.py:231
  147.8 1.9 collective-permute-done.10
  150.7 2.1 collective-permute-start.13
  152.8 1.2 collective-permute-start.12
  155.9 2.9 %collective-permute-done.13 = f16[64,1024]{1,0:T(8,128)(2,1)S(1)} collective-permute-done((f16[64,1024]{1,0:T(8,128)(2,1)}, f16[64,1024]{1,0:T(8,128)(2,1)S(1)}, u32[]{:S(2)}, u32[]{:S(2)}) %collective-permute-start.13) | collective-permute-done | bytes 131104 | tf_op jit(solution)/shard_map/ppermute | solution.py:28
  158.7 1.1 collective-permute-done.12
  160.9 1.2 multiply_convert_fusion.19
  162.6 1.1 collective-permute-start.14
  163.7 2.2 collective-permute-start.15
  166.7 5.1 %collective-permute-done.14 = bf16[64,2176]{1,0:T(8,128)(2,1)S(1)} collective-permute-done((bf16[64,2176]{1,0:T(8,128)(2,1)S(1)}, bf16[64,2176]{1,0:T(8,128)(2,1)S(1)}, u32[]{:S(2)}, u32[]{:S(2)}) %collective-permute-start.14) | collective-permute-done | bytes 278560 | tf_op jit(solution)/shard_map/ppermute | solution.py:28
  171.8 1.4 collective-permute-done.15
  173.3 5.6 %collective-permute-done.16 = bf16[64,2176]{1,0:T(8,128)(2,1)S(1)} collective-permute-done((bf16[64,2176]{1,0:T(8,128)(2,1)S(1)}, bf16[64,2176]{1,0:T(8,128)(2,1)S(1)}, u32[]{:S(2)}, u32[]{:S(2)}) %collective-permute-start.16) | collective-permute-done | bytes 278560 | tf_op jit(solution)/shard_map/ppermute | solution.py:28
  179.0 2.9 %collective-permute-done.17 = bf16[256,2176]{1,0:T(8,128)(2,1)} collective-permute-done((bf16[256,2176]{1,0:T(8,128)(2,1)S(1)}, bf16[256,2176]{1,0:T(8,128)(2,1)}, u32[]{:S(2)}, u32[]{:S(2)}) %collective-permute-start.17) | collective-permute-done | bytes 1114144 | tf_op jit(solution)/shard_map/ppermute | solution.py:32
  181.8 1.4 broadcast_select_fusion.1
  183.3 1.3 fusion.7
  184.8 1.3 add_convert_fusion.1
  186.2 33.6 %all_to_all.45 = bf16[32,16,1024]{2,1,0:T(8,128)(2,1)S(1)} all-to-all(bf16[32,16,1024]{2,1,0:T(8,128)(2,1)S(1)} %bitcast.90), channel_id=1, replica_groups=mesh['ctx'=8,'exp'=32] {'exp'}, dimensions={0} | all-to-all | bytes 2097152 | tf_op jit(solution)/shard_map/all_to_all | solution.py:13
  (122 shorter events, 23.1 us)
Async XLA Ops:
  7.2 92.5 %copy-start = (bf16[1,896,1024]{2,1,0:T(8,128)(2,1)S(1)}, bf16[1,896,1024]{2,1,0:T(8,128)(2,1)}, u32[]{:S(2)}) copy-start(bf16[1,896,1024]{2,1,0:T(8,128)(2,1)} %param.20) | copy-start | bytes 5505028
  7.2 5.7 %copy-start.7 = (bf16[32,896]{1,0:T(8,128)(2,1)S(1)}, bf16[32,896]{1,0:T(8,128)(2,1)}, u32[]{:S(2)}) copy-start(bf16[32,896]{1,0:T(8,128)(2,1)} %param.16) | copy-start | bytes 172036
  7.2 58.8 %all-gather.2.cloned.1.call-start = ((), (), s32[]{:S(2)}) async-start(), calls=%async_computation.5 | async-start | bytes 5898240 | tf_op jit(solution)/shard_map/all_gather | solution.py:124
  13.3 12.7 %copy-start.14 = (s32[128]{0:T(128)S(1)}, s32[128]{0:T(128)}, u32[]{:S(2)}) copy-start(s32[128]{0:T(128)} %param.13) | copy-start | bytes 1540
  13.3 12.7 %copy-start.9 = (s32[16]{0:T(128)S(1)}, s32[16]{0:T(128)}, u32[]{:S(2)}) copy-start(s32[16]{0:T(128)} %param.14) | copy-start | bytes 196
  13.3 41.9 %copy-start.10 = (f32[128]{0:T(128)S(1)}, f32[128]{0:T(128)}, u32[]{:S(2)}) copy-start(f32[128]{0:T(128)} %param.15) | copy-start | bytes 1540
  14.5 39.9 %all-to-all-start = ((bf16[32,16,1024]{2,1,0:T(8,128)(2,1)}), bf16[32,16,1024]{2,1,0:T(8,128)(2,1)S(1)}, u32[]{:S(2)}, u32[]{:S(2)}) async-start(bf16[32,16,1024]{2,1,0:T(8,128)(2,1)} %fusion.52), calls=%async_computation | async-start | bytes 2097152 | tf_op jit(solution)/shard_map/all_to_all | solution.py:13
  54.5 0.7 copy-start.4
  55.8 10.2 %all-to-all-start.1 = ((f32[8,1,512]{2,1,0:T(1,128)}), f32[8,1,512]{2,1,0:T(1,128)S(1)}, u32[]{:S(2)}, u32[]{:S(2)}) async-start(f32[8,1,512]{2,1,0:T(1,128)} %broadcast_in_dim.156), calls=%async_computation.1 | async-start | bytes 32768 | tf_op jit(solution)/shard_map/all_to_all | solution.py:13
  64.9 8.8 %slice-start = ((s8[4587520]{0:T(1024)(128)(4,1)}), s8[393216]{0:T(1024)(128)(4,1)S(1)}, s32[]{:S(2)}) async-start(s8[4587520]{0:T(1024)(128)(4,1)} %bitcast.84), calls=%async_computation.6 | async-start | bytes 786432
  67.8 6.0 %slice-start.1 = ((s8[4587520]{0:T(1024)(128)(4,1)}), s8[4194304]{0:T(1024)(128)(4,1)S(1)}, s32[]{:S(2)}) async-start(s8[4587520]{0:T(1024)(128)(4,1)} %bitcast.84), calls=%async_computation.7 | async-start | bytes 8388608
  67.8 6.0 %copy-start.11 = (bf16[1024,2560]{1,0:T(8,128)(2,1)S(1)}, bf16[1024,2560]{1,0:T(8,128)(2,1)}, u32[]{:S(2)}) copy-start(bf16[1024,2560]{1,0:T(8,128)(2,1)} %all-gather.2.cloned.1.call-done) | copy-start | bytes 15728644
  72.5 17.0 %collective-permute-start.2 = (f16[128,896]{1,0:T(8,128)(2,1)S(1)}, f16[128,896]{1,0:T(8,128)(2,1)S(1)}, u32[]{:S(2)}, u32[]{:S(2)}) collective-permute-start(f16[128,896]{1,0:T(8,128)(2,1)S(1)} %slice.141), channel_id=1, source_target_pairs={{0,24},{1,25},{2,26},{3,27},{4,28},{5,29},{6,30},{7,31},{8,0},{9,1... | collective-permute-start | bytes 688136 | tf_op jit(solution)/shard_map/ppermute | solution.py:71
  75.7 9.1 %collective-permute-start = (f16[128,896]{1,0:T(8,128)(2,1)S(1)}, f16[128,896]{1,0:T(8,128)(2,1)S(1)}, u32[]{:S(2)}, u32[]{:S(2)}) collective-permute-start(f16[128,896]{1,0:T(8,128)(2,1)S(1)} %get-tuple-element.34), channel_id=1, source_target_pairs={{0,8},{1,9},{2,10},{3,11},{4,12},{5,13},{6,14},{7,15},{8,16},{9,17... | collective-permute-start | bytes 688136 | tf_op jit(solution)/shard_map/ppermute | solution.py:71
  76.6 8.9 %collective-permute-start.4 = (f16[128,896]{1,0:T(8,128)(2,1)S(1)}, f16[128,896]{1,0:T(8,128)(2,1)S(1)}, u32[]{:S(2)}, u32[]{:S(2)}) collective-permute-start(f16[128,896]{1,0:T(8,128)(2,1)S(1)} %get-tuple-element.35), channel_id=1, source_target_pairs={{0,24},{1,25},{2,26},{3,27},{4,28},{5,29},{6,30},{7,31},{8,0},{9,1... | collective-permute-start | bytes 688136 | tf_op jit(solution)/shard_map/ppermute | solution.py:71
  80.9 10.0 %collective-permute-start.3 = (f16[128,896]{1,0:T(8,128)(2,1)S(1)}, f16[128,896]{1,0:T(8,128)(2,1)S(1)}, u32[]{:S(2)}, u32[]{:S(2)}) collective-permute-start(f16[128,896]{1,0:T(8,128)(2,1)S(1)} %slice.143), channel_id=1, source_target_pairs={{0,8},{1,9},{2,10},{3,11},{4,12},{5,13},{6,14},{7,15},{8,16},{9,17... | collective-permute-start | bytes 688136 | tf_op jit(solution)/shard_map/ppermute | solution.py:71
  81.2 7.1 %copy-start.3 = (bf16[512,896]{1,0:T(8,128)(2,1)S(1)}, bf16[512,896]{1,0:T(8,128)(2,1)}, u32[]{:S(2)}) copy-start(bf16[512,896]{1,0:T(8,128)(2,1)} %slice.140) | copy-start | bytes 2752516
  81.2 7.1 %copy-start.12 = (bf16[1,896,1024]{2,1,0:T(8,128)(2,1)S(1)}, bf16[1,896,1024]{2,1,0:T(8,128)(2,1)}, u32[]{:S(2)}) copy-start(bf16[1,896,1024]{2,1,0:T(8,128)(2,1)} %param.19) | copy-start | bytes 5505028
  84.8 9.7 %collective-permute-start.1 = (f16[128,896]{1,0:T(8,128)(2,1)S(1)}, f16[128,896]{1,0:T(8,128)(2,1)S(1)}, u32[]{:S(2)}, u32[]{:S(2)}) collective-permute-start(f16[128,896]{1,0:T(8,128)(2,1)S(1)} %add_convert_fusion.4), channel_id=1, source_target_pairs={{0,8},{1,9},{2,10},{3,11},{4,12},{5,13},{6,14},{7,15},{8,16},{9,17... | collective-permute-start | bytes 688136 | tf_op jit(solution)/shard_map/ppermute | solution.py:71
  85.6 8.9 %collective-permute-start.5 = (f16[128,896]{1,0:T(8,128)(2,1)S(1)}, f16[128,896]{1,0:T(8,128)(2,1)S(1)}, u32[]{:S(2)}, u32[]{:S(2)}) collective-permute-start(f16[128,896]{1,0:T(8,128)(2,1)S(1)} %add_convert_fusion.3), channel_id=1, source_target_pairs={{0,24},{1,25},{2,26},{3,27},{4,28},{5,29},{6,30},{7,31},{8,0},{9,1... | collective-permute-start | bytes 688136 | tf_op jit(solution)/shard_map/ppermute | solution.py:71
  95.6 17.7 %all-to-all-start.2 = ((f16[8,32,896]{2,1,0:T(8,128)(2,1)}), f16[8,32,896]{2,1,0:T(8,128)(2,1)S(1)}, u32[]{:S(2)}, u32[]{:S(2)}) async-start(f16[8,32,896]{2,1,0:T(8,128)(2,1)} %bitcast.32), calls=%async_computation.2 | async-start | bytes 917504 | tf_op jit(solution)/shard_map/all_to_all | solution.py:13
  102.1 1.0 copy-start.1
  104.3 16.2 %collective-permute-start.6 = (f16[256,2048]{1,0:T(8,128)(2,1)}, f16[256,2048]{1,0:T(8,128)(2,1)}, u32[]{:S(2)}, u32[]{:S(2)}) collective-permute-start(f16[256,2048]{1,0:T(8,128)(2,1)} %fusion.55), channel_id=1, source_target_pairs={{0,32},{32,0},{64,96},{96,64},{128,160},{160,128},{192,224},{224,1... | collective-permute-start | bytes 3145736 | tf_op jit(solution)/shard_map/ppermute | solution.py:32
  114.7 29.8 %all-to-all-start.3 = ((bf16[32,16,896]{2,1,0:T(8,128)(2,1)}), bf16[32,16,896]{2,1,0:T(8,128)(2,1)}, u32[]{:S(2)}, u32[]{:S(2)}) async-start(bf16[32,16,896]{2,1,0:T(8,128)(2,1)} %bitcast.91), calls=%async_computation.3 | async-start | bytes 1835008 | tf_op jit(solution)/shard_map/all_to_all | solution.py:13
  122.3 1.0 copy-start.2
  123.5 10.0 %collective-permute-start.9 = (f16[64,2048]{1,0:T(8,128)(2,1)S(1)}, f16[64,2048]{1,0:T(8,128)(2,1)S(1)}, u32[]{:S(2)}, u32[]{:S(2)}) collective-permute-start(f16[64,2048]{1,0:T(8,128)(2,1)S(1)} %get-tuple-element.25), channel_id=1, source_target_pairs={{0,128},{32,160},{64,192},{96,224},{128,0},{160,32},{192,64},{224,... | collective-permute-start | bytes 786440 | tf_op jit(solution)/shard_map/ppermute | solution.py:28
  126.3 9.1 %collective-permute-start.8 = (f16[64,2048]{1,0:T(8,128)(2,1)S(1)}, f16[64,2048]{1,0:T(8,128)(2,1)S(1)}, u32[]{:S(2)}, u32[]{:S(2)}) collective-permute-start(f16[64,2048]{1,0:T(8,128)(2,1)S(1)} %get-tuple-element.26), channel_id=1, source_target_pairs={{0,192},{32,224},{64,0},{96,32},{128,64},{160,96},{192,128},{224,1... | collective-permute-start | bytes 786440 | tf_op jit(solution)/shard_map/ppermute | solution.py:28
  127.5 8.8 %collective-permute-start.7 = (f16[64,2048]{1,0:T(8,128)(2,1)S(1)}, f16[64,2048]{1,0:T(8,128)(2,1)}, u32[]{:S(2)}, u32[]{:S(2)}) collective-permute-start(f16[64,2048]{1,0:T(8,128)(2,1)S(1)} %get-tuple-element.24), channel_id=1, source_target_pairs={{0,64},{32,96},{64,128},{96,160},{128,192},{160,224},{192,0},{224,... | collective-permute-start | bytes 786440 | tf_op jit(solution)/shard_map/ppermute | solution.py:28
  147.7 2.0 collective-permute-start.10
  150.7 8.1 %collective-permute-start.13 = (f16[64,1024]{1,0:T(8,128)(2,1)}, f16[64,1024]{1,0:T(8,128)(2,1)S(1)}, u32[]{:S(2)}, u32[]{:S(2)}) collective-permute-start(f16[64,1024]{1,0:T(8,128)(2,1)} %get-tuple-element.32), channel_id=1, source_target_pairs={{0,128},{32,160},{64,192},{96,224},{128,0},{160,32},{192,64},{224,... | collective-permute-start | bytes 393224 | tf_op jit(solution)/shard_map/ppermute | solution.py:28
  152.8 7.1 %collective-permute-start.12 = (f16[64,1024]{1,0:T(8,128)(2,1)}, f16[64,1024]{1,0:T(8,128)(2,1)S(1)}, u32[]{:S(2)}, u32[]{:S(2)}) collective-permute-start(f16[64,1024]{1,0:T(8,128)(2,1)} %get-tuple-element.33), channel_id=1, source_target_pairs={{0,192},{32,224},{64,0},{96,32},{128,64},{160,96},{192,128},{224,1... | collective-permute-start | bytes 393224 | tf_op jit(solution)/shard_map/ppermute | solution.py:28
  153.9 7.0 %collective-permute-start.11 = (f16[64,1024]{1,0:T(8,128)(2,1)S(1)}, f16[64,1024]{1,0:T(8,128)(2,1)}, u32[]{:S(2)}, u32[]{:S(2)}) collective-permute-start(f16[64,1024]{1,0:T(8,128)(2,1)S(1)} %get-tuple-element.31), channel_id=1, source_target_pairs={{0,64},{32,96},{64,128},{96,160},{128,192},{160,224},{192,0},{224,... | collective-permute-start | bytes 393224 | tf_op jit(solution)/shard_map/ppermute | solution.py:28
  158.7 1.1 copy-start.5
  159.8 0.7 copy-start.6
  162.6 9.2 %collective-permute-start.14 = (bf16[64,2176]{1,0:T(8,128)(2,1)S(1)}, bf16[64,2176]{1,0:T(8,128)(2,1)S(1)}, u32[]{:S(2)}, u32[]{:S(2)}) collective-permute-start(bf16[64,2176]{1,0:T(8,128)(2,1)S(1)} %get-tuple-element.36), channel_id=1, source_target_pairs={{0,64},{32,96},{64,128},{96,160},{128,192},{160,224},{192,0},{224,... | collective-permute-start | bytes 835592 | tf_op jit(solution)/shard_map/ppermute | solution.py:28
  163.7 9.5 %collective-permute-start.15 = (bf16[64,2176]{1,0:T(8,128)(2,1)S(1)}, bf16[64,2176]{1,0:T(8,128)(2,1)S(1)}, u32[]{:S(2)}, u32[]{:S(2)}) collective-permute-start(bf16[64,2176]{1,0:T(8,128)(2,1)S(1)} %get-tuple-element.36), channel_id=1, source_target_pairs={{0,192},{32,224},{64,0},{96,32},{128,64},{160,96},{192,128},{224,1... | collective-permute-start | bytes 835592 | tf_op jit(solution)/shard_map/ppermute | solution.py:28
  165.9 13.0 %collective-permute-start.16 = (bf16[64,2176]{1,0:T(8,128)(2,1)S(1)}, bf16[64,2176]{1,0:T(8,128)(2,1)S(1)}, u32[]{:S(2)}, u32[]{:S(2)}) collective-permute-start(bf16[64,2176]{1,0:T(8,128)(2,1)S(1)} %get-tuple-element.36), channel_id=1, source_target_pairs={{0,128},{32,160},{64,192},{96,224},{128,0},{160,32},{192,64},{224,... | collective-permute-start | bytes 835592 | tf_op jit(solution)/shard_map/ppermute | solution.py:28
  178.9 3.0 %collective-permute-start.17 = (bf16[256,2176]{1,0:T(8,128)(2,1)S(1)}, bf16[256,2176]{1,0:T(8,128)(2,1)}, u32[]{:S(2)}, u32[]{:S(2)}) collective-permute-start(bf16[256,2176]{1,0:T(8,128)(2,1)S(1)} %constant_dynamic-update-slice_fusion), channel_id=1, source_target_pairs={{0,32},{32,0},{64,96},{96,64},{128,160},{160,128},{192,224},{224,1... | collective-permute-start | bytes 3342344 | tf_op jit(solution)/shard_map/ppermute | solution.py:32
  183.3 1.5 copy-start.13
  186.2 35.1 %copy-start.8 = (s32[32,8]{0,1:T(8,128)S(1)}, s32[32,8]{0,1:T(8,128)}, u32[]{:S(2)}) copy-start(s32[32,8]{0,1:T(8,128)} %param.17) | copy-start | bytes 3076
Sparse Core Ops, SparseCore 0:
  9.9 41.6 all-gather.1

commit v8 on v7

--- a/solution.py
+++ b/solution.py
@@ -168,8 +168,12 @@
     row_total = jnp.sum(
         (stats[:, 1] + stats[:, 2] + stats[:, 3]) * jnp.exp(all_max - row_max), axis=0
     )
-    rows = jnp.concatenate([row_max, row_total, token_weights, token_ids.astype(jnp.float32)])
-    rows, head_weight = lax.optimization_barrier((rows, head_weight))
+    own_ids = token_ids.astype(jnp.float32)
+    later_id = lax.ppermute(
+        own_ids[:1], "ctx", [((i + 1) % ctx_count, i) for i in range(ctx_count)]
+    )
+    own_next = jnp.concatenate([own_ids[1:], later_id])
+    rows = jnp.concatenate([row_max, row_total, token_weights, own_next])
     rows = exchange(jnp.broadcast_to(rows[None], (ctx_count, 4 * row_count)), "ctx")
     rows = rows.reshape(ctx_count, 4, row_count).transpose(1, 0, 2).reshape(4, seq_length)
     rows, all_logits = lax.optimization_barrier((rows, all_logits))
@@ -178,13 +182,13 @@
     up_w = w_up[0]
     down_w = w_down[0]
     row_max, row_total, weights = rows[0], rows[1], rows[2]
-    all_ids = rows[3].astype(jnp.int32)
+    all_next = rows[3].astype(jnp.int32)
 
     one = 1 - jnp.minimum(lax.axis_index("ctx"), 0)
     head_weight = lax.optimization_barrier(head_weight * one.astype(jnp.bfloat16))
 
     slab_count = slab_order.shape[0]
-    next_ids = jnp.concatenate([all_ids[1:], all_ids[-1:]]).reshape(slab_count, SLAB)
+    next_ids = all_next.reshape(slab_count, SLAB)
     slab_match = slab_order[:, None] == jnp.arange(slab_count, dtype=jnp.int32)[None, :]
     target = jnp.sum(jnp.where(slab_match[:, :, None], next_ids[None], 0), axis=1).reshape(-1)
     position = (slab_order[:, None] * SLAB + jnp.arange(SLAB, dtype=jnp.int32)).reshape(-1)

time: 230 us -> 225 us (0.978)
  waiting for transfers between devices: 81.2 us -> 78.6 us
    all_to_all x4, waiting for transfers between devices: 44.1 us -> 41.2 us  [exchange(): return lax.all_to_all(x, axis, 0, 0, tiled=True, axis_index_groups=groups)]
    ppermute x9, starting transfers between devices: 13.1 us -> 10.3 us  [ctx_shift(): return lax.ppermute(x, 'ctx', [(i, (i + 2 * shift) % 8) for i in range(8)])]
  transfers between devices with their start and end apart: 23 -> 24, of which waited for: 18 -> 19; matrix products, arithmetic and copies ran while one was open for 13% -> 14% of each run, Pallas kernels for 0% -> 0%
where the time goes in v8:
time: 225 us; the launch traced here: 224 us
  waiting for transfers between devices  78.6 us (35%)
  starting transfers between devices  45.4 us (20%)
  blocking collectives  33.6 us (15%)
  matrix products  22.2 us (10%)
  other arithmetic  21.9 us (10%)
  between operations  14.7 us (7%)
  local copies, waits for them, and re-layouts  7.62 us (3%)
    all_to_all x4, waiting for transfers between devices, exchange(): return lax.all_to_all(x, axis, 0, 0, tiled=True, axis_index_groups=groups)  41.2 us
    all_to_all x1, blocking collectives, exchange(): return lax.all_to_all(x, axis, 0, 0, tiled=True, axis_index_groups=groups)  33.6 us
    ppermute x9, waiting for transfers between devices, ctx_shift(): return lax.ppermute(x, 'ctx', [(i, (i + 2 * shift) % 8) for i in range(8)])  25.6 us
    all_to_all x4, starting transfers between devices, exchange(): return lax.all_to_all(x, axis, 0, 0, tiled=True, axis_index_groups=groups)  25.4 us
    ppermute x9, starting transfers between devices, ctx_shift(): return lax.ppermute(x, 'ctx', [(i, (i + 2 * shift) % 8) for i in range(8)])  10.3 us
    dot_general x4, matrix products, upstream_block(): jnp.dot(logit_grads, head_weight, preferred_element_type=jnp.float32)  10.1 us
    ppermute x6, starting transfers between devices, y_shift(): lax.ppermute(x, 'exp', [(i, (i + NZ * shift) % (NY * NZ)) for i in range(...  7.8 us
    ppermute x6, waiting for transfers between devices, y_shift(): lax.ppermute(x, 'exp', [(i, (i + NZ * shift) % (NY * NZ)) for i in range(...  6.41 us
  transfers between devices with their start and end apart: 24, of which 19 were waited for; matrix products, arithmetic and copies ran while one was open for 14% of the time, Pallas kernels for 0%

profile of v8, /device:TPU:32, one launch (start us, length us, event | category | flops | bytes accessed | tf_op | source)
XLA Modules:
  0.0 224.1 jit_solution(8469406637754300934)
XLA Ops:
  10.1 1.3 reduce_max.25
  11.4 1.5 exponential_reduce_fusion
  13.3 1.2 fusion.52
  14.5 11.4 %all-to-all-start = ((bf16[32,16,1024]{2,1,0:T(8,128)(2,1)}), bf16[32,16,1024]{2,1,0:T(8,128)(2,1)S(1)}, u32[]{:S(2)}, u32[]{:S(2)}) async-start(bf16[32,16,1024]{2,1,0:T(8,128)(2,1)} %fusion.52), calls=%async_computation | async-start | bytes 2097152 | tf_op jit(solution)/shard_map/all_to_all | solution.py:13
  25.9 1.6 collective-permute-start
  27.7 4.9 %broadcast_multiply_fusion = bf16[2560,896]{1,0:T(8,128)(2,1)} fusion(bf16[2560,896]{1,0:T(8,128)(2,1)} %param.12, bf16[]{:T(256)S(6)} %convert_element_type.293), kind=kLoop, calls=%fused_computation.16 | loop fusion | flops 2293760 | bytes 9175042 | tf_op jit(solution)/shard_map/mul | solution.py:188
  32.6 21.8 %all-to-all-done = bf16[32,16,1024]{2,1,0:T(8,128)(2,1)S(1)} async-done(((bf16[32,16,1024]{2,1,0:T(8,128)(2,1)}), bf16[32,16,1024]{2,1,0:T(8,128)(2,1)S(1)}, u32[]{:S(2)}, u32[]{:S(2)}) %all-to-all-start) | async-done | bytes 1048608 | tf_op jit(solution)/shard_map/all_to_all | solution.py:13
  55.9 4.3 %all-to-all-start.1 = ((f32[8,1,512]{2,1,0:T(1,128)}), f32[8,1,512]{2,1,0:T(1,128)S(1)}, u32[]{:S(2)}, u32[]{:S(2)}) async-start(f32[8,1,512]{2,1,0:T(1,128)} %broadcast_in_dim.154), calls=%async_computation.1 | async-start | bytes 32768 | tf_op jit(solution)/shard_map/all_to_all | solution.py:13
  61.4 4.2 %all-to-all-done.1 = f32[8,1,512]{2,1,0:T(1,128)S(1)} async-done(((f32[8,1,512]{2,1,0:T(1,128)}), f32[8,1,512]{2,1,0:T(1,128)S(1)}, u32[]{:S(2)}, u32[]{:S(2)}) %all-to-all-start.1) | async-done | bytes 16416 | tf_op jit(solution)/shard_map/all_to_all | solution.py:13
  66.1 4.7 %fusion.50 = f16[256,896]{1,0:T(8,128)(2,1)S(1)} fusion(bf16[2560,896]{1,0:T(8,128)(2,1)} %broadcast_multiply_fusion, s32[256]{0:T(256)S(1)} %bitcast.125, f32[256]{0:T(256)S(1)} %bitcast.122, f32[256]{0:T(256)S(1)} %bitcast.123, bf16[1024,2560]{1,0:T(8,128)(2,1)} %all-gather.2.cloned.1.call-done, s32[]{:T(128)S(6)} %select_n.174, f32[256]{0:T(256)S(1)} %bitcast.124), kind=kOutput, calls=%fused_computation.71 | convolution fusion | flops 1180106752 | bytes 6361092 | tf_op jit(solution)/shard_map/dot_general | solution.py:213
  70.8 1.2 collective-permute-start.3
  72.1 1.8 fusion.49
  75.0 2.4 %collective-permute-start.5 = (f16[128,896]{1,0:T(8,128)(2,1)S(1)}, f16[128,896]{1,0:T(8,128)(2,1)S(1)}, u32[]{:S(2)}, u32[]{:S(2)}) collective-permute-start(f16[128,896]{1,0:T(8,128)(2,1)S(1)} %get-tuple-element.31), channel_id=1, source_target_pairs={{0,24},{1,25},{2,26},{3,27},{4,28},{5,29},{6,30},{7,31},{8,0},{9,1... | collective-permute-start | bytes 688136 | tf_op jit(solution)/shard_map/ppermute | solution.py:71
  77.3 1.8 fusion.48
  79.5 1.8 fusion.47
  81.3 1.0 collective-permute-done.1
  83.2 2.7 %collective-permute-start.6 = (f16[128,896]{1,0:T(8,128)(2,1)S(1)}, f16[128,896]{1,0:T(8,128)(2,1)S(1)}, u32[]{:S(2)}, u32[]{:S(2)}) collective-permute-start(f16[128,896]{1,0:T(8,128)(2,1)S(1)} %add_convert_fusion.3), channel_id=1, source_target_pairs={{0,24},{1,25},{2,26},{3,27},{4,28},{5,29},{6,30},{7,31},{8,0},{9,1... | collective-permute-start | bytes 688136 | tf_op jit(solution)/shard_map/ppermute | solution.py:71
  85.9 1.3 fusion.15
  87.2 2.0 collective-permute-done.4
  89.2 3.0 %collective-permute-done.2 = f16[128,896]{1,0:T(8,128)(2,1)S(1)} collective-permute-done((f16[128,896]{1,0:T(8,128)(2,1)S(1)}, f16[128,896]{1,0:T(8,128)(2,1)S(1)}, u32[]{:S(2)}, u32[]{:S(2)}) %collective-permute-start.2) | collective-permute-done | bytes 229408 | tf_op jit(solution)/shard_map/ppermute | solution.py:71
  93.3 4.0 %all-to-all-start.2 = ((f16[8,32,896]{2,1,0:T(8,128)(2,1)}), f16[8,32,896]{2,1,0:T(8,128)(2,1)S(1)}, u32[]{:S(2)}, u32[]{:S(2)}) async-start(f16[8,32,896]{2,1,0:T(8,128)(2,1)} %bitcast.29), calls=%async_computation.2 | async-start | bytes 917504 | tf_op jit(solution)/shard_map/all_to_all | solution.py:13
  97.3 2.4 %fusion.18 = f16[512,1024]{1,0:T(8,128)(2,1)S(1)} fusion(bf16[512,896]{1,0:T(8,128)(2,1)} %slice.130, bf16[1,896,1024]{2,1,0:T(8,128)(2,1)S(1)} %copy-done), kind=kOutput, calls=%fused_computation.38 | convolution fusion | flops 940048384 | bytes 3801088 | tf_op jit(solution)/shard_map/dot_general | solution.py:221
  100.7 1.2 fusion.55
  101.9 8.3 %all-to-all-done.2 = f16[8,32,896]{2,1,0:T(8,128)(2,1)S(1)} async-done(((f16[8,32,896]{2,1,0:T(8,128)(2,1)}), f16[8,32,896]{2,1,0:T(8,128)(2,1)S(1)}, u32[]{:S(2)}, u32[]{:S(2)}) %all-to-all-start.2) | async-done | bytes 458784 | tf_op jit(solution)/shard_map/all_to_all | solution.py:13
  110.3 1.3 convolution_convert_fusion
  111.6 5.7 %all-to-all-start.3 = ((bf16[32,16,896]{2,1,0:T(8,128)(2,1)}), bf16[32,16,896]{2,1,0:T(8,128)(2,1)}, u32[]{:S(2)}, u32[]{:S(2)}) async-start(bf16[32,16,896]{2,1,0:T(8,128)(2,1)} %bitcast.94), calls=%async_computation.3 | async-start | bytes 1835008 | tf_op jit(solution)/shard_map/all_to_all | solution.py:13
  117.4 1.8 add_convert_fusion
  120.4 1.2 collective-permute-start.10
  121.6 2.1 collective-permute-start.9
  123.7 6.0 %collective-permute-done.10 = f16[64,2048]{1,0:T(8,128)(2,1)S(1)} collective-permute-done((f16[64,2048]{1,0:T(8,128)(2,1)S(1)}, f16[64,2048]{1,0:T(8,128)(2,1)S(1)}, u32[]{:S(2)}, u32[]{:S(2)}) %collective-permute-start.10) | collective-permute-done | bytes 262176 | tf_op jit(solution)/shard_map/ppermute | solution.py:28
  129.7 1.2 collective-permute-done.9
  130.9 1.6 collective-permute-done.8
  132.5 1.2 convert_add_fusion
  133.7 6.9 %all-to-all-done.3 = bf16[32,16,896]{2,1,0:T(8,128)(2,1)} async-done(((bf16[32,16,896]{2,1,0:T(8,128)(2,1)}), bf16[32,16,896]{2,1,0:T(8,128)(2,1)}, u32[]{:S(2)}, u32[]{:S(2)}) %all-to-all-start.3) | async-done | bytes 917536 | tf_op jit(solution)/shard_map/all_to_all | solution.py:13
  140.5 3.1 %fusion.21 = f16[512,1024]{1,0:T(8,128)(2,1)S(1)} fusion(bf16[512,896]{1,0:T(8,128)(2,1)} %bitcast.31, bf16[1,1024,896]{2,1,0:T(8,128)(2,1)} %param.21), kind=kOutput, calls=%fused_computation.39 | convolution fusion | flops 940048384 | bytes 3801088 | tf_op jit(solution)/shard_map/dot_general | solution.py:235
  143.8 1.9 collective-permute-done.11
  146.7 1.1 collective-permute-start.14
  147.8 2.1 collective-permute-start.13
  151.0 3.8 %collective-permute-done.14 = f16[64,1024]{1,0:T(8,128)(2,1)S(1)} collective-permute-done((f16[64,1024]{1,0:T(8,128)(2,1)}, f16[64,1024]{1,0:T(8,128)(2,1)S(1)}, u32[]{:S(2)}, u32[]{:S(2)}) %collective-permute-start.14) | collective-permute-done | bytes 131104 | tf_op jit(solution)/shard_map/ppermute | solution.py:28
  157.0 1.2 multiply_convert_fusion.19
  159.4 2.5 %collective-permute-start.16 = (bf16[64,2176]{1,0:T(8,128)(2,1)S(1)}, bf16[64,2176]{1,0:T(8,128)(2,1)S(1)}, u32[]{:S(2)}, u32[]{:S(2)}) collective-permute-start(bf16[64,2176]{1,0:T(8,128)(2,1)S(1)} %get-tuple-element.32), channel_id=1, source_target_pairs={{0,192},{32,224},{64,0},{96,32},{128,64},{160,96},{192,128},{224,1... | collective-permute-start | bytes 835592 | tf_op jit(solution)/shard_map/ppermute | solution.py:28
  162.4 6.3 %collective-permute-done.15 = bf16[64,2176]{1,0:T(8,128)(2,1)S(1)} collective-permute-done((bf16[64,2176]{1,0:T(8,128)(2,1)S(1)}, bf16[64,2176]{1,0:T(8,128)(2,1)S(1)}, u32[]{:S(2)}, u32[]{:S(2)}) %collective-permute-start.15) | collective-permute-done | bytes 278560 | tf_op jit(solution)/shard_map/ppermute | solution.py:28
  168.7 4.4 %collective-permute-done.16 = bf16[64,2176]{1,0:T(8,128)(2,1)S(1)} collective-permute-done((bf16[64,2176]{1,0:T(8,128)(2,1)S(1)}, bf16[64,2176]{1,0:T(8,128)(2,1)S(1)}, u32[]{:S(2)}, u32[]{:S(2)}) %collective-permute-start.16) | collective-permute-done | bytes 278560 | tf_op jit(solution)/shard_map/ppermute | solution.py:28
  174.2 2.9 %collective-permute-done.18 = bf16[256,2176]{1,0:T(8,128)(2,1)} collective-permute-done((bf16[256,2176]{1,0:T(8,128)(2,1)S(1)}, bf16[256,2176]{1,0:T(8,128)(2,1)}, u32[]{:S(2)}, u32[]{:S(2)}) %collective-permute-start.18) | collective-permute-done | bytes 1114144 | tf_op jit(solution)/shard_map/ppermute | solution.py:32
  177.1 1.4 broadcast_select_fusion.1
  178.5 1.3 fusion.7
  180.0 1.3 add_convert_fusion.1
  181.5 33.6 %all_to_all.45 = bf16[32,16,1024]{2,1,0:T(8,128)(2,1)S(1)} all-to-all(bf16[32,16,1024]{2,1,0:T(8,128)(2,1)S(1)} %bitcast.93), channel_id=1, replica_groups=mesh['ctx'=8,'exp'=32] {'exp'}, dimensions={0} | all-to-all | bytes 2097152 | tf_op jit(solution)/shard_map/all_to_all | solution.py:13
  (125 shorter events, 21.8 us)
Async XLA Ops:
  7.2 90.1 %copy-start = (bf16[1,896,1024]{2,1,0:T(8,128)(2,1)S(1)}, bf16[1,896,1024]{2,1,0:T(8,128)(2,1)}, u32[]{:S(2)}) copy-start(bf16[1,896,1024]{2,1,0:T(8,128)(2,1)} %param.20) | copy-start | bytes 5505028
  7.2 5.7 %copy-start.7 = (bf16[32,896]{1,0:T(8,128)(2,1)S(1)}, bf16[32,896]{1,0:T(8,128)(2,1)}, u32[]{:S(2)}) copy-start(bf16[32,896]{1,0:T(8,128)(2,1)} %param.16) | copy-start | bytes 172036
  7.2 58.4 %all-gather.2.cloned.1.call-start = ((), (), s32[]{:S(2)}) async-start(), calls=%async_computation.5 | async-start | bytes 5898240 | tf_op jit(solution)/shard_map/all_gather | solution.py:124
  13.3 12.6 %copy-start.14 = (s32[128]{0:T(128)S(1)}, s32[128]{0:T(128)}, u32[]{:S(2)}) copy-start(s32[128]{0:T(128)} %param.13) | copy-start | bytes 1540
  13.3 14.4 %copy-start.9 = (s32[16]{0:T(128)S(1)}, s32[16]{0:T(128)}, u32[]{:S(2)}) copy-start(s32[16]{0:T(128)} %param.14) | copy-start | bytes 196
  14.5 39.9 %all-to-all-start = ((bf16[32,16,1024]{2,1,0:T(8,128)(2,1)}), bf16[32,16,1024]{2,1,0:T(8,128)(2,1)S(1)}, u32[]{:S(2)}, u32[]{:S(2)}) async-start(bf16[32,16,1024]{2,1,0:T(8,128)(2,1)} %fusion.52), calls=%async_computation | async-start | bytes 2097152 | tf_op jit(solution)/shard_map/all_to_all | solution.py:13
  25.9 28.7 %collective-permute-start = (f32[1]{0:T(128)S(1)}, f32[1]{0:T(128)}, u32[]{:S(2)}, u32[]{:S(2)}) collective-permute-start(f32[1]{0:T(128)S(1)} %bitcast.126), channel_id=1, source_target_pairs={{32,0},{64,32},{96,64},{128,96},{160,128},{192,160},{224,192},{0,2... | collective-permute-start | bytes 20 | tf_op jit(solution)/shard_map/ppermute | solution.py:172
  27.7 26.9 %copy-start.10 = (f32[128]{0:T(128)S(1)}, f32[128]{0:T(128)}, u32[]{:S(2)}) copy-start(f32[128]{0:T(128)} %param.15) | copy-start | bytes 1540
  54.4 11.7 %copy-start.4 = (bf16[512,128]{1,0:T(8,128)(2,1)}, bf16[512,128]{1,0:T(8,128)(2,1)S(1)}, u32[]{:S(2)}) copy-start(bf16[512,128]{1,0:T(8,128)(2,1)S(1)} %slice.122) | copy-start | bytes 393220
  55.9 9.7 %all-to-all-start.1 = ((f32[8,1,512]{2,1,0:T(1,128)}), f32[8,1,512]{2,1,0:T(1,128)S(1)}, u32[]{:S(2)}, u32[]{:S(2)}) async-start(f32[8,1,512]{2,1,0:T(1,128)} %broadcast_in_dim.154), calls=%async_computation.1 | async-start | bytes 32768 | tf_op jit(solution)/shard_map/all_to_all | solution.py:13
  65.6 6.5 %slice-start = ((s8[4587520]{0:T(1024)(128)(4,1)}), s8[393216]{0:T(1024)(128)(4,1)S(1)}, s32[]{:S(2)}) async-start(s8[4587520]{0:T(1024)(128)(4,1)} %bitcast.87), calls=%async_computation.6 | async-start | bytes 786432
  66.1 6.0 %slice-start.1 = ((s8[4587520]{0:T(1024)(128)(4,1)}), s8[4194304]{0:T(1024)(128)(4,1)S(1)}, s32[]{:S(2)}) async-start(s8[4587520]{0:T(1024)(128)(4,1)} %bitcast.87), calls=%async_computation.7 | async-start | bytes 8388608
  66.1 6.0 %copy-start.11 = (bf16[1024,2560]{1,0:T(8,128)(2,1)S(1)}, bf16[1024,2560]{1,0:T(8,128)(2,1)}, u32[]{:S(2)}) copy-start(bf16[1024,2560]{1,0:T(8,128)(2,1)} %all-gather.2.cloned.1.call-done) | copy-start | bytes 15728644
  70.8 16.3 %collective-permute-start.3 = (f16[128,896]{1,0:T(8,128)(2,1)S(1)}, f16[128,896]{1,0:T(8,128)(2,1)S(1)}, u32[]{:S(2)}, u32[]{:S(2)}) collective-permute-start(f16[128,896]{1,0:T(8,128)(2,1)S(1)} %slice.131), channel_id=1, source_target_pairs={{0,24},{1,25},{2,26},{3,27},{4,28},{5,29},{6,30},{7,31},{8,0},{9,1... | collective-permute-start | bytes 688136 | tf_op jit(solution)/shard_map/ppermute | solution.py:71
  74.0 8.4 %collective-permute-start.1 = (f16[128,896]{1,0:T(8,128)(2,1)S(1)}, f16[128,896]{1,0:T(8,128)(2,1)S(1)}, u32[]{:S(2)}, u32[]{:S(2)}) collective-permute-start(f16[128,896]{1,0:T(8,128)(2,1)S(1)} %get-tuple-element.30), channel_id=1, source_target_pairs={{0,8},{1,9},{2,10},{3,11},{4,12},{5,13},{6,14},{7,15},{8,16},{9,17... | collective-permute-start | bytes 688136 | tf_op jit(solution)/shard_map/ppermute | solution.py:71
  75.0 8.2 %collective-permute-start.5 = (f16[128,896]{1,0:T(8,128)(2,1)S(1)}, f16[128,896]{1,0:T(8,128)(2,1)S(1)}, u32[]{:S(2)}, u32[]{:S(2)}) collective-permute-start(f16[128,896]{1,0:T(8,128)(2,1)S(1)} %get-tuple-element.31), channel_id=1, source_target_pairs={{0,24},{1,25},{2,26},{3,27},{4,28},{5,29},{6,30},{7,31},{8,0},{9,1... | collective-permute-start | bytes 688136 | tf_op jit(solution)/shard_map/ppermute | solution.py:71
  79.2 10.0 %collective-permute-start.4 = (f16[128,896]{1,0:T(8,128)(2,1)S(1)}, f16[128,896]{1,0:T(8,128)(2,1)S(1)}, u32[]{:S(2)}, u32[]{:S(2)}) collective-permute-start(f16[128,896]{1,0:T(8,128)(2,1)S(1)} %slice.133), channel_id=1, source_target_pairs={{0,8},{1,9},{2,10},{3,11},{4,12},{5,13},{6,14},{7,15},{8,16},{9,17... | collective-permute-start | bytes 688136 | tf_op jit(solution)/shard_map/ppermute | solution.py:71
  79.5 6.4 %copy-start.3 = (bf16[512,896]{1,0:T(8,128)(2,1)S(1)}, bf16[512,896]{1,0:T(8,128)(2,1)}, u32[]{:S(2)}) copy-start(bf16[512,896]{1,0:T(8,128)(2,1)} %slice.130) | copy-start | bytes 2752516
  79.5 6.4 %copy-start.12 = (bf16[1,896,1024]{2,1,0:T(8,128)(2,1)S(1)}, bf16[1,896,1024]{2,1,0:T(8,128)(2,1)}, u32[]{:S(2)}) copy-start(bf16[1,896,1024]{2,1,0:T(8,128)(2,1)} %param.19) | copy-start | bytes 5505028
  82.4 9.7 %collective-permute-start.2 = (f16[128,896]{1,0:T(8,128)(2,1)S(1)}, f16[128,896]{1,0:T(8,128)(2,1)S(1)}, u32[]{:S(2)}, u32[]{:S(2)}) collective-permute-start(f16[128,896]{1,0:T(8,128)(2,1)S(1)} %add_convert_fusion.4), channel_id=1, source_target_pairs={{0,8},{1,9},{2,10},{3,11},{4,12},{5,13},{6,14},{7,15},{8,16},{9,17... | collective-permute-start | bytes 688136 | tf_op jit(solution)/shard_map/ppermute | solution.py:71
  83.2 8.9 %collective-permute-start.6 = (f16[128,896]{1,0:T(8,128)(2,1)S(1)}, f16[128,896]{1,0:T(8,128)(2,1)S(1)}, u32[]{:S(2)}, u32[]{:S(2)}) collective-permute-start(f16[128,896]{1,0:T(8,128)(2,1)S(1)} %add_convert_fusion.3), channel_id=1, source_target_pairs={{0,24},{1,25},{2,26},{3,27},{4,28},{5,29},{6,30},{7,31},{8,0},{9,1... | collective-permute-start | bytes 688136 | tf_op jit(solution)/shard_map/ppermute | solution.py:71
  93.3 16.9 %all-to-all-start.2 = ((f16[8,32,896]{2,1,0:T(8,128)(2,1)}), f16[8,32,896]{2,1,0:T(8,128)(2,1)S(1)}, u32[]{:S(2)}, u32[]{:S(2)}) async-start(f16[8,32,896]{2,1,0:T(8,128)(2,1)} %bitcast.29), calls=%async_computation.2 | async-start | bytes 917504 | tf_op jit(solution)/shard_map/all_to_all | solution.py:13
  99.7 1.0 copy-start.1
  101.9 15.5 %collective-permute-start.7 = (f16[256,2048]{1,0:T(8,128)(2,1)}, f16[256,2048]{1,0:T(8,128)(2,1)}, u32[]{:S(2)}, u32[]{:S(2)}) collective-permute-start(f16[256,2048]{1,0:T(8,128)(2,1)} %fusion.55), channel_id=1, source_target_pairs={{0,32},{32,0},{64,96},{96,64},{128,160},{160,128},{192,224},{224,1... | collective-permute-start | bytes 3145736 | tf_op jit(solution)/shard_map/ppermute | solution.py:32
  111.6 28.9 %all-to-all-start.3 = ((bf16[32,16,896]{2,1,0:T(8,128)(2,1)}), bf16[32,16,896]{2,1,0:T(8,128)(2,1)}, u32[]{:S(2)}, u32[]{:S(2)}) async-start(bf16[32,16,896]{2,1,0:T(8,128)(2,1)} %bitcast.94), calls=%async_computation.3 | async-start | bytes 1835008 | tf_op jit(solution)/shard_map/all_to_all | solution.py:13
  119.2 1.0 copy-start.2
  120.4 9.3 %collective-permute-start.10 = (f16[64,2048]{1,0:T(8,128)(2,1)S(1)}, f16[64,2048]{1,0:T(8,128)(2,1)S(1)}, u32[]{:S(2)}, u32[]{:S(2)}) collective-permute-start(f16[64,2048]{1,0:T(8,128)(2,1)S(1)} %get-tuple-element.21), channel_id=1, source_target_pairs={{0,128},{32,160},{64,192},{96,224},{128,0},{160,32},{192,64},{224,... | collective-permute-start | bytes 786440 | tf_op jit(solution)/shard_map/ppermute | solution.py:28
  121.6 9.3 %collective-permute-start.9 = (f16[64,2048]{1,0:T(8,128)(2,1)S(1)}, f16[64,2048]{1,0:T(8,128)(2,1)S(1)}, u32[]{:S(2)}, u32[]{:S(2)}) collective-permute-start(f16[64,2048]{1,0:T(8,128)(2,1)S(1)} %get-tuple-element.22), channel_id=1, source_target_pairs={{0,192},{32,224},{64,0},{96,32},{128,64},{160,96},{192,128},{224,1... | collective-permute-start | bytes 786440 | tf_op jit(solution)/shard_map/ppermute | solution.py:28
  123.7 8.8 %collective-permute-start.8 = (f16[64,2048]{1,0:T(8,128)(2,1)S(1)}, f16[64,2048]{1,0:T(8,128)(2,1)}, u32[]{:S(2)}, u32[]{:S(2)}) collective-permute-start(f16[64,2048]{1,0:T(8,128)(2,1)S(1)} %get-tuple-element.20), channel_id=1, source_target_pairs={{0,64},{32,96},{64,128},{96,160},{128,192},{160,224},{192,0},{224,... | collective-permute-start | bytes 786440 | tf_op jit(solution)/shard_map/ppermute | solution.py:28
  143.7 2.0 collective-permute-start.11
  146.7 8.1 %collective-permute-start.14 = (f16[64,1024]{1,0:T(8,128)(2,1)}, f16[64,1024]{1,0:T(8,128)(2,1)S(1)}, u32[]{:S(2)}, u32[]{:S(2)}) collective-permute-start(f16[64,1024]{1,0:T(8,128)(2,1)} %get-tuple-element.28), channel_id=1, source_target_pairs={{0,128},{32,160},{64,192},{96,224},{128,0},{160,32},{192,64},{224,... | collective-permute-start | bytes 393224 | tf_op jit(solution)/shard_map/ppermute | solution.py:28
  147.8 7.4 %collective-permute-start.13 = (f16[64,1024]{1,0:T(8,128)(2,1)}, f16[64,1024]{1,0:T(8,128)(2,1)S(1)}, u32[]{:S(2)}, u32[]{:S(2)}) collective-permute-start(f16[64,1024]{1,0:T(8,128)(2,1)} %get-tuple-element.29), channel_id=1, source_target_pairs={{0,192},{32,224},{64,0},{96,32},{128,64},{160,96},{192,128},{224,1... | collective-permute-start | bytes 393224 | tf_op jit(solution)/shard_map/ppermute | solution.py:28
  150.0 7.0 %collective-permute-start.12 = (f16[64,1024]{1,0:T(8,128)(2,1)S(1)}, f16[64,1024]{1,0:T(8,128)(2,1)}, u32[]{:S(2)}, u32[]{:S(2)}) collective-permute-start(f16[64,1024]{1,0:T(8,128)(2,1)S(1)} %get-tuple-element.27), channel_id=1, source_target_pairs={{0,64},{32,96},{64,128},{96,160},{128,192},{160,224},{192,0},{224,... | collective-permute-start | bytes 393224 | tf_op jit(solution)/shard_map/ppermute | solution.py:28
  154.8 0.6 copy-start.5
  155.4 0.7 copy-start.6
  158.6 10.1 %collective-permute-start.15 = (bf16[64,2176]{1,0:T(8,128)(2,1)S(1)}, bf16[64,2176]{1,0:T(8,128)(2,1)S(1)}, u32[]{:S(2)}, u32[]{:S(2)}) collective-permute-start(bf16[64,2176]{1,0:T(8,128)(2,1)S(1)} %get-tuple-element.32), channel_id=1, source_target_pairs={{0,64},{32,96},{64,128},{96,160},{128,192},{160,224},{192,0},{224,... | collective-permute-start | bytes 835592 | tf_op jit(solution)/shard_map/ppermute | solution.py:28
  159.4 13.7 %collective-permute-start.16 = (bf16[64,2176]{1,0:T(8,128)(2,1)S(1)}, bf16[64,2176]{1,0:T(8,128)(2,1)S(1)}, u32[]{:S(2)}, u32[]{:S(2)}) collective-permute-start(bf16[64,2176]{1,0:T(8,128)(2,1)S(1)} %get-tuple-element.32), channel_id=1, source_target_pairs={{0,192},{32,224},{64,0},{96,32},{128,64},{160,96},{192,128},{224,1... | collective-permute-start | bytes 835592 | tf_op jit(solution)/shard_map/ppermute | solution.py:28
  161.9 12.2 %collective-permute-start.17 = (bf16[64,2176]{1,0:T(8,128)(2,1)S(1)}, bf16[64,2176]{1,0:T(8,128)(2,1)S(1)}, u32[]{:S(2)}, u32[]{:S(2)}) collective-permute-start(bf16[64,2176]{1,0:T(8,128)(2,1)S(1)} %get-tuple-element.32), channel_id=1, source_target_pairs={{0,128},{32,160},{64,192},{96,224},{128,0},{160,32},{192,64},{224,... | collective-permute-start | bytes 835592 | tf_op jit(solution)/shard_map/ppermute | solution.py:28
  174.1 3.0 %collective-permute-start.18 = (bf16[256,2176]{1,0:T(8,128)(2,1)S(1)}, bf16[256,2176]{1,0:T(8,128)(2,1)}, u32[]{:S(2)}, u32[]{:S(2)}) collective-permute-start(bf16[256,2176]{1,0:T(8,128)(2,1)S(1)} %constant_dynamic-update-slice_fusion), channel_id=1, source_target_pairs={{0,32},{32,0},{64,96},{96,64},{128,160},{160,128},{192,224},{224,1... | collective-permute-start | bytes 3342344 | tf_op jit(solution)/shard_map/ppermute | solution.py:32
  178.5 1.5 copy-start.13
  181.5 35.1 %copy-start.8 = (s32[32,8]{0,1:T(8,128)S(1)}, s32[32,8]{0,1:T(8,128)}, u32[]{:S(2)}) copy-start(s32[32,8]{0,1:T(8,128)} %param.17) | copy-start | bytes 3076
Sparse Core Ops, SparseCore 0:
  9.9 41.6 all-gather.1

commit v9 on v8

--- a/solution.py
+++ b/solution.py
@@ -53,18 +53,14 @@
     return own
 
 
-def ctx_gather(own):
-    core = lax.axis_index("ctx") % 2
+def chips_gather(own):
     chip = lax.axis_index("ctx") // 2
     own_rows, width = own.shape
     from_one, from_three, from_two = [ctx_shift(own, shift) for shift in (1, 3, 2)]
     half = jnp.zeros((4 * own_rows, width), own.dtype)
     for piece, shift in ((own, 0), (from_one, 1), (from_three, 3), (from_two, 2)):
         half = lax.dynamic_update_slice_in_dim(half, piece, (chip + 4 - shift) % 4 * own_rows, axis=0)
-    other = ctx_swap(half)
-    first = jnp.where(core == 0, half, other)
-    second = jnp.where(core == 0, other, half)
-    return jnp.concatenate([first, second], axis=0)
+    return half
 
 
 def y_shift(x, shift):
@@ -249,15 +245,22 @@
     prob_block = jnp.where(
         lane == 0, prob_high[:, None], jnp.where(lane == 1, prob_low[:, None], 0)
     ).astype(jnp.bfloat16)
-    grads = ctx_gather(jnp.concatenate([gate_grad, up_grad, prob_block], axis=1))
-    input_grad = lax.dot_general(
-        grads[:, :hidden], gate_w, CONTRACT_LAST, preferred_element_type=jnp.float32
-    ) + lax.dot_general(
-        grads[:, hidden : 2 * hidden], up_w, CONTRACT_LAST, preferred_element_type=jnp.float32
-    )
-    back = exchange(
-        jnp.concatenate([input_grad.astype(jnp.bfloat16), grads[:, 2 * hidden :]], axis=1), "exp"
-    )
+    def route_gradients(grads):
+        input_grad = lax.dot_general(
+            grads[:, :hidden], gate_w, CONTRACT_LAST, preferred_element_type=jnp.float32
+        ) + lax.dot_general(
+            grads[:, hidden : 2 * hidden], up_w, CONTRACT_LAST, preferred_element_type=jnp.float32
+        )
+        return jnp.concatenate([input_grad.astype(jnp.bfloat16), grads[:, 2 * hidden :]], axis=1)
+
+    grads = chips_gather(jnp.concatenate([gate_grad, up_grad, prob_block], axis=1))
+    other_grads = ctx_swap(grads)
+    mine, others = route_gradients(grads), route_gradients(other_grads)
+    core = lax.axis_index("ctx") % 2
+    send_back = jnp.concatenate(
+        [jnp.where(core == 0, mine, others), jnp.where(core == 0, others, mine)], axis=0
+    )
+    back = exchange(send_back, "exp")
     d_x = upstream + lax.dot_general(
         slot_owner,
         back[:, :feature_width],

time: 225 us -> 226 us (level)
  matrix products: 22.2 us -> 24.8 us
  waiting for transfers between devices: 78.6 us -> 76.3 us
    dot_general x2 -> x4, matrix products: 2.59 us -> 5.12 us  [the longest x2 2.6 us: route_gradients(): lax.dot_general(grads[:, :hidden], gate_w, CONTRACT_LAST, preferred_eleme...]
    ppermute x3, waiting for transfers between devices: 4.77 us -> 2.48 us  [ctx_swap(): return lax.ppermute(x, 'ctx', [(i, i ^ 1) for i in range(8)])]
where the time goes in v9:
time: 226 us; the launch traced here: 224 us
  waiting for transfers between devices  76.3 us (34%)
  starting transfers between devices  45.4 us (20%)
  blocking collectives  33.6 us (15%)
  matrix products  24.8 us (11%)
  other arithmetic  20.6 us (9%)
  between operations  14.7 us (7%)
  local copies, waits for them, and re-layouts  9 us (4%)
    all_to_all x4, waiting for transfers between devices, exchange(): return lax.all_to_all(x, axis, 0, 0, tiled=True, axis_index_groups=groups)  41.2 us
    all_to_all x1, blocking collectives, exchange(): return lax.all_to_all(x, axis, 0, 0, tiled=True, axis_index_groups=groups)  33.6 us
    ppermute x9, waiting for transfers between devices, ctx_shift(): return lax.ppermute(x, 'ctx', [(i, (i + 2 * shift) % 8) for i in range(8)])  25.6 us
    all_to_all x4, starting transfers between devices, exchange(): return lax.all_to_all(x, axis, 0, 0, tiled=True, axis_index_groups=groups)  25.4 us
    ppermute x9, starting transfers between devices, ctx_shift(): return lax.ppermute(x, 'ctx', [(i, (i + 2 * shift) % 8) for i in range(8)])  10.3 us
    dot_general x4, matrix products, upstream_block(): jnp.dot(logit_grads, head_weight, preferred_element_type=jnp.float32)  10.1 us
    ppermute x6, starting transfers between devices, y_shift(): lax.ppermute(x, 'exp', [(i, (i + NZ * shift) % (NY * NZ)) for i in range(...  7.8 us
    ppermute x6, waiting for transfers between devices, y_shift(): lax.ppermute(x, 'exp', [(i, (i + NZ * shift) % (NY * NZ)) for i in range(...  6.41 us
  transfers between devices with their start and end apart: 24, of which 19 were waited for; matrix products, arithmetic and copies ran while one was open for 14% of the time, Pallas kernels for 0%

profile of v9, /device:TPU:32, one launch (start us, length us, event | category | flops | bytes accessed | tf_op | source)
XLA Modules:
  0.0 224.5 jit_solution(14761834256816564954)
XLA Ops:
  10.1 1.3 reduce_max.25
  11.4 1.5 exponential_reduce_fusion
  13.3 1.2 fusion.64
  14.5 11.4 %all-to-all-start = ((bf16[32,16,1024]{2,1,0:T(8,128)(2,1)}), bf16[32,16,1024]{2,1,0:T(8,128)(2,1)S(1)}, u32[]{:S(2)}, u32[]{:S(2)}) async-start(bf16[32,16,1024]{2,1,0:T(8,128)(2,1)} %fusion.64), calls=%async_computation | async-start | bytes 2097152 | tf_op jit(solution)/shard_map/all_to_all | solution.py:13
  25.9 1.6 collective-permute-start
  27.7 4.9 %broadcast_multiply_fusion = bf16[2560,896]{1,0:T(8,128)(2,1)} fusion(bf16[2560,896]{1,0:T(8,128)(2,1)} %param.12, bf16[]{:T(256)S(6)} %convert_element_type.296), kind=kLoop, calls=%fused_computation.12 | loop fusion | flops 2293760 | bytes 9175042 | tf_op jit(solution)/shard_map/mul | solution.py:184
  32.6 21.8 %all-to-all-done = bf16[32,16,1024]{2,1,0:T(8,128)(2,1)S(1)} async-done(((bf16[32,16,1024]{2,1,0:T(8,128)(2,1)}), bf16[32,16,1024]{2,1,0:T(8,128)(2,1)S(1)}, u32[]{:S(2)}, u32[]{:S(2)}) %all-to-all-start) | async-done | bytes 1048608 | tf_op jit(solution)/shard_map/all_to_all | solution.py:13
  55.9 4.3 %all-to-all-start.1 = ((f32[8,1,512]{2,1,0:T(1,128)}), f32[8,1,512]{2,1,0:T(1,128)S(1)}, u32[]{:S(2)}, u32[]{:S(2)}) async-start(f32[8,1,512]{2,1,0:T(1,128)} %broadcast_in_dim.154), calls=%async_computation.1 | async-start | bytes 32768 | tf_op jit(solution)/shard_map/all_to_all | solution.py:13
  60.4 1.0 slice.142
  61.4 4.2 %all-to-all-done.1 = f32[8,1,512]{2,1,0:T(1,128)S(1)} async-done(((f32[8,1,512]{2,1,0:T(1,128)}), f32[8,1,512]{2,1,0:T(1,128)S(1)}, u32[]{:S(2)}, u32[]{:S(2)}) %all-to-all-start.1) | async-done | bytes 16416 | tf_op jit(solution)/shard_map/all_to_all | solution.py:13
  66.1 4.7 %fusion.56 = f16[256,896]{1,0:T(8,128)(2,1)S(1)} fusion(bf16[2560,896]{1,0:T(8,128)(2,1)} %broadcast_multiply_fusion, s32[256]{0:T(256)S(1)} %bitcast.135, f32[256]{0:T(256)S(1)} %bitcast.132, f32[256]{0:T(256)S(1)} %bitcast.133, bf16[1024,2560]{1,0:T(8,128)(2,1)} %all-gather.2.cloned.1.call-done, s32[]{:T(128)S(6)} %select_n.174, f32[256]{0:T(256)S(1)} %bitcast.134), kind=kOutput, calls=%fused_computation.69 | convolution fusion | flops 1180106752 | bytes 6361092 | tf_op jit(solution)/shard_map/dot_general | solution.py:209
  70.8 1.2 collective-permute-start.3
  72.1 1.8 fusion.55
  75.0 2.4 %collective-permute-start.5 = (f16[128,896]{1,0:T(8,128)(2,1)S(1)}, f16[128,896]{1,0:T(8,128)(2,1)S(1)}, u32[]{:S(2)}, u32[]{:S(2)}) collective-permute-start(f16[128,896]{1,0:T(8,128)(2,1)S(1)} %get-tuple-element.31), channel_id=1, source_target_pairs={{0,24},{1,25},{2,26},{3,27},{4,28},{5,29},{6,30},{7,31},{8,0},{9,1... | collective-permute-start | bytes 688136 | tf_op jit(solution)/shard_map/ppermute | solution.py:67
  77.3 1.8 fusion.54
  79.5 1.8 fusion.53
  81.3 1.0 collective-permute-done.1
  83.2 2.7 %collective-permute-start.6 = (f16[128,896]{1,0:T(8,128)(2,1)S(1)}, f16[128,896]{1,0:T(8,128)(2,1)S(1)}, u32[]{:S(2)}, u32[]{:S(2)}) collective-permute-start(f16[128,896]{1,0:T(8,128)(2,1)S(1)} %add_convert_fusion.2), channel_id=1, source_target_pairs={{0,24},{1,25},{2,26},{3,27},{4,28},{5,29},{6,30},{7,31},{8,0},{9,1... | collective-permute-start | bytes 688136 | tf_op jit(solution)/shard_map/ppermute | solution.py:67
  85.9 1.3 fusion.17
  87.2 2.0 collective-permute-done.4
  89.2 3.0 %collective-permute-done.2 = f16[128,896]{1,0:T(8,128)(2,1)S(1)} collective-permute-done((f16[128,896]{1,0:T(8,128)(2,1)S(1)}, f16[128,896]{1,0:T(8,128)(2,1)S(1)}, u32[]{:S(2)}, u32[]{:S(2)}) %collective-permute-start.2) | collective-permute-done | bytes 229408 | tf_op jit(solution)/shard_map/ppermute | solution.py:67
  93.3 4.0 %all-to-all-start.2 = ((f16[8,32,896]{2,1,0:T(8,128)(2,1)}), f16[8,32,896]{2,1,0:T(8,128)(2,1)S(1)}, u32[]{:S(2)}, u32[]{:S(2)}) async-start(f16[8,32,896]{2,1,0:T(8,128)(2,1)} %bitcast.29), calls=%async_computation.2 | async-start | bytes 917504 | tf_op jit(solution)/shard_map/all_to_all | solution.py:13
  97.3 2.4 %fusion.20 = f16[512,1024]{1,0:T(8,128)(2,1)S(1)} fusion(bf16[512,896]{1,0:T(8,128)(2,1)} %slice.142, bf16[1,896,1024]{2,1,0:T(8,128)(2,1)S(1)} %copy-done), kind=kOutput, calls=%fused_computation.34 | convolution fusion | flops 940048384 | bytes 3801088 | tf_op jit(solution)/shard_map/dot_general | solution.py:217
  100.7 1.2 fusion.65
  101.9 8.3 %all-to-all-done.2 = f16[8,32,896]{2,1,0:T(8,128)(2,1)S(1)} async-done(((f16[8,32,896]{2,1,0:T(8,128)(2,1)}), f16[8,32,896]{2,1,0:T(8,128)(2,1)S(1)}, u32[]{:S(2)}, u32[]{:S(2)}) %all-to-all-start.2) | async-done | bytes 458784 | tf_op jit(solution)/shard_map/all_to_all | solution.py:13
  110.3 1.3 convolution_convert_fusion
  111.6 5.7 %all-to-all-start.3 = ((bf16[32,16,896]{2,1,0:T(8,128)(2,1)}), bf16[32,16,896]{2,1,0:T(8,128)(2,1)}, u32[]{:S(2)}, u32[]{:S(2)}) async-start(bf16[32,16,896]{2,1,0:T(8,128)(2,1)} %bitcast.104), calls=%async_computation.3 | async-start | bytes 1835008 | tf_op jit(solution)/shard_map/all_to_all | solution.py:13
  117.4 1.8 add_convert_fusion
  120.4 1.2 collective-permute-start.10
  121.6 2.1 collective-permute-start.9
  123.7 6.0 %collective-permute-done.10 = f16[64,2048]{1,0:T(8,128)(2,1)S(1)} collective-permute-done((f16[64,2048]{1,0:T(8,128)(2,1)S(1)}, f16[64,2048]{1,0:T(8,128)(2,1)S(1)}, u32[]{:S(2)}, u32[]{:S(2)}) %collective-permute-start.10) | collective-permute-done | bytes 262176 | tf_op jit(solution)/shard_map/ppermute | solution.py:28
  129.7 1.2 collective-permute-done.9
  130.9 1.6 collective-permute-done.8
  132.5 1.2 convert_add_fusion
  133.7 6.9 %all-to-all-done.3 = bf16[32,16,896]{2,1,0:T(8,128)(2,1)} async-done(((bf16[32,16,896]{2,1,0:T(8,128)(2,1)}), bf16[32,16,896]{2,1,0:T(8,128)(2,1)}, u32[]{:S(2)}, u32[]{:S(2)}) %all-to-all-start.3) | async-done | bytes 917536 | tf_op jit(solution)/shard_map/all_to_all | solution.py:13
  140.5 3.1 %fusion.23 = f16[512,1024]{1,0:T(8,128)(2,1)S(1)} fusion(bf16[512,896]{1,0:T(8,128)(2,1)} %bitcast.31, bf16[1,1024,896]{2,1,0:T(8,128)(2,1)} %param.21), kind=kOutput, calls=%fused_computation.35 | convolution fusion | flops 940048384 | bytes 3801088 | tf_op jit(solution)/shard_map/dot_general | solution.py:231
  143.8 1.9 collective-permute-done.11
  146.7 1.1 collective-permute-start.14
  147.8 2.1 collective-permute-start.13
  151.0 3.8 %collective-permute-done.14 = f16[64,1024]{1,0:T(8,128)(2,1)S(1)} collective-permute-done((f16[64,1024]{1,0:T(8,128)(2,1)}, f16[64,1024]{1,0:T(8,128)(2,1)S(1)}, u32[]{:S(2)}, u32[]{:S(2)}) %collective-permute-start.14) | collective-permute-done | bytes 131104 | tf_op jit(solution)/shard_map/ppermute | solution.py:28
  157.0 1.2 multiply_convert_fusion.19
  159.4 2.5 %collective-permute-start.16 = (bf16[64,2176]{1,0:T(8,128)(2,1)S(1)}, bf16[64,2176]{1,0:T(8,128)(2,1)S(1)}, u32[]{:S(2)}, u32[]{:S(2)}) collective-permute-start(bf16[64,2176]{1,0:T(8,128)(2,1)S(1)} %get-tuple-element.32), channel_id=1, source_target_pairs={{0,192},{32,224},{64,0},{96,32},{128,64},{160,96},{192,128},{224,1... | collective-permute-start | bytes 835592 | tf_op jit(solution)/shard_map/ppermute | solution.py:28
  162.4 6.3 %collective-permute-done.15 = bf16[64,2176]{1,0:T(8,128)(2,1)S(1)} collective-permute-done((bf16[64,2176]{1,0:T(8,128)(2,1)S(1)}, bf16[64,2176]{1,0:T(8,128)(2,1)S(1)}, u32[]{:S(2)}, u32[]{:S(2)}) %collective-permute-start.15) | collective-permute-done | bytes 278560 | tf_op jit(solution)/shard_map/ppermute | solution.py:28
  168.7 4.4 %collective-permute-done.16 = bf16[64,2176]{1,0:T(8,128)(2,1)S(1)} collective-permute-done((bf16[64,2176]{1,0:T(8,128)(2,1)S(1)}, bf16[64,2176]{1,0:T(8,128)(2,1)S(1)}, u32[]{:S(2)}, u32[]{:S(2)}) %collective-permute-start.16) | collective-permute-done | bytes 278560 | tf_op jit(solution)/shard_map/ppermute | solution.py:28
  173.1 1.0 collective-permute-done.17
  177.9 1.8 fusion.5
  179.7 1.8 fusion.57
  181.9 33.6 %all_to_all.45 = bf16[32,16,1024]{2,1,0:T(8,128)(2,1)S(1)} all-to-all(bf16[32,16,1024]{2,1,0:T(8,128)(2,1)S(1)} %bitcast.103), channel_id=1, replica_groups=mesh['ctx'=8,'exp'=32] {'exp'}, dimensions={0} | all-to-all | bytes 2097152 | tf_op jit(solution)/shard_map/all_to_all | solution.py:13
  (129 shorter events, 23.5 us)
Async XLA Ops:
  7.2 90.1 %copy-start = (bf16[1,896,1024]{2,1,0:T(8,128)(2,1)S(1)}, bf16[1,896,1024]{2,1,0:T(8,128)(2,1)}, u32[]{:S(2)}) copy-start(bf16[1,896,1024]{2,1,0:T(8,128)(2,1)} %param.20) | copy-start | bytes 5505028
  7.2 5.7 %copy-start.9 = (bf16[32,896]{1,0:T(8,128)(2,1)S(1)}, bf16[32,896]{1,0:T(8,128)(2,1)}, u32[]{:S(2)}) copy-start(bf16[32,896]{1,0:T(8,128)(2,1)} %param.16) | copy-start | bytes 172036
  7.2 58.4 %all-gather.2.cloned.1.call-start = ((), (), s32[]{:S(2)}) async-start(), calls=%async_computation.5 | async-start | bytes 5898240 | tf_op jit(solution)/shard_map/all_gather | solution.py:120
  13.3 12.6 %copy-start.14 = (s32[128]{0:T(128)S(1)}, s32[128]{0:T(128)}, u32[]{:S(2)}) copy-start(s32[128]{0:T(128)} %param.13) | copy-start | bytes 1540
  13.3 14.4 %copy-start.11 = (s32[16]{0:T(128)S(1)}, s32[16]{0:T(128)}, u32[]{:S(2)}) copy-start(s32[16]{0:T(128)} %param.14) | copy-start | bytes 196
  14.5 39.9 %all-to-all-start = ((bf16[32,16,1024]{2,1,0:T(8,128)(2,1)}), bf16[32,16,1024]{2,1,0:T(8,128)(2,1)S(1)}, u32[]{:S(2)}, u32[]{:S(2)}) async-start(bf16[32,16,1024]{2,1,0:T(8,128)(2,1)} %fusion.64), calls=%async_computation | async-start | bytes 2097152 | tf_op jit(solution)/shard_map/all_to_all | solution.py:13
  25.9 28.7 %collective-permute-start = (f32[1]{0:T(128)S(1)}, f32[1]{0:T(128)}, u32[]{:S(2)}, u32[]{:S(2)}) collective-permute-start(f32[1]{0:T(128)S(1)} %bitcast.136), channel_id=1, source_target_pairs={{32,0},{64,32},{96,64},{128,96},{160,128},{192,160},{224,192},{0,2... | collective-permute-start | bytes 20 | tf_op jit(solution)/shard_map/ppermute | solution.py:168
  27.7 26.9 %copy-start.12 = (f32[128]{0:T(128)S(1)}, f32[128]{0:T(128)}, u32[]{:S(2)}) copy-start(f32[128]{0:T(128)} %param.15) | copy-start | bytes 1540
  54.4 11.7 %copy-start.6 = (bf16[512,128]{1,0:T(8,128)(2,1)}, bf16[512,128]{1,0:T(8,128)(2,1)S(1)}, u32[]{:S(2)}) copy-start(bf16[512,128]{1,0:T(8,128)(2,1)S(1)} %slice.134) | copy-start | bytes 393220
  55.9 9.7 %all-to-all-start.1 = ((f32[8,1,512]{2,1,0:T(1,128)}), f32[8,1,512]{2,1,0:T(1,128)S(1)}, u32[]{:S(2)}, u32[]{:S(2)}) async-start(f32[8,1,512]{2,1,0:T(1,128)} %broadcast_in_dim.154), calls=%async_computation.1 | async-start | bytes 32768 | tf_op jit(solution)/shard_map/all_to_all | solution.py:13
  65.6 6.5 %slice-start = ((s8[4587520]{0:T(1024)(128)(4,1)}), s8[393216]{0:T(1024)(128)(4,1)S(1)}, s32[]{:S(2)}) async-start(s8[4587520]{0:T(1024)(128)(4,1)} %bitcast.97), calls=%async_computation.6 | async-start | bytes 786432
  66.1 6.0 %slice-start.1 = ((s8[4587520]{0:T(1024)(128)(4,1)}), s8[4194304]{0:T(1024)(128)(4,1)S(1)}, s32[]{:S(2)}) async-start(s8[4587520]{0:T(1024)(128)(4,1)} %bitcast.97), calls=%async_computation.7 | async-start | bytes 8388608
  66.1 6.0 %copy-start.13 = (bf16[1024,2560]{1,0:T(8,128)(2,1)S(1)}, bf16[1024,2560]{1,0:T(8,128)(2,1)}, u32[]{:S(2)}) copy-start(bf16[1024,2560]{1,0:T(8,128)(2,1)} %all-gather.2.cloned.1.call-done) | copy-start | bytes 15728644
  70.8 16.3 %collective-permute-start.3 = (f16[128,896]{1,0:T(8,128)(2,1)S(1)}, f16[128,896]{1,0:T(8,128)(2,1)S(1)}, u32[]{:S(2)}, u32[]{:S(2)}) collective-permute-start(f16[128,896]{1,0:T(8,128)(2,1)S(1)} %slice.143), channel_id=1, source_target_pairs={{0,24},{1,25},{2,26},{3,27},{4,28},{5,29},{6,30},{7,31},{8,0},{9,1... | collective-permute-start | bytes 688136 | tf_op jit(solution)/shard_map/ppermute | solution.py:67
  74.0 8.4 %collective-permute-start.1 = (f16[128,896]{1,0:T(8,128)(2,1)S(1)}, f16[128,896]{1,0:T(8,128)(2,1)S(1)}, u32[]{:S(2)}, u32[]{:S(2)}) collective-permute-start(f16[128,896]{1,0:T(8,128)(2,1)S(1)} %get-tuple-element.30), channel_id=1, source_target_pairs={{0,8},{1,9},{2,10},{3,11},{4,12},{5,13},{6,14},{7,15},{8,16},{9,17... | collective-permute-start | bytes 688136 | tf_op jit(solution)/shard_map/ppermute | solution.py:67
  75.0 8.2 %collective-permute-start.5 = (f16[128,896]{1,0:T(8,128)(2,1)S(1)}, f16[128,896]{1,0:T(8,128)(2,1)S(1)}, u32[]{:S(2)}, u32[]{:S(2)}) collective-permute-start(f16[128,896]{1,0:T(8,128)(2,1)S(1)} %get-tuple-element.31), channel_id=1, source_target_pairs={{0,24},{1,25},{2,26},{3,27},{4,28},{5,29},{6,30},{7,31},{8,0},{9,1... | collective-permute-start | bytes 688136 | tf_op jit(solution)/shard_map/ppermute | solution.py:67
  79.2 10.0 %collective-permute-start.4 = (f16[128,896]{1,0:T(8,128)(2,1)S(1)}, f16[128,896]{1,0:T(8,128)(2,1)S(1)}, u32[]{:S(2)}, u32[]{:S(2)}) collective-permute-start(f16[128,896]{1,0:T(8,128)(2,1)S(1)} %slice.145), channel_id=1, source_target_pairs={{0,8},{1,9},{2,10},{3,11},{4,12},{5,13},{6,14},{7,15},{8,16},{9,17... | collective-permute-start | bytes 688136 | tf_op jit(solution)/shard_map/ppermute | solution.py:67
  79.5 6.4 %copy-start.1 = (bf16[1,896,1024]{2,1,0:T(8,128)(2,1)S(1)}, bf16[1,896,1024]{2,1,0:T(8,128)(2,1)}, u32[]{:S(2)}) copy-start(bf16[1,896,1024]{2,1,0:T(8,128)(2,1)} %param.19) | copy-start | bytes 5505028
  79.5 6.4 %copy-start.5 = (bf16[512,896]{1,0:T(8,128)(2,1)S(1)}, bf16[512,896]{1,0:T(8,128)(2,1)}, u32[]{:S(2)}) copy-start(bf16[512,896]{1,0:T(8,128)(2,1)} %slice.142) | copy-start | bytes 2752516
  82.4 9.7 %collective-permute-start.2 = (f16[128,896]{1,0:T(8,128)(2,1)S(1)}, f16[128,896]{1,0:T(8,128)(2,1)S(1)}, u32[]{:S(2)}, u32[]{:S(2)}) collective-permute-start(f16[128,896]{1,0:T(8,128)(2,1)S(1)} %add_convert_fusion.3), channel_id=1, source_target_pairs={{0,8},{1,9},{2,10},{3,11},{4,12},{5,13},{6,14},{7,15},{8,16},{9,17... | collective-permute-start | bytes 688136 | tf_op jit(solution)/shard_map/ppermute | solution.py:67
  83.2 8.9 %collective-permute-start.6 = (f16[128,896]{1,0:T(8,128)(2,1)S(1)}, f16[128,896]{1,0:T(8,128)(2,1)S(1)}, u32[]{:S(2)}, u32[]{:S(2)}) collective-permute-start(f16[128,896]{1,0:T(8,128)(2,1)S(1)} %add_convert_fusion.2), channel_id=1, source_target_pairs={{0,24},{1,25},{2,26},{3,27},{4,28},{5,29},{6,30},{7,31},{8,0},{9,1... | collective-permute-start | bytes 688136 | tf_op jit(solution)/shard_map/ppermute | solution.py:67
  93.3 16.9 %all-to-all-start.2 = ((f16[8,32,896]{2,1,0:T(8,128)(2,1)}), f16[8,32,896]{2,1,0:T(8,128)(2,1)S(1)}, u32[]{:S(2)}, u32[]{:S(2)}) async-start(f16[8,32,896]{2,1,0:T(8,128)(2,1)} %bitcast.29), calls=%async_computation.2 | async-start | bytes 917504 | tf_op jit(solution)/shard_map/all_to_all | solution.py:13
  99.7 1.0 copy-start.3
  101.9 15.5 %collective-permute-start.7 = (f16[256,2048]{1,0:T(8,128)(2,1)}, f16[256,2048]{1,0:T(8,128)(2,1)}, u32[]{:S(2)}, u32[]{:S(2)}) collective-permute-start(f16[256,2048]{1,0:T(8,128)(2,1)} %fusion.65), channel_id=1, source_target_pairs={{0,32},{32,0},{64,96},{96,64},{128,160},{160,128},{192,224},{224,1... | collective-permute-start | bytes 3145736 | tf_op jit(solution)/shard_map/ppermute | solution.py:32
  111.6 28.9 %all-to-all-start.3 = ((bf16[32,16,896]{2,1,0:T(8,128)(2,1)}), bf16[32,16,896]{2,1,0:T(8,128)(2,1)}, u32[]{:S(2)}, u32[]{:S(2)}) async-start(bf16[32,16,896]{2,1,0:T(8,128)(2,1)} %bitcast.104), calls=%async_computation.3 | async-start | bytes 1835008 | tf_op jit(solution)/shard_map/all_to_all | solution.py:13
  119.2 1.0 copy-start.4
  120.4 9.3 %collective-permute-start.10 = (f16[64,2048]{1,0:T(8,128)(2,1)S(1)}, f16[64,2048]{1,0:T(8,128)(2,1)S(1)}, u32[]{:S(2)}, u32[]{:S(2)}) collective-permute-start(f16[64,2048]{1,0:T(8,128)(2,1)S(1)} %get-tuple-element.21), channel_id=1, source_target_pairs={{0,128},{32,160},{64,192},{96,224},{128,0},{160,32},{192,64},{224,... | collective-permute-start | bytes 786440 | tf_op jit(solution)/shard_map/ppermute | solution.py:28
  121.6 9.3 %collective-permute-start.9 = (f16[64,2048]{1,0:T(8,128)(2,1)S(1)}, f16[64,2048]{1,0:T(8,128)(2,1)S(1)}, u32[]{:S(2)}, u32[]{:S(2)}) collective-permute-start(f16[64,2048]{1,0:T(8,128)(2,1)S(1)} %get-tuple-element.22), channel_id=1, source_target_pairs={{0,192},{32,224},{64,0},{96,32},{128,64},{160,96},{192,128},{224,1... | collective-permute-start | bytes 786440 | tf_op jit(solution)/shard_map/ppermute | solution.py:28
  123.7 8.8 %collective-permute-start.8 = (f16[64,2048]{1,0:T(8,128)(2,1)S(1)}, f16[64,2048]{1,0:T(8,128)(2,1)}, u32[]{:S(2)}, u32[]{:S(2)}) collective-permute-start(f16[64,2048]{1,0:T(8,128)(2,1)S(1)} %get-tuple-element.20), channel_id=1, source_target_pairs={{0,64},{32,96},{64,128},{96,160},{128,192},{160,224},{192,0},{224,... | collective-permute-start | bytes 786440 | tf_op jit(solution)/shard_map/ppermute | solution.py:28
  143.7 2.0 collective-permute-start.11
  146.7 8.1 %collective-permute-start.14 = (f16[64,1024]{1,0:T(8,128)(2,1)}, f16[64,1024]{1,0:T(8,128)(2,1)S(1)}, u32[]{:S(2)}, u32[]{:S(2)}) collective-permute-start(f16[64,1024]{1,0:T(8,128)(2,1)} %get-tuple-element.28), channel_id=1, source_target_pairs={{0,128},{32,160},{64,192},{96,224},{128,0},{160,32},{192,64},{224,... | collective-permute-start | bytes 393224 | tf_op jit(solution)/shard_map/ppermute | solution.py:28
  147.8 7.4 %collective-permute-start.13 = (f16[64,1024]{1,0:T(8,128)(2,1)}, f16[64,1024]{1,0:T(8,128)(2,1)S(1)}, u32[]{:S(2)}, u32[]{:S(2)}) collective-permute-start(f16[64,1024]{1,0:T(8,128)(2,1)} %get-tuple-element.29), channel_id=1, source_target_pairs={{0,192},{32,224},{64,0},{96,32},{128,64},{160,96},{192,128},{224,1... | collective-permute-start | bytes 393224 | tf_op jit(solution)/shard_map/ppermute | solution.py:28
  150.0 7.0 %collective-permute-start.12 = (f16[64,1024]{1,0:T(8,128)(2,1)S(1)}, f16[64,1024]{1,0:T(8,128)(2,1)}, u32[]{:S(2)}, u32[]{:S(2)}) collective-permute-start(f16[64,1024]{1,0:T(8,128)(2,1)S(1)} %get-tuple-element.27), channel_id=1, source_target_pairs={{0,64},{32,96},{64,128},{96,160},{128,192},{160,224},{192,0},{224,... | collective-permute-start | bytes 393224 | tf_op jit(solution)/shard_map/ppermute | solution.py:28
  154.8 0.6 copy-start.7
  155.4 0.7 copy-start.8
  158.6 10.1 %collective-permute-start.15 = (bf16[64,2176]{1,0:T(8,128)(2,1)S(1)}, bf16[64,2176]{1,0:T(8,128)(2,1)S(1)}, u32[]{:S(2)}, u32[]{:S(2)}) collective-permute-start(bf16[64,2176]{1,0:T(8,128)(2,1)S(1)} %get-tuple-element.32), channel_id=1, source_target_pairs={{0,64},{32,96},{64,128},{96,160},{128,192},{160,224},{192,0},{224,... | collective-permute-start | bytes 835592 | tf_op jit(solution)/shard_map/ppermute | solution.py:28
  159.4 13.7 %collective-permute-start.16 = (bf16[64,2176]{1,0:T(8,128)(2,1)S(1)}, bf16[64,2176]{1,0:T(8,128)(2,1)S(1)}, u32[]{:S(2)}, u32[]{:S(2)}) collective-permute-start(bf16[64,2176]{1,0:T(8,128)(2,1)S(1)} %get-tuple-element.32), channel_id=1, source_target_pairs={{0,192},{32,224},{64,0},{96,32},{128,64},{160,96},{192,128},{224,1... | collective-permute-start | bytes 835592 | tf_op jit(solution)/shard_map/ppermute | solution.py:28
  161.9 12.2 %collective-permute-start.17 = (bf16[64,2176]{1,0:T(8,128)(2,1)S(1)}, bf16[64,2176]{1,0:T(8,128)(2,1)S(1)}, u32[]{:S(2)}, u32[]{:S(2)}) collective-permute-start(bf16[64,2176]{1,0:T(8,128)(2,1)S(1)} %get-tuple-element.32), channel_id=1, source_target_pairs={{0,128},{32,160},{64,192},{96,224},{128,0},{160,32},{192,64},{224,... | collective-permute-start | bytes 835592 | tf_op jit(solution)/shard_map/ppermute | solution.py:28
  174.1 3.0 %collective-permute-start.18 = (bf16[256,2176]{1,0:T(8,128)(2,1)S(1)}, bf16[256,2176]{1,0:T(8,128)(2,1)}, u32[]{:S(2)}, u32[]{:S(2)}) collective-permute-start(bf16[256,2176]{1,0:T(8,128)(2,1)S(1)} %constant_dynamic-update-slice_fusion), channel_id=1, source_target_pairs={{0,32},{32,0},{64,96},{96,64},{128,160},{160,128},{192,224},{224,1... | collective-permute-start | bytes 3342344 | tf_op jit(solution)/shard_map/ppermute | solution.py:32
  174.2 1.5 copy-start.2
  181.9 35.1 %copy-start.10 = (s32[32,8]{0,1:T(8,128)S(1)}, s32[32,8]{0,1:T(8,128)}, u32[]{:S(2)}) copy-start(s32[32,8]{0,1:T(8,128)} %param.17) | copy-start | bytes 3076
Sparse Core Ops, SparseCore 0:
  9.9 41.6 all-gather.1
